TPU v7x, 32 devices: a whole 2x2x4 slice. The times are simulated.
32 devices in a mesh: dp: 4 (over x, core), ctx: 4 (over z), tensor: 2 (over y).
Axes of the slice: x: 2, y: 2, z: 4, core: 2. Of those that a mesh axis runs over, the one named last changes fastest.
Arguments:
- hidden_in: bfloat16 [4, 1024, 1536], P('dp', 'ctx'), may hold values from -6 to 6
- doc_pos: int32 [4, 1024], P('dp', 'ctx'), may hold values from 0 to 1022, as said below
- mixer_gain: bfloat16 [1536], P(('dp', 'ctx')), may hold values from 0.25 to 1.75
- mixer_in: bfloat16 [3, 1536, 1536], P(None, ('dp', 'ctx'), 'tensor'), may hold values from -0.15625 to 0.15625
- conv_taps: bfloat16 [3, 1536], P(None, 'tensor'), may hold values from -3 to 3
- mixer_out: bfloat16 [1536, 1536], P('tensor', ('dp', 'ctx')), may hold values from -0.15625 to 0.15625
- feed_first: bfloat16 [1536], P(('dp', 'ctx')), may hold values from 0.25 to 1.75
- gate_first: bfloat16 [1536, 6912], P(('dp', 'ctx'), 'tensor'), may hold values from -0.15625 to 0.15625
- lift_first: bfloat16 [1536, 6912], P(('dp', 'ctx'), 'tensor'), may hold values from -0.15625 to 0.15625
- down_first: bfloat16 [6912, 1536], P('tensor', ('dp', 'ctx')), may hold values from -0.078125 to 0.078125
- attend_gain: bfloat16 [1536], P(('dp', 'ctx')), may hold values from 0.25 to 1.75
- query_proj: bfloat16 [1536, 1536], P(('dp', 'ctx'), 'tensor'), may hold values from -0.15625 to 0.15625
- key_proj: bfloat16 [1536, 512], P(('dp', 'ctx'), 'tensor'), may hold values from -0.15625 to 0.15625
- value_proj: bfloat16 [1536, 512], P(('dp', 'ctx'), 'tensor'), may hold values from -0.15625 to 0.15625
- query_gain: bfloat16 [64], replicated, may hold values from 0.25 to 1.75
- key_gain: bfloat16 [64], replicated, may hold values from 0.25 to 1.75
- attend_out: bfloat16 [1536, 1536], P('tensor', ('dp', 'ctx')), may hold values from -1.25 to 1.25
- feed_second: bfloat16 [1536], P(('dp', 'ctx')), may hold values from 0.25 to 1.75
- gate_second: bfloat16 [1536, 6912], P(('dp', 'ctx'), 'tensor'), may hold values from -0.15625 to 0.15625
- lift_second: bfloat16 [1536, 6912], P(('dp', 'ctx'), 'tensor'), may hold values from -0.15625 to 0.15625
- down_second: bfloat16 [6912, 1536], P('tensor', ('dp', 'ctx')), may hold values from -0.078125 to 0.078125
- output_grad: bfloat16 [4, 1024, 1536], P('dp', 'ctx'), may hold values from -6 to 6
Outputs:
- hidden_out: bfloat16 [4, 1024, 1536], P('dp', 'ctx')
- hidden_grad: bfloat16 [4, 1024, 1536], P('dp', 'ctx')
- mixer_gain_grad: float32 [1536], P(('dp', 'ctx'))
- mixer_in_grad: float32 [3, 1536, 1536], P(None, ('dp', 'ctx'), 'tensor')
- conv_taps_grad: float32 [3, 1536], P(None, 'tensor')
- mixer_out_grad: float32 [1536, 1536], P('tensor', ('dp', 'ctx'))
- feed_first_grad: float32 [1536], P(('dp', 'ctx'))
- gate_first_grad: float32 [1536, 6912], P(('dp', 'ctx'), 'tensor')
- lift_first_grad: float32 [1536, 6912], P(('dp', 'ctx'), 'tensor')
- down_first_grad: float32 [6912, 1536], P('tensor', ('dp', 'ctx'))
- attend_gain_grad: float32 [1536], P(('dp', 'ctx'))
- query_proj_grad: float32 [1536, 1536], P(('dp', 'ctx'), 'tensor')
- key_proj_grad: float32 [1536, 512], P(('dp', 'ctx'), 'tensor')
- value_proj_grad: float32 [1536, 512], P(('dp', 'ctx'), 'tensor')
- query_gain_grad: float32 [64], replicated
- key_gain_grad: float32 [64], replicated
- attend_out_grad: float32 [1536, 1536], P('tensor', ('dp', 'ctx'))
- feed_second_grad: float32 [1536], P(('dp', 'ctx'))
- gate_second_grad: float32 [1536, 6912], P(('dp', 'ctx'), 'tensor')
- lift_second_grad: float32 [1536, 6912], P(('dp', 'ctx'), 'tensor')
- down_second_grad: float32 [6912, 1536], P('tensor', ('dp', 'ctx'))
Inputs may be any that keep to these rules, and one draw needn't show every extreme that they name: doc_pos[s, t] is t minus the first index of the contiguous document of sequence s that holds token t, so documents start where it is 0; token 0 starts one; every sequence holds one document that starts within its first 256 tokens and ends within its last 256; in one sequence that document runs from token 1 to the end.
All inputs are finite; a program needn't handle non-finite values.
Results may differ from a plain program's by a relative error of at most 0.025.
Values may be sent and summed in bfloat16 or wider, within the bound.
A program may use at most 832 MiB of HBM per device.

v0:
```python
import math

import jax
import jax.numpy as jnp
from jax import lax
from jax.sharding import PartitionSpec as P

H = 24
KV = 8
HD = 64


epsilon = 1e-05


def shifted(block, axis, distance):
    devices = range(lax.axis_size(axis))
    route = [(i - distance, i) for i in devices if i - distance in devices]
    return lax.ppermute(block, axis, route)


def rms_scale(values):
    return lax.rsqrt(jnp.mean(values * values, -1, keepdims=True) + epsilon)


def rms_back(values, upstream):
    row_scale = rms_scale(values)
    normed = values * row_scale
    return row_scale * (upstream - normed * jnp.mean(upstream * normed, -1, keepdims=True))


def low_dot(left, right):
    return jnp.dot(left, right, preferred_element_type=jnp.float32)


def tensor_total(term_sum):
    return lax.psum(term_sum, "tensor")


def pack_grads(gradients, dim_list, pieces):
    flattened = []
    for gradient, dim_index in zip(gradients, dim_list):
        flattened.append(jnp.moveaxis(gradient, dim_index, 0).reshape(pieces, -1))
    return jnp.concatenate(flattened, 1)


def unpack_grads(packed, gradients, dim_list, pieces):
    results = []
    position = 0
    for gradient, dim_index in zip(gradients, dim_list):
        moved_shape = jnp.moveaxis(gradient, dim_index, 0).shape
        entries = gradient.size // pieces
        portion = packed[0, position : position + entries].reshape(
            (moved_shape[0] // pieces,) + tuple(moved_shape[1:])
        )
        results.append(jnp.moveaxis(portion, 0, dim_index))
        position = position + entries
    return results


def gather_mixer(mixer_gain, mixer_in, mixer_out, feed_first, gate_first, lift_first, down_first):
    return (
        lax.all_gather(mixer_gain, ("dp", "ctx"), axis=0, tiled=True),
        lax.all_gather(mixer_in, ("dp", "ctx"), axis=1, tiled=True),
        lax.all_gather(mixer_out, ("dp", "ctx"), axis=1, tiled=True),
        lax.all_gather(feed_first, ("dp", "ctx"), axis=0, tiled=True),
        lax.all_gather(gate_first, ("dp", "ctx"), axis=0, tiled=True),
        lax.all_gather(lift_first, ("dp", "ctx"), axis=0, tiled=True),
        lax.all_gather(down_first, ("dp", "ctx"), axis=1, tiled=True),
    )


def gather_attend(
    attend_gain,
    query_proj,
    key_proj,
    value_proj,
    attend_out,
    feed_second,
    gate_second,
    lift_second,
    down_second,
):
    return (
        lax.all_gather(attend_gain, ("dp", "ctx"), axis=0, tiled=True),
        lax.all_gather(query_proj, ("dp", "ctx"), axis=0, tiled=True),
        lax.all_gather(key_proj, ("dp", "ctx"), axis=0, tiled=True),
        lax.all_gather(value_proj, ("dp", "ctx"), axis=0, tiled=True),
        lax.all_gather(attend_out, ("dp", "ctx"), axis=1, tiled=True),
        lax.all_gather(feed_second, ("dp", "ctx"), axis=0, tiled=True),
        lax.all_gather(gate_second, ("dp", "ctx"), axis=0, tiled=True),
        lax.all_gather(lift_second, ("dp", "ctx"), axis=0, tiled=True),
        lax.all_gather(down_second, ("dp", "ctx"), axis=1, tiled=True),
    )


def gather_keys(key_local, value_local):
    return (
        lax.all_gather(key_local, "ctx", axis=1, tiled=True),
        lax.all_gather(value_local, "ctx", axis=1, tiled=True),
    )


def rotary_tables(positions, head_dim):
    half_dim = head_dim // 2
    freqs = jnp.exp(-math.log(1000000.0) * 2.0 * jnp.arange(half_dim, dtype=jnp.float32) / head_dim)
    angles = positions.astype(jnp.float32)[:, None] * freqs[None, :]
    return (jnp.cos(angles), jnp.sin(angles))


def rotate(values, cosine, sine):
    half_dim = values.shape[-1] // 2
    first_half = values[..., :half_dim]
    second_half = values[..., half_dim:]
    cos_rows = cosine[:, None, :]
    sin_rows = sine[:, None, :]
    return jnp.concatenate(
        [
            first_half * cos_rows - second_half * sin_rows,
            second_half * cos_rows + first_half * sin_rows,
        ],
        -1,
    )


def rotate_back(grads, cosine, sine):
    half_dim = grads.shape[-1] // 2
    first_half = grads[..., :half_dim]
    second_half = grads[..., half_dim:]
    cos_rows = cosine[:, None, :]
    sin_rows = sine[:, None, :]
    return jnp.concatenate(
        [
            first_half * cos_rows + second_half * sin_rows,
            second_half * cos_rows - first_half * sin_rows,
        ],
        -1,
    )


def group_rows(values, groups):
    row_count, heads, head_dim = values.shape
    return (
        values.reshape(row_count, heads // groups, groups, head_dim)
        .transpose(1, 2, 0, 3)
        .reshape(heads // groups, groups * row_count, head_dim)
    )


def ungroup_rows(values, groups):
    kv_heads, rows, head_dim = values.shape
    row_count = rows // groups
    return (
        values.reshape(kv_heads, groups, row_count, head_dim)
        .transpose(2, 0, 1, 3)
        .reshape(row_count, kv_heads * groups, head_dim)
    )


def key_layout(positions, row_count, groups, length):
    index = lax.axis_index("ctx")
    query_at = index * row_count + jnp.tile(jnp.arange(row_count, dtype=jnp.int32), groups)
    query_from = query_at - jnp.tile(positions, groups)
    block_size = min(512, length)
    block_count = ((index + 1) * row_count + block_size - 1) // block_size
    return (query_at, query_from, block_size, block_count)


def block_scores(query_rows, key_block, layout, block_index):
    query_at, query_from, block_size, block_count = layout
    key_at = block_index * block_size + jnp.arange(block_size, dtype=jnp.int32)
    allowed = (key_at[None, :] <= query_at[:, None]) & (key_at[None, :] >= query_from[:, None])
    scores = jnp.einsum(
        "grd,gkd->grk", query_rows, key_block, preferred_element_type=jnp.float32
    ) / math.sqrt(query_rows.shape[-1])
    return (jnp.where(allowed[None], scores, -1e30), allowed[None])


def softmax_totals(query_rows, key_all, layout):
    block_size, block_count = (layout[2], layout[3])

    def total_step(block_index, carry):
        run_max, run_sum = carry
        key_block = lax.dynamic_slice_in_dim(key_all, block_index * block_size, block_size, 1)
        scores, allowed = block_scores(query_rows, key_block, layout, block_index)
        new_max = jnp.maximum(run_max, jnp.max(scores, -1))
        weights = jnp.where(allowed, jnp.exp(scores - new_max[..., None]), 0.0)
        return (new_max, run_sum * jnp.exp(run_max - new_max) + jnp.sum(weights, -1))

    shape_rows = query_rows.shape[:2]
    start_carry = (jnp.full(shape_rows, -1e30, jnp.float32), jnp.zeros(shape_rows, jnp.float32))
    run_max, run_sum = lax.fori_loop(0, block_count, total_step, start_carry)
    return run_max + jnp.log(run_sum)


def block_probs(query_rows, key_all, log_total, layout, block_index):
    block_size = layout[2]
    key_block = lax.dynamic_slice_in_dim(key_all, block_index * block_size, block_size, 1)
    scores, allowed = block_scores(query_rows, key_block, layout, block_index)
    return (jnp.where(allowed, jnp.exp(scores - log_total[..., None]), 0.0), key_block)


def attend_values(query_rows, key_all, value_all, log_total, layout):
    block_size, block_count = (layout[2], layout[3])

    def value_step(block_index, context):
        probs, key_block = block_probs(query_rows, key_all, log_total, layout, block_index)
        value_block = lax.dynamic_slice_in_dim(value_all, block_index * block_size, block_size, 1)
        return context + jnp.einsum(
            "grk,gkd->grd",
            probs.astype(jnp.bfloat16),
            value_block,
            preferred_element_type=jnp.float32,
        )

    return lax.fori_loop(0, block_count, value_step, jnp.zeros(query_rows.shape, jnp.float32))


def softmax_deltas(query_rows, key_all, value_all, log_total, grad_rows, layout):
    block_size, block_count = (layout[2], layout[3])

    def delta_step(block_index, deltas):
        probs, key_block = block_probs(query_rows, key_all, log_total, layout, block_index)
        value_block = lax.dynamic_slice_in_dim(value_all, block_index * block_size, block_size, 1)
        prob_grad = jnp.einsum(
            "grd,gkd->grk", grad_rows, value_block, preferred_element_type=jnp.float32
        )
        return deltas + jnp.sum(probs * prob_grad, -1)

    return lax.fori_loop(0, block_count, delta_step, jnp.zeros(query_rows.shape[:2], jnp.float32))


def attend_grads(query_rows, key_all, value_all, log_total, grad_rows, deltas, layout):
    block_size, block_count = (layout[2], layout[3])
    inverse_root = 1.0 / math.sqrt(query_rows.shape[-1])

    def grad_step(block_index, carry):
        query_acc, key_acc, value_acc = carry
        start_row = block_index * block_size
        probs, key_block = block_probs(query_rows, key_all, log_total, layout, block_index)
        value_block = lax.dynamic_slice_in_dim(value_all, start_row, block_size, 1)
        prob_grad = jnp.einsum(
            "grd,gkd->grk", grad_rows, value_block, preferred_element_type=jnp.float32
        )
        score_grad = (probs * (prob_grad - deltas[..., None])).astype(jnp.bfloat16)
        query_acc = query_acc + jnp.einsum(
            "grk,gkd->grd", score_grad, key_block, preferred_element_type=jnp.float32
        )
        key_part = (
            jnp.einsum("grk,grd->gkd", score_grad, query_rows, preferred_element_type=jnp.float32)
            * inverse_root
        )
        value_part = jnp.einsum(
            "grk,grd->gkd",
            probs.astype(jnp.bfloat16),
            grad_rows,
            preferred_element_type=jnp.float32,
        )
        key_acc = lax.dynamic_update_slice_in_dim(
            key_acc,
            lax.dynamic_slice_in_dim(key_acc, start_row, block_size, 1) + key_part,
            start_row,
            1,
        )
        value_acc = lax.dynamic_update_slice_in_dim(
            value_acc,
            lax.dynamic_slice_in_dim(value_acc, start_row, block_size, 1) + value_part,
            start_row,
            1,
        )
        return (query_acc, key_acc, value_acc)

    start_carry = (
        jnp.zeros(query_rows.shape, jnp.float32),
        jnp.zeros(key_all.shape, jnp.float32),
        jnp.zeros(value_all.shape, jnp.float32),
    )
    query_acc, key_acc, value_acc = lax.fori_loop(0, block_count, grad_step, start_carry)
    return (query_acc * inverse_root, key_acc, value_acc)


def conv_apply(extended, positions, conv_taps, row_count):
    conv_sum = jnp.zeros((row_count, extended.shape[1]), jnp.float32)
    for offset in range(3):
        in_doc = (positions >= offset).astype(jnp.float32)[:, None]
        conv_sum = (
            conv_sum + conv_taps[offset] * extended[2 - offset : 2 - offset + row_count] * in_doc
        )
    return conv_sum


def mixer_forward(stream, positions, conv_taps, weights):
    norm_gain, lift_in, lift_out = (weights[0], weights[1], weights[2])
    row_scale = rms_scale(stream)
    normed = (stream * row_scale * norm_gain.astype(jnp.float32)).astype(jnp.bfloat16)
    projected = jnp.einsum("td,kde->kte", normed, lift_in, preferred_element_type=jnp.float32)
    conv_src = (projected[0] * projected[2]).astype(jnp.bfloat16)
    earlier = shifted(conv_src[-2:], "ctx", 1)
    extended = jnp.concatenate([earlier, conv_src], 0).astype(jnp.float32)
    row_count = conv_src.shape[0]
    conv_sum = conv_apply(extended, positions, conv_taps, row_count)
    gated = (projected[1] * conv_sum).astype(jnp.bfloat16)
    branch_out = tensor_total(low_dot(gated, lift_out))
    return (stream + branch_out, (row_scale, normed, projected, extended, conv_sum, gated))


def mixer_backward(upstream, stream, positions, conv_taps, weights, saved):
    norm_gain, lift_in, lift_out = (weights[0], weights[1], weights[2])
    row_scale, normed, projected, extended, conv_sum, gated = saved
    row_count = stream.shape[0]
    branch_grad = upstream.astype(jnp.bfloat16)
    out_grad = jnp.einsum("tc,td->cd", gated, branch_grad, preferred_element_type=jnp.float32)
    gated_grad = jnp.einsum("td,cd->tc", branch_grad, lift_out, preferred_element_type=jnp.float32)
    gate_c_grad = (gated_grad * conv_sum).astype(jnp.bfloat16)
    sum_grad = gated_grad * projected[1]
    tap_rows = []
    spread = jnp.zeros_like(extended)
    for offset in range(3):
        in_doc = (positions >= offset).astype(jnp.float32)[:, None]
        masked = sum_grad * in_doc
        tap_rows.append(jnp.sum(masked * extended[2 - offset : 2 - offset + row_count], 0))
        spread = spread + jnp.pad(conv_taps[offset] * masked, ((2 - offset, offset), (0, 0)))
    returned = shifted(spread[:2], "ctx", -1)
    src_grad = spread[2:] + jnp.concatenate(
        [jnp.zeros((row_count - 2, spread.shape[1]), jnp.float32), returned], 0
    )
    proj_grad = jnp.stack(
        [src_grad * projected[2], gate_c_grad.astype(jnp.float32), src_grad * projected[0]]
    ).astype(jnp.bfloat16)
    in_grad = jnp.einsum("td,kte->kde", normed, proj_grad, preferred_element_type=jnp.float32)
    normed_grad = tensor_total(
        jnp.einsum("kte,kde->td", proj_grad, lift_in, preferred_element_type=jnp.float32)
    )
    gain_grad = jnp.sum(normed_grad * stream * row_scale, 0)
    stream_grad = upstream + rms_back(stream, normed_grad * norm_gain.astype(jnp.float32))
    return (stream_grad, (gain_grad, in_grad, out_grad), jnp.stack(tap_rows))


def feed_forward(stream, norm_gain, gate_weight, lift_weight, down_weight):
    row_scale = rms_scale(stream)
    normed = (stream * row_scale * norm_gain.astype(jnp.float32)).astype(jnp.bfloat16)
    gate_out = low_dot(normed, gate_weight)
    lift_out = low_dot(normed, lift_weight)
    hidden = (jax.nn.silu(gate_out) * lift_out).astype(jnp.bfloat16)
    branch_out = tensor_total(low_dot(hidden, down_weight))
    return (stream + branch_out, (row_scale, normed, gate_out, lift_out, hidden))


def feed_backward(upstream, stream, norm_gain, gate_weight, lift_weight, down_weight, saved):
    row_scale, normed, gate_out, lift_out, hidden = saved
    branch_grad = upstream.astype(jnp.bfloat16)
    down_grad = jnp.einsum("tf,td->fd", hidden, branch_grad, preferred_element_type=jnp.float32)
    hidden_grad = jnp.einsum(
        "td,fd->tf", branch_grad, down_weight, preferred_element_type=jnp.float32
    )
    sigmoid_gate = jax.nn.sigmoid(gate_out)
    gate_grad = (
        hidden_grad * lift_out * sigmoid_gate * (1.0 + gate_out * (1.0 - sigmoid_gate))
    ).astype(jnp.bfloat16)
    lift_grad = (hidden_grad * gate_out * sigmoid_gate).astype(jnp.bfloat16)
    gate_weight_grad = jnp.einsum(
        "td,tf->df", normed, gate_grad, preferred_element_type=jnp.float32
    )
    lift_weight_grad = jnp.einsum(
        "td,tf->df", normed, lift_grad, preferred_element_type=jnp.float32
    )
    normed_grad = tensor_total(
        jnp.einsum("tf,df->td", gate_grad, gate_weight, preferred_element_type=jnp.float32)
        + jnp.einsum("tf,df->td", lift_grad, lift_weight, preferred_element_type=jnp.float32)
    )
    gain_grad = jnp.sum(normed_grad * stream * row_scale, 0)
    stream_grad = upstream + rms_back(stream, normed_grad * norm_gain.astype(jnp.float32))
    return (stream_grad, (gain_grad, gate_weight_grad, lift_weight_grad, down_grad))


def attend_forward(stream, positions, cosine, sine, query_gain, key_gain, weights, groups):
    norm_gain, query_proj, key_proj, value_proj, attend_out = (
        weights[0],
        weights[1],
        weights[2],
        weights[3],
        weights[4],
    )
    row_count = stream.shape[0]
    row_scale = rms_scale(stream)
    normed = (stream * row_scale * norm_gain.astype(jnp.float32)).astype(jnp.bfloat16)
    queries = low_dot(normed, query_proj).reshape(row_count, -1, HD)
    keys_raw = low_dot(normed, key_proj).reshape(row_count, -1, HD)
    values_raw = low_dot(normed, value_proj).reshape(row_count, -1, HD)
    query_scale = rms_scale(queries)
    key_scale = rms_scale(keys_raw)
    query_rot = rotate(queries * query_scale * query_gain, cosine, sine).astype(jnp.bfloat16)
    key_rot = rotate(keys_raw * key_scale * key_gain, cosine, sine).astype(jnp.bfloat16)
    query_rows = group_rows(query_rot, groups)
    key_local = key_rot.transpose(1, 0, 2)
    value_local = values_raw.astype(jnp.bfloat16).transpose(1, 0, 2)
    key_all, value_all = gather_keys(key_local, value_local)
    layout = key_layout(positions, row_count, groups, key_all.shape[1])
    log_total = softmax_totals(query_rows, key_all, layout)
    context = attend_values(query_rows, key_all, value_all, log_total, layout)
    context_low = ungroup_rows(context, groups).reshape(row_count, -1).astype(jnp.bfloat16)
    branch_out = tensor_total(low_dot(context_low, attend_out))
    saved = (
        row_scale,
        normed,
        queries,
        keys_raw,
        query_scale,
        key_scale,
        query_rows,
        key_local,
        value_local,
        key_all,
        value_all,
        log_total,
        context_low,
    )
    return (stream + branch_out, saved)


def attend_backward(
    upstream,
    stream,
    positions,
    cosine,
    sine,
    query_gain,
    key_gain,
    weights,
    saved,
    key_all,
    value_all,
    groups,
):
    norm_gain, query_proj, key_proj, value_proj, attend_out = (
        weights[0],
        weights[1],
        weights[2],
        weights[3],
        weights[4],
    )
    row_scale, normed, queries, keys_raw, query_scale, key_scale, query_rows = (
        saved[0],
        saved[1],
        saved[2],
        saved[3],
        saved[4],
        saved[5],
        saved[6],
    )
    log_total, context_low = (saved[11], saved[12])
    row_count = stream.shape[0]
    branch_grad = upstream.astype(jnp.bfloat16)
    out_grad = jnp.einsum("te,td->ed", context_low, branch_grad, preferred_element_type=jnp.float32)
    context_grad = jnp.einsum(
        "td,ed->te", branch_grad, attend_out, preferred_element_type=jnp.float32
    ).astype(jnp.bfloat16)
    grad_rows = group_rows(context_grad.reshape(row_count, -1, HD), groups)
    layout = key_layout(positions, row_count, groups, key_all.shape[1])
    deltas = softmax_deltas(query_rows, key_all, value_all, log_total, grad_rows, layout)
    query_acc, key_acc, value_acc = attend_grads(
        query_rows, key_all, value_all, log_total, grad_rows, deltas, layout
    )
    stacked_grads = jnp.stack([key_acc, value_acc])
    mine_grads = lax.psum_scatter(
        stacked_grads.astype(jnp.bfloat16), "ctx", scatter_dimension=2, tiled=True
    ).astype(jnp.float32)
    key_mine, value_mine = (mine_grads[0], mine_grads[1])
    query_norm_grad = rotate_back(ungroup_rows(query_acc, groups), cosine, sine)
    key_norm_grad = rotate_back(key_mine.transpose(1, 0, 2), cosine, sine)
    query_gain_part = jnp.sum(query_norm_grad * queries * query_scale, (0, 1))
    key_gain_part = jnp.sum(key_norm_grad * keys_raw * key_scale, (0, 1))
    query_grad = (
        rms_back(queries, query_norm_grad * query_gain).reshape(row_count, -1).astype(jnp.bfloat16)
    )
    key_grad = (
        rms_back(keys_raw, key_norm_grad * key_gain).reshape(row_count, -1).astype(jnp.bfloat16)
    )
    value_grad = value_mine.transpose(1, 0, 2).reshape(row_count, -1).astype(jnp.bfloat16)
    query_proj_grad = jnp.einsum(
        "td,te->de", normed, query_grad, preferred_element_type=jnp.float32
    )
    key_proj_grad = jnp.einsum("td,te->de", normed, key_grad, preferred_element_type=jnp.float32)
    value_proj_grad = jnp.einsum(
        "td,te->de", normed, value_grad, preferred_element_type=jnp.float32
    )
    normed_part = jnp.einsum(
        "te,de->td", query_grad, query_proj, preferred_element_type=jnp.float32
    )
    normed_part = normed_part + jnp.einsum(
        "te,de->td", key_grad, key_proj, preferred_element_type=jnp.float32
    )
    normed_part = normed_part + jnp.einsum(
        "te,de->td", value_grad, value_proj, preferred_element_type=jnp.float32
    )
    normed_grad, query_gain_grad, key_gain_grad = (
        lax.psum(normed_part.astype(jnp.bfloat16), "tensor").astype(jnp.float32),
        lax.psum(query_gain_part.astype(jnp.bfloat16), "tensor").astype(jnp.float32),
        lax.psum(key_gain_part.astype(jnp.bfloat16), "tensor").astype(jnp.float32),
    )
    gain_grad = jnp.sum(normed_grad * stream * row_scale, 0)
    stream_grad = upstream + rms_back(stream, normed_grad * norm_gain.astype(jnp.float32))
    return (
        stream_grad,
        (gain_grad, query_proj_grad, key_proj_grad, value_proj_grad, out_grad),
        (query_gain_grad, key_gain_grad),
    )


def shards(
    hidden_in,
    doc_pos,
    mixer_gain,
    mixer_in,
    conv_taps,
    mixer_out,
    feed_first,
    gate_first,
    lift_first,
    down_first,
    attend_gain,
    query_proj,
    key_proj,
    value_proj,
    query_gain,
    key_gain,
    attend_out,
    feed_second,
    gate_second,
    lift_second,
    down_second,
    output_grad,
):
    positions = doc_pos[0]
    stream_zero = hidden_in[0].astype(jnp.float32)
    taps_float = conv_taps.astype(jnp.float32)
    query_scale_gain = query_gain.astype(jnp.float32)
    key_scale_gain = key_gain.astype(jnp.float32)
    groups = H // KV
    cosine, sine = rotary_tables(positions, HD)
    pieces = lax.axis_size("dp") * lax.axis_size("ctx")
    attend_dims = (0, 0, 0, 0, 1, 0, 0, 0, 1)
    mixer_dims = (0, 1, 1, 0, 0, 0, 1)
    mixer_set = gather_mixer(
        mixer_gain, mixer_in, mixer_out, feed_first, gate_first, lift_first, down_first
    )
    stream_one, mixer_saved = mixer_forward(stream_zero, positions, taps_float, mixer_set)
    stream_two, first_saved = feed_forward(
        stream_one, mixer_set[3], mixer_set[4], mixer_set[5], mixer_set[6]
    )
    attend_set = gather_attend(
        attend_gain,
        query_proj,
        key_proj,
        value_proj,
        attend_out,
        feed_second,
        gate_second,
        lift_second,
        down_second,
    )
    stream_three, attend_saved = attend_forward(
        stream_two, positions, cosine, sine, query_scale_gain, key_scale_gain, attend_set, groups
    )
    stream_four, second_saved = feed_forward(
        stream_three, attend_set[5], attend_set[6], attend_set[7], attend_set[8]
    )
    hidden_out = stream_four.astype(jnp.bfloat16)[None]
    back_attend = gather_attend(
        attend_gain,
        query_proj,
        key_proj,
        value_proj,
        attend_out,
        feed_second,
        gate_second,
        lift_second,
        down_second,
    )
    key_all, value_all = gather_keys(attend_saved[7], attend_saved[8])
    upstream = output_grad[0].astype(jnp.float32)
    grad_three, second_grads = feed_backward(
        upstream,
        stream_three,
        back_attend[5],
        back_attend[6],
        back_attend[7],
        back_attend[8],
        second_saved,
    )
    grad_two, attend_grads_out, head_gain_grads = attend_backward(
        grad_three,
        stream_two,
        positions,
        cosine,
        sine,
        query_scale_gain,
        key_scale_gain,
        back_attend,
        attend_saved,
        key_all,
        value_all,
        groups,
    )
    attend_list = list(attend_grads_out) + list(second_grads)
    attend_packed = pack_grads(attend_list, attend_dims, pieces)
    attend_summed = lax.psum_scatter(attend_packed, ("dp", "ctx"), scatter_dimension=0, tiled=True)
    attend_done = unpack_grads(attend_summed, attend_list, attend_dims, pieces)
    back_mixer = gather_mixer(
        mixer_gain, mixer_in, mixer_out, feed_first, gate_first, lift_first, down_first
    )
    grad_one, first_grads = feed_backward(
        grad_two,
        stream_one,
        back_mixer[3],
        back_mixer[4],
        back_mixer[5],
        back_mixer[6],
        first_saved,
    )
    grad_zero, mixer_grads, tap_part = mixer_backward(
        grad_one, stream_zero, positions, taps_float, back_mixer, mixer_saved
    )
    mixer_list = list(mixer_grads) + list(first_grads)
    mixer_packed = pack_grads(mixer_list, mixer_dims, pieces)
    mixer_summed = lax.psum_scatter(mixer_packed, ("dp", "ctx"), scatter_dimension=0, tiled=True)
    mixer_done = unpack_grads(mixer_summed, mixer_list, mixer_dims, pieces)
    taps_grad, query_gain_grad, key_gain_grad = lax.psum(
        (tap_part, head_gain_grads[0], head_gain_grads[1]), ("dp", "ctx")
    )
    hidden_grad = grad_zero.astype(jnp.bfloat16)[None]
    return (
        hidden_out,
        hidden_grad,
        mixer_done[0],
        mixer_done[1],
        taps_grad,
        mixer_done[2],
        mixer_done[3],
        mixer_done[4],
        mixer_done[5],
        mixer_done[6],
        attend_done[0],
        attend_done[1],
        attend_done[2],
        attend_done[3],
        query_gain_grad,
        key_gain_grad,
        attend_done[4],
        attend_done[5],
        attend_done[6],
        attend_done[7],
        attend_done[8],
    )


def solution(mesh):
    placed = (
        P("dp", "ctx", None),
        P("dp", "ctx"),
        P(("dp", "ctx")),
        P(None, ("dp", "ctx"), "tensor"),
        P(None, "tensor"),
        P("tensor", ("dp", "ctx")),
        P(("dp", "ctx")),
        P(("dp", "ctx"), "tensor"),
        P(("dp", "ctx"), "tensor"),
        P("tensor", ("dp", "ctx")),
        P(("dp", "ctx")),
        P(("dp", "ctx"), "tensor"),
        P(("dp", "ctx"), "tensor"),
        P(("dp", "ctx"), "tensor"),
        P(),
        P(),
        P("tensor", ("dp", "ctx")),
        P(("dp", "ctx")),
        P(("dp", "ctx"), "tensor"),
        P(("dp", "ctx"), "tensor"),
        P("tensor", ("dp", "ctx")),
        P("dp", "ctx", None),
    )
    return jax.shard_map(
        shards,
        mesh=mesh,
        in_specs=placed,
        out_specs=(
            P("dp", "ctx", None),
            P("dp", "ctx", None),
            P(("dp", "ctx")),
            P(None, ("dp", "ctx"), "tensor"),
            P(None, "tensor"),
            P("tensor", ("dp", "ctx")),
            P(("dp", "ctx")),
            P(("dp", "ctx"), "tensor"),
            P(("dp", "ctx"), "tensor"),
            P("tensor", ("dp", "ctx")),
            P(("dp", "ctx")),
            P(("dp", "ctx"), "tensor"),
            P(("dp", "ctx"), "tensor"),
            P(("dp", "ctx"), "tensor"),
            P(),
            P(),
            P("tensor", ("dp", "ctx")),
            P(("dp", "ctx")),
            P(("dp", "ctx"), "tensor"),
            P(("dp", "ctx"), "tensor"),
            P("tensor", ("dp", "ctx")),
        ),
        check_vma=False,
    )
```

profile of v0, /device:TPU:0, one launch (start us, length us, event | category | flops | bytes accessed | tf_op | source)
XLA Modules:
  0.0 4259.2 jit_solution(2534976876076742097)
XLA Ops:
  14.1 64.7 %all-reduce.12 = (bf16[1536]{0:T(1024)(128)(2,1)S(1)}, bf16[1536]{0:T(1024)(128)(2,1)S(1)}, bf16[1536]{0:T(1024)(128)(2,1)S(1)}, bf16[1536]{0:T(1024)(128)(2,1)S(1)}) all-reduce(bf16[1536]{0:T(1024)(128)(2,1)S(1)} %dynamic-update-slice, ...), channel_id=1, replica_groups=mesh['dp'=4,'ctx'=4,'tensor'=2] {'dp','ctx'}, use_global_device_ids=true, to_apply=%add.4 | all-reduce | flops 6144 | bytes 24576
  81.6 5.4 convolution_bitcast_fusion.2
  93.2 31.0 all-gather.13.cloned.1.call-done
  129.6 48.6 %all-reduce.24.cloned.1.call-done = f32[256,1536]{1,0:T(8,128)} async-done(((f32[256,1536]{1,0:T(8,128)}), f32[256,1536]{1,0:T(8,128)}) %all-reduce.24.cloned.1.call-update) | async-done | bytes 1572880 | tf_op jit(solution)/shard_map/psum | solution.py:37
  180.7 88.6 %all-gather.15.cloned.1.call-done = bf16[1536,3456]{1,0:T(8,128)(2,1)} async-done(((bf16[96,3456]{1,0:T(8,128)(2,1)}), bf16[1536,3456]{1,0:T(8,128)(2,1)}) %all-gather.15.cloned.1.call-update) | async-done | bytes 10616848 | tf_op jit(solution)/shard_map/all_gather | solution.py:67
  269.3 8.8 fusion.129
  278.1 80.5 %all-gather.17.cloned.1.call-done = bf16[1536,3456]{1,0:T(8,128)(2,1)} async-done(((bf16[96,3456]{1,0:T(8,128)(2,1)}), bf16[1536,3456]{1,0:T(8,128)(2,1)}) %all-gather.17.cloned.1.call-update) | async-done | bytes 10616848 | tf_op jit(solution)/shard_map/all_gather | solution.py:68
  358.6 10.1 multiply_convert_fusion.5
  368.8 79.2 %all-gather.19.cloned.1.call-done = bf16[3456,1536]{0,1:T(8,128)(2,1)} async-done(((bf16[3456,96]{0,1:T(8,128)(2,1)}), bf16[3456,1536]{0,1:T(8,128)(2,1)}) %all-gather.19.cloned.1.call-update) | async-done | bytes 10616848 | tf_op jit(solution)/shard_map/all_gather | solution.py:69
  447.9 8.7 fusion.130
  458.4 39.9 all_gather.80
  498.3 41.6 all_gather.83
  544.2 17.0 all_gather.81
  572.4 25.1 all_gather.84
  613.1 52.4 %all-reduce.28.cloned.1.call-done = f32[256,1536]{1,0:T(8,128)} async-done(((f32[256,1536]{1,0:T(8,128)}), f32[256,1536]{1,0:T(8,128)}) %all-reduce.28.cloned.1.call-update) | async-done | bytes 1572880 | tf_op jit(solution)/shard_map/psum | solution.py:37
  669.4 87.4 %all-gather.25.cloned.1.call-done = bf16[1536,3456]{1,0:T(8,128)(2,1)} async-done(((bf16[96,3456]{1,0:T(8,128)(2,1)}), bf16[1536,3456]{1,0:T(8,128)(2,1)}) %all-gather.25.cloned.1.call-update) | async-done | bytes 10616848 | tf_op jit(solution)/shard_map/all_gather | solution.py:91
  756.8 9.2 fusion.133
  766.0 80.2 %all-gather.27.cloned.1.call-done = bf16[1536,3456]{1,0:T(8,128)(2,1)} async-done(((bf16[96,3456]{1,0:T(8,128)(2,1)}), bf16[1536,3456]{1,0:T(8,128)(2,1)}) %all-gather.27.cloned.1.call-update) | async-done | bytes 10616848 | tf_op jit(solution)/shard_map/all_gather | solution.py:92
  846.1 9.1 fusion.134
  855.2 80.4 %all-gather.29.cloned.1.call-done = bf16[3456,1536]{0,1:T(8,128)(2,1)} async-done(((bf16[3456,96]{0,1:T(8,128)(2,1)}), bf16[3456,1536]{0,1:T(8,128)(2,1)}) %all-gather.29.cloned.1.call-update) | async-done | bytes 10616848 | tf_op jit(solution)/shard_map/all_gather | solution.py:93
  935.6 11.4 multiply_convert_fusion.2
  947.0 7.1 fusion.136
  959.8 49.6 %all-reduce.30.cloned.1.call-done = f32[256,1536]{1,0:T(8,128)} async-done(((f32[256,1536]{1,0:T(8,128)}), f32[256,1536]{1,0:T(8,128)}) %all-reduce.30.cloned.1.call-update) | async-done | bytes 1572880 | tf_op jit(solution)/shard_map/psum | solution.py:37
  1017.2 9.1 while.56
  1029.5 14.4 while.57
  1063.0 34.5 reduce-scatter.2.cloned.1.call-done
  1102.1 33.1 all-reduce.32.cloned.1.call-done
  1138.4 9.4 multiply_convert_fusion
  1151.0 8.4 convolution_add_fusion.3
  1159.9 8.4 fusion.135
  1168.3 8.9 fusion.144
  1177.1 33.9 all-reduce.34.cloned.1.call-done
  1231.3 9.4 fusion.145
  1240.7 19.7 reshape.548
  1260.4 21.1 reshape.549
  1281.5 9.0 convolution_bitcast_fusion
  1290.5 20.8 copy.112
  1311.3 19.8 reshape.550
  1355.4 14.9 dynamic-update-slice.5
  1370.3 6.3 dynamic-update-slice.6
  1376.6 6.6 dynamic-update-slice.7
  1383.2 15.0 dynamic-update-slice.8
  1399.7 58.0 %dynamic-update-slice.10 = f32[16,1192128]{1,0:T(8,128)} dynamic-update-slice(f32[16,1192128]{1,0:T(8,128)} %dynamic-update-slice.9, f32[16,331776]{1,0:T(8,128)} %reshape.548, s32[]{} %constant.209, s32[]{} %constant.215) | dynamic-update-slice | bytes 42467332
  1457.7 58.0 %dynamic-update-slice.11 = f32[16,1192128]{1,0:T(8,128)} dynamic-update-slice(f32[16,1192128]{1,0:T(8,128)} %dynamic-update-slice.10, f32[16,331776]{1,0:T(8,128)} %reshape.549, s32[]{} %constant.209, s32[]{} %constant.216) | dynamic-update-slice | bytes 42467332
  1515.7 57.9 %dynamic-update-slice.12 = f32[16,1192128]{1,0:T(8,128)} dynamic-update-slice(f32[16,1192128]{1,0:T(8,128)} %dynamic-update-slice.11, f32[16,331776]{1,0:T(8,128)} %reshape.550, s32[]{} %constant.209, s32[]{} %constant.217) | dynamic-update-slice | bytes 42467332 | tf_op jit(solution)/shard_map/concatenate | solution.py:44
  1575.3 9.9 fusion.139
  1585.1 20.1 reshape.539
  1605.2 9.0 fusion.140
  1614.3 20.0 reshape.540
  1634.3 9.0 fusion.110
  1643.3 20.6 reshape.541
  1675.1 34.5 copy.111
  1709.6 23.4 reshape.536
  1736.4 40.4 dynamic-update-slice.14
  1776.9 15.3 dynamic-update-slice.15
  1793.6 58.4 %dynamic-update-slice.17 = f32[16,1290432]{1,0:T(8,128)} dynamic-update-slice(f32[16,1290432]{1,0:T(8,128)} %dynamic-update-slice.16, f32[16,331776]{1,0:T(8,128)} %reshape.539, s32[]{} %constant.209, s32[]{} %constant.221) | dynamic-update-slice | bytes 42467332
  1852.1 58.6 %dynamic-update-slice.18 = f32[16,1290432]{1,0:T(8,128)} dynamic-update-slice(f32[16,1290432]{1,0:T(8,128)} %dynamic-update-slice.17, f32[16,331776]{1,0:T(8,128)} %reshape.540, s32[]{} %constant.209, s32[]{} %constant.222) | dynamic-update-slice | bytes 42467332
  1910.7 58.6 %dynamic-update-slice.19 = f32[16,1290432]{1,0:T(8,128)} dynamic-update-slice(f32[16,1290432]{1,0:T(8,128)} %dynamic-update-slice.18, f32[16,331776]{1,0:T(8,128)} %reshape.541, s32[]{} %constant.209, s32[]{} %constant.223) | dynamic-update-slice | bytes 42467332 | tf_op jit(solution)/shard_map/concatenate | solution.py:44
  1975.1 63.6 %all-reduce.10 = (f32[3,768]{1,0:T(4,128)}, f32[64]{0:T(128)}, f32[64]{0:T(128)}) all-reduce(f32[3,768]{1,0:T(4,128)S(1)} %pad_maximum_fusion.6, bf16[64]{0:T(256)(128)(2,1)S(1)} %get-tuple-element.657, bf16[64]{0:T(256)(128)(2,1)S(1)} %get-tuple-element.658), channel_id=1, replica_groups=mesh['dp'=4,'ctx'=4,'tensor'=2] {'dp','ctx'}, use_global_device_ids=true, to_apply=%region_38.39 | all-reduce | flops 2432 | bytes 19200 | tf_op jit(solution)/shard_map/psum | solution.py:628
  2042.8 793.7 %all-reduce.38.cloned.1.call-done = f32[16,1192128]{1,0:T(8,128)} async-done(((f32[16,1192128]{1,0:T(8,128)}), f32[16,1192128]{1,0:T(8,128)}) %all-reduce.38.cloned.1.call-update) | async-done | bytes 76296208
  2846.7 20.1 dynamic-slice_reduce_fusion
  2873.8 1333.4 %all-reduce.36.cloned.1.call-done = f32[16,1290432]{1,0:T(8,128)} async-done(((f32[16,1290432]{1,0:T(8,128)}), f32[16,1290432]{1,0:T(8,128)}) %all-reduce.36.cloned.1.call-update) | async-done | bytes 82587664
  4207.3 12.1 dynamic-slice_reduce_fusion.6
  4224.9 20.1 dynamic-slice_reduce_fusion.3
  (538 shorter events, 240.3 us)
Async XLA Ops:
  7.2 74.4 %all-gather.11.cloned.1.call-start = ((), (), s32[]{:S(2)}) async-start(), calls=%async_computation.1 | async-start | bytes 7520256 | tf_op jit(solution)/shard_map/all_gather | solution.py:64
  7.9 116.2 %all-gather.13.cloned.1.call-start = ((), (), s32[]{:S(2)}) async-start(), calls=%async_computation.2 | async-start | bytes 2506752 | tf_op jit(solution)/shard_map/all_gather | solution.py:65
  8.7 169.5 %all-reduce.24.cloned.1.call-start = ((), (), s32[]{:S(2)}) async-start(), calls=%async_computation.3 | async-start | bytes 3145728 | tf_op jit(solution)/shard_map/psum | solution.py:37
  81.6 9.4 copy-start.115
  87.1 3.8 collective-permute-start
  93.1 34.6 copy-start.48
  127.7 50.5 %copy-start.19 = (bf16[1,256,1536]{2,1,0:T(8,128)(2,1)S(1)}, bf16[1,256,1536]{2,1,0:T(8,128)(2,1)}, u32[]{:S(2)}) copy-start(bf16[1,256,1536]{2,1,0:T(8,128)(2,1)} %param.30) | copy-start | bytes 2359300
  127.7 141.6 %all-gather.15.cloned.1.call-start = ((), (), s32[]{:S(2)}) async-start(), calls=%async_computation.4 | async-start | bytes 11280384 | tf_op jit(solution)/shard_map/all_gather | solution.py:67
  128.3 230.3 %all-gather.17.cloned.1.call-start = ((), (), s32[]{:S(2)}) async-start(), calls=%async_computation.5 | async-start | bytes 11280384 | tf_op jit(solution)/shard_map/all_gather | solution.py:68
  128.9 319.0 %all-gather.19.cloned.1.call-start = ((), (), s32[]{:S(2)}) async-start(), calls=%async_computation.6 | async-start | bytes 11280384 | tf_op jit(solution)/shard_map/all_gather | solution.py:69
  129.5 410.7 %all-reduce.26.cloned.1.call-start = ((), (), s32[]{:S(2)}) async-start(), calls=%async_computation.7 | async-start | bytes 3145728 | tf_op jit(solution)/shard_map/psum | solution.py:37
  129.5 50.3 %copy-start.90 = (f32[1536]{0:T(1024)}, f32[1536]{0:T(1024)S(1)}, u32[]{:S(2)}) copy-start(f32[1536]{0:T(1024)S(1)} %convert_element_type.211) | copy-start | bytes 18436
  179.9 360.3 %copy-start = (f32[256,1536]{1,0:T(8,128)}, f32[256,1536]{1,0:T(8,128)S(1)}, u32[]{:S(2)}) copy-start(f32[256,1536]{1,0:T(8,128)S(1)} %get-tuple-element.665) | copy-start | bytes 4718596
  180.7 177.9 %copy-start.27 = (bf16[256,1536]{1,0:T(8,128)(2,1)}, bf16[256,1536]{1,0:T(8,128)(2,1)S(1)}, u32[]{:S(2)}) copy-start(bf16[256,1536]{1,0:T(8,128)(2,1)S(1)} %multiply_convert_fusion.8) | copy-start | bytes 2359300
  456.7 41.5 copy-start.129
  456.7 41.5 copy-start.127
  456.7 41.5 copy-start.97
  456.7 104.5 %all-gather.21.cloned.1.call-start = ((), (), s32[]{:S(2)}) async-start(), calls=%async_computation.8 | async-start | bytes 2506752 | tf_op jit(solution)/shard_map/all_gather | solution.py:86
  457.5 149.3 %all-gather.23.cloned.1.call-start = ((), (), s32[]{:S(2)}) async-start(), calls=%async_computation.9 | async-start | bytes 2506752 | tf_op jit(solution)/shard_map/all_gather | solution.py:89
  458.2 207.3 %all-reduce.28.cloned.1.call-start = ((), (), s32[]{:S(2)}) async-start(), calls=%async_computation.10 | async-start | bytes 3145728 | tf_op jit(solution)/shard_map/psum | solution.py:37
  458.3 83.5 %copy-start.92 = (f32[1536]{0:T(1024)}, f32[1536]{0:T(1024)S(1)}, u32[]{:S(2)}) copy-start(f32[1536]{0:T(1024)S(1)} %convert_element_type.214) | copy-start | bytes 18436
  498.2 45.3 %copy-start.123 = (f32[64]{0:T(128)}, f32[64]{0:T(128)S(1)}, u32[]{:S(2)}) copy-start(f32[64]{0:T(128)S(1)} %convert_element_type.216) | copy-start | bytes 772
  498.2 67.9 %copy-start.125 = (f32[64]{0:T(128)}, f32[64]{0:T(128)S(1)}, u32[]{:S(2)}) copy-start(f32[64]{0:T(128)S(1)} %convert_element_type.218) | copy-start | bytes 772
  540.1 26.9 copy-start.77
  540.1 26.9 copy-start.80
  543.0 18.2 copy-start.12
  543.5 21.1 copy-start.94
  610.6 146.2 %all-gather.25.cloned.1.call-start = ((), (), s32[]{:S(2)}) async-start(), calls=%async_computation.11 | async-start | bytes 11280384 | tf_op jit(solution)/shard_map/all_gather | solution.py:91
  611.3 234.8 %all-gather.27.cloned.1.call-start = ((), (), s32[]{:S(2)}) async-start(), calls=%async_computation.12 | async-start | bytes 11280384 | tf_op jit(solution)/shard_map/all_gather | solution.py:92
  611.9 323.7 %all-gather.29.cloned.1.call-start = ((), (), s32[]{:S(2)}) async-start(), calls=%async_computation.13 | async-start | bytes 11280384 | tf_op jit(solution)/shard_map/all_gather | solution.py:93
  612.6 396.7 %all-reduce.30.cloned.1.call-start = ((), (), s32[]{:S(2)}) async-start(), calls=%async_computation.14 | async-start | bytes 3145728 | tf_op jit(solution)/shard_map/psum | solution.py:37
  959.6 137.9 %reduce-scatter.2.cloned.1.call-start = ((), (), s32[]{:S(2)}) async-start(), calls=%async_computation.15 | async-start | bytes 1310720 | tf_op jit(solution)/shard_map/reduce_scatter | solution.py:465
  1046.7 88.5 %all-reduce.32.cloned.1.call-start = ((), (), s32[]{:S(2)}) async-start(), calls=%async_computation.16 | async-start | bytes 1572864 | tf_op jit(solution)/shard_map/psum | solution.py:497
  1061.0 37.7 copy-start.79
  1061.0 37.7 copy-start.82
  1061.0 37.7 copy-start.45
  1061.0 37.7 copy-start.95
  1061.0 37.7 copy-start.124
  1063.0 36.6 copy-start.37
  1100.8 34.5 copy-start.93
  1102.1 35.0 copy-start.15
  1102.1 109.0 %all-reduce.34.cloned.1.call-start = ((), (), s32[]{:S(2)}) async-start(), calls=%async_computation.17 | async-start | bytes 3145728 | tf_op jit(solution)/shard_map/psum | solution.py:37
  1137.1 10.8 slice-start.2
  1138.4 9.5 copy-start.22
  1138.4 9.5 slice-start.3
  1138.4 9.5 slice-start.4
  1159.4 573.6 %all-reduce.40.cloned.1.call-start = ((), (), s32[]{:S(2)}) async-start(), calls=%async_computation.20 | async-start | bytes 6291456 | tf_op jit(solution)/shard_map/psum | solution.py:37
  1168.3 42.8 %copy-start.1 = (f32[256,1536]{1,0:T(8,128)S(1)}, f32[256,1536]{1,0:T(8,128)}, u32[]{:S(2)}) copy-start(f32[256,1536]{1,0:T(8,128)} %copy-done) | copy-start | bytes 4718596
  1168.3 42.8 %copy-start.91 = (f32[1536]{0:T(1024)S(1)}, f32[1536]{0:T(1024)}, u32[]{:S(2)}) copy-start(f32[1536]{0:T(1024)} %copy-done.90) | copy-start | bytes 18436
  1177.1 36.6 copy-start.23
  1219.5 5.8 collective-permute-start.1
  1229.6 1606.8 %all-reduce.38.cloned.1.call-start = ((), (), s32[]{:S(2)}) async-start(), calls=%async_computation.19 | async-start | bytes 152600576
  1260.4 21.1 copy-start.47
  1260.4 21.1 copy-start.56
  1311.3 19.8 copy-start.13
  1573.6 2633.7 %all-reduce.36.cloned.1.call-start = ((), (), s32[]{:S(2)}) async-start(), calls=%async_computation.18 | async-start | bytes 165183488
  1585.1 20.1 copy-start.63
  1614.3 20.0 copy-start.24
  1614.3 20.0 copy-start.66
  1643.3 20.6 copy-start.11
  1643.3 20.6 copy-start.49
  1709.6 23.4 copy-start.121
  1776.9 15.3 copy-start.106
  1969.3 69.5 %copy-start.4 = (f32[256,1536]{1,0:T(8,128)S(1)}, f32[256,1536]{1,0:T(8,128)}, u32[]{:S(2)}) copy-start(f32[256,1536]{1,0:T(8,128)} %copy-done.2) | copy-start | bytes 4718596
  (98 other events, 321.5 us)
Sparse Core Ops, SparseCore 0:
  10.4 70.3 all-gather.10
  83.1 40.9 all-gather.12
  127.9 50.2 all-reduce.23
  180.6 88.6 all-gather.14
  271.7 86.8 all-gather.16
  361.0 86.8 all-gather.18
  456.9 49.6 all-reduce.25
  508.8 44.0 all-gather.20
  555.2 44.1 all-gather.22
  610.7 54.7 all-reduce.27
  668.1 88.6 all-gather.24
  759.2 86.8 all-gather.26
  848.7 86.8 all-gather.28
  959.7 49.6 all-reduce.29
  1046.8 50.6 reduce-scatter.1
  1102.2 32.9 all-reduce.31
  1159.5 51.4 all-reduce.33
  1229.8 85.0 all-reduce.39
  1573.7 1262.7 all-reduce.37
  2840.6 1366.6 all-reduce.35
where the time goes:
time: 4280 us; the launch traced here: 4260 us
  waiting for transfers between devices  2920 us (68%)
  local copies, waits for them, and re-layouts  795 us (19%)
  blocking collectives  257 us (6%)
  matrix products  221 us (5%)
  other arithmetic  43.8 us (1%)
    unnamed x22, waiting for transfers between devices  2130 us
    unnamed x286, local copies, waits for them, and re-layouts  360 us
    psum x6, waiting for transfers between devices, tensor_total(): return lax.psum(term_sum, 'tensor')  185 us
    reshape x16, local copies, waits for them, and re-layouts, pack_grads(): flattened.append(jnp.moveaxis(gradient, dim_index, 0).reshape(pieces, -1))  164 us
    concatenate x2, local copies, waits for them, and re-layouts, pack_grads(): return jnp.concatenate(flattened, 1)  116 us
    all_gather x1, waiting for transfers between devices, gather_mixer(): lax.all_gather(gate_first, ('dp', 'ctx'), axis=0, tiled=True)  88.6 us
    all_gather x1, waiting for transfers between devices, gather_attend(): lax.all_gather(gate_second, ('dp', 'ctx'), axis=0, tiled=True)  87.4 us
  transfers between devices with their start and end apart: 22, of which 17 were waited for; matrix products, arithmetic and copies ran while one was open for 21% of the time, Pallas kernels for 0%

commit v1 on v0

v1 whole, which is shorter than its diff:
```python
import functools
import math

import jax
import jax.numpy as jnp
from jax import lax
from jax.experimental import pallas as pl
from jax.experimental.pallas import tpu as pltpu
from jax.sharding import PartitionSpec as P

H = 24
KV = 8
HD = 64
GROUPS = H // KV
LANES = 128

epsilon = 1e-05
MESH = pl.DeviceIdType.MESH


def plane_place():
    dp = lax.axis_index("dp")
    ten = lax.axis_index("tensor")
    core = lax.rem(dp, 2)
    across = lax.rem(dp + 2, 4)
    twin = dp + 1 - 2 * core
    return dp, ten, core, across, twin


def greet(dp, ten, across, twin):
    barrier = pltpu.get_barrier_semaphore()
    pl.semaphore_signal(barrier, 1, device_id={"dp": across}, device_id_type=MESH)
    pl.semaphore_signal(barrier, 1, device_id={"tensor": 1 - ten}, device_id_type=MESH)
    pl.semaphore_signal(barrier, 1, device_id={"dp": twin}, device_id_type=MESH)
    pl.semaphore_wait(barrier, 3)


def remote(src, dst, send, recv, place):
    return pltpu.make_async_remote_copy(
        src_ref=src,
        dst_ref=dst,
        send_sem=send,
        recv_sem=recv,
        device_id=place,
        device_id_type=MESH,
    )


def gather_kernel(x_ref, o_ref, own_sem, send, recv):
    dp, ten, core, across, twin = plane_place()
    greet(dp, ten, across, twin)
    to_across = {"dp": across, "tensor": ten}
    to_side = {"dp": dp, "tensor": 1 - ten}
    to_twin = {"dp": twin, "tensor": ten}
    own = dp * 2 + ten
    first = (across * (1 - core) + dp * core) * 2 + ten * (1 - core) + (1 - ten) * core
    other = (dp * (1 - core) + across * core) * 2 + (1 - ten) * (1 - core) + ten * core
    onward = {
        "dp": dp * (1 - core) + across * core,
        "tensor": (1 - ten) * (1 - core) + ten * core,
    }
    far = across * 2 + 1 - ten

    def move(src, slot, number, place):
        copy = remote(src, o_ref.at[slot], send.at[number], recv.at[slot], place)
        copy.start()
        return copy

    copies = [
        move(x_ref, own, 0, to_across),
        move(x_ref, own, 1, to_side),
        move(x_ref, own, 2, to_twin),
    ]
    local = pltpu.make_async_copy(x_ref, o_ref.at[own], own_sem)
    local.start()

    def arrived(slot):
        remote(x_ref, o_ref.at[slot], send.at[0], recv.at[slot], to_twin).wait_recv()

    arrived(first)
    copies.append(move(o_ref.at[first], first, 3, onward))
    copies.append(move(o_ref.at[first], first, 4, to_twin))
    arrived(other)
    copies.append(move(o_ref.at[other], other, 5, to_twin))
    arrived(far)
    copies.append(move(o_ref.at[far], far, 6, to_twin))
    twin_across = lax.rem(twin + 2, 4)
    for there in (twin, twin_across):
        for side in range(2):
            arrived(there * 2 + side)
    local.wait()
    for copy in copies:
        copy.wait_send()


def plane_gather(block):
    rows, width = block.shape
    slots = lax.axis_size("dp") * lax.axis_size("tensor")
    gathered = pl.pallas_call(
        gather_kernel,
        out_shape=jax.ShapeDtypeStruct((slots, rows, width), block.dtype),
        in_specs=[pl.BlockSpec(memory_space=pltpu.VMEM)],
        out_specs=pl.BlockSpec(memory_space=pl.ANY),
        scratch_shapes=[
            pltpu.SemaphoreType.DMA,
            pltpu.SemaphoreType.DMA((7,)),
            pltpu.SemaphoreType.DMA((8,)),
        ],
        compiler_params=pltpu.CompilerParams(
            collective_id=1, has_side_effects=True, vmem_limit_bytes=16 << 20
        ),
    )(block)
    return gathered.reshape(slots * rows, width)


def scatter_kernel(p_ref, o_ref, mine, theirs, out_box, in_box, load, send, recv):
    dp, ten, core, across, twin = plane_place()
    greet(dp, ten, across, twin)
    twin_across = lax.rem(twin + 2, 4)
    to_twin = {"dp": twin, "tensor": ten}
    sides = (ten, 1 - ten, ten, 1 - ten)
    home = (dp, dp, across, across)
    away = (twin, twin, twin_across, twin_across)
    order = (3, 1, 2, 0)
    loads = {}
    gifts = {}
    for rel in order:
        gifts[rel] = remote(
            p_ref.at[away[rel] * 2 + sides[rel]],
            theirs.at[rel],
            send.at[rel],
            recv.at[rel],
            to_twin,
        )
        gifts[rel].start()
        loads[rel] = pltpu.make_async_copy(
            p_ref.at[home[rel] * 2 + sides[rel]], mine.at[rel], load.at[rel]
        )
        loads[rel].start()
    direct = 1 + core
    relayed = 2 - core
    to_direct = {
        "dp": dp * (1 - core) + across * core,
        "tensor": (1 - ten) * (1 - core) + ten * core,
    }
    to_relayed = {
        "dp": across * (1 - core) + dp * core,
        "tensor": ten * (1 - core) + (1 - ten) * core,
    }

    def total(rel):
        return mine[rel].astype(jnp.float32) + theirs[rel].astype(jnp.float32)

    def post(number, value, place):
        out_box[number] = value.astype(out_box.dtype)
        copy = remote(
            out_box.at[number], in_box.at[number], send.at[4 + number], recv.at[4 + number], place
        )
        copy.start()
        return copy

    loads[3].wait()
    gifts[3].wait_recv()
    relay = post(0, total(3), to_direct)
    for rel in (1, 2):
        loads[rel].wait()
        gifts[rel].wait_recv()
    straight = post(1, total(direct), to_direct)
    relay.wait_recv()
    bent = post(2, total(relayed) + in_box[0].astype(jnp.float32), to_relayed)
    loads[0].wait()
    gifts[0].wait_recv()
    partial = total(0)
    straight.wait_recv()
    partial = partial + in_box[1].astype(jnp.float32)
    bent.wait_recv()
    o_ref[...] = partial + in_box[2].astype(jnp.float32)
    for rel in order:
        gifts[rel].wait_send()
    for copy in (relay, straight, bent):
        copy.wait_send()


def plane_scatter(partial):
    slots = lax.axis_size("dp") * lax.axis_size("tensor")
    rows, width = partial.shape[0] // slots, partial.shape[1]
    block = (rows, width)
    return pl.pallas_call(
        scatter_kernel,
        out_shape=jax.ShapeDtypeStruct(block, jnp.float32),
        in_specs=[pl.BlockSpec(memory_space=pl.ANY)],
        out_specs=pl.BlockSpec(memory_space=pltpu.VMEM),
        scratch_shapes=[
            pltpu.VMEM((4,) + block, jnp.bfloat16),
            pltpu.VMEM((4,) + block, jnp.bfloat16),
            pltpu.VMEM((3,) + block, jnp.bfloat16),
            pltpu.VMEM((3,) + block, jnp.bfloat16),
            pltpu.SemaphoreType.DMA((4,)),
            pltpu.SemaphoreType.DMA((7,)),
            pltpu.SemaphoreType.DMA((7,)),
        ],
        compiler_params=pltpu.CompilerParams(
            collective_id=2, has_side_effects=True, vmem_limit_bytes=24 << 20
        ),
    )(partial.astype(jnp.bfloat16).reshape((slots,) + block))


def swap_kernel(x_ref, o_ref, own_sem, send, recv):
    dp = lax.axis_index("dp")
    ten = lax.axis_index("tensor")
    barrier = pltpu.get_barrier_semaphore()
    for step in (1, 2, 3):
        pl.semaphore_signal(
            barrier,
            1,
            device_id={"dp": lax.rem(dp + step, 4), "tensor": ten},
            device_id_type=MESH,
        )
    pl.semaphore_wait(barrier, 3)
    copies = []
    for step in (2, 1, 3):
        there = lax.rem(dp + step, 4)
        copy = remote(
            x_ref.at[there],
            o_ref.at[dp],
            send.at[step],
            recv.at[step],
            {"dp": there, "tensor": ten},
        )
        copy.start()
        copies.append(copy)
    local = pltpu.make_async_copy(x_ref.at[dp], o_ref.at[dp], own_sem)
    local.start()
    for copy in copies:
        copy.wait()
    local.wait()


def swap_blocks(blocks, number):
    return pl.pallas_call(
        swap_kernel,
        out_shape=jax.ShapeDtypeStruct(blocks.shape, blocks.dtype),
        in_specs=[pl.BlockSpec(memory_space=pltpu.VMEM)],
        out_specs=pl.BlockSpec(memory_space=pl.ANY),
        scratch_shapes=[
            pltpu.SemaphoreType.DMA,
            pltpu.SemaphoreType.DMA((4,)),
            pltpu.SemaphoreType.DMA((4,)),
        ],
        compiler_params=pltpu.CompilerParams(
            collective_id=number, has_side_effects=True, vmem_limit_bytes=16 << 20
        ),
    )(blocks)


def return_blocks(blocks):
    dp = lax.axis_index("dp")
    devices = range(lax.axis_size("dp"))
    parts = [lax.dynamic_index_in_dim(blocks, dp, 0, keepdims=False)]
    for flip in (1, 2, 3):
        sent = lax.dynamic_index_in_dim(blocks, dp ^ flip, 0, keepdims=False)
        parts.append(lax.ppermute(sent, "dp", [(i, i ^ flip) for i in devices]))
    ordered = [lax.select_n(dp, *(parts[j ^ i] for i in devices)) for j in devices]
    return jnp.stack(ordered, 1)


def from_all_dp(block):
    dp = lax.axis_index("dp")
    devices = range(lax.axis_size("dp"))
    parts = [block] + [
        lax.ppermute(block, "dp", [(i, i ^ flip) for i in devices]) for flip in (1, 2, 3)
    ]
    return jnp.concatenate([lax.select_n(dp, *(parts[j ^ i] for i in devices)) for j in devices], 0)


def after(values, *others):
    return lax.optimization_barrier((values,) + others)[0]


def small_sum_kernel(x_ref, o_ref, plane_box, plane_sum, line_box, send, recv, line_send, line_recv):
    dp, ten, ctx = (lax.axis_index(name) for name in ("dp", "tensor", "ctx"))
    dps, tens, ctxs = (lax.axis_size(name) for name in ("dp", "tensor", "ctx"))
    slots = dps * tens
    own = dp * tens + ten
    barrier = pltpu.get_barrier_semaphore()

    def plane_peer(step):
        slot = lax.rem(own + step, slots)
        return {"dp": slot // tens, "tensor": lax.rem(slot, tens), "ctx": ctx}

    def line_peer(step):
        return {"dp": dp, "tensor": ten, "ctx": lax.rem(ctx + step, ctxs)}

    for step in range(1, slots):
        pl.semaphore_signal(barrier, 1, device_id=plane_peer(step), device_id_type=MESH)
    for step in range(1, ctxs):
        pl.semaphore_signal(barrier, 1, device_id=line_peer(step), device_id_type=MESH)
    pl.semaphore_wait(barrier, slots + ctxs - 2)
    copies = []
    for step in range(1, slots):
        copy = remote(
            x_ref, plane_box.at[step], send.at[step], recv.at[step], plane_peer(step)
        )
        copy.start()
        copies.append(copy)
    total = x_ref[...]
    for copy in copies:
        copy.wait_recv()
    for step in range(1, slots):
        total = total + plane_box[step]
    plane_sum[...] = total
    lines = []
    for step in range(1, ctxs):
        copy = remote(
            plane_sum, line_box.at[step], line_send.at[step], line_recv.at[step], line_peer(step)
        )
        copy.start()
        lines.append(copy)
    for copy in lines:
        copy.wait_recv()
    for step in range(1, ctxs):
        total = total + line_box[step]
    o_ref[...] = total
    for copy in copies + lines:
        copy.wait_send()


def small_sum(values, number):
    count = values.size
    rows = -(-count // (8 * LANES)) * 8
    block = jnp.pad(values.reshape(-1), (0, rows * LANES - count)).reshape(rows, LANES)
    slots = lax.axis_size("dp") * lax.axis_size("tensor")
    ctxs = lax.axis_size("ctx")
    total = pl.pallas_call(
        small_sum_kernel,
        out_shape=jax.ShapeDtypeStruct(block.shape, jnp.float32),
        in_specs=[pl.BlockSpec(memory_space=pltpu.VMEM)],
        out_specs=pl.BlockSpec(memory_space=pltpu.VMEM),
        scratch_shapes=[
            pltpu.VMEM((slots,) + block.shape, jnp.float32),
            pltpu.VMEM(block.shape, jnp.float32),
            pltpu.VMEM((ctxs,) + block.shape, jnp.float32),
            pltpu.SemaphoreType.DMA((slots,)),
            pltpu.SemaphoreType.DMA((slots,)),
            pltpu.SemaphoreType.DMA((ctxs,)),
            pltpu.SemaphoreType.DMA((ctxs,)),
        ],
        compiler_params=pltpu.CompilerParams(
            collective_id=number, has_side_effects=True, vmem_limit_bytes=16 << 20
        ),
    )(block)
    return total.reshape(-1)[:count]


def rms_scale(values):
    return lax.rsqrt(jnp.mean(values * values, -1, keepdims=True) + epsilon)


def rms_back(values, upstream):
    row_scale = rms_scale(values)
    normed = values * row_scale
    return row_scale * (upstream - normed * jnp.mean(upstream * normed, -1, keepdims=True))


def low(values):
    return values.astype(jnp.bfloat16)


def wide(values):
    return values.astype(jnp.float32)


def dot_nn(left, right):
    return lax.dot_general(left, right, (((1,), (0,)), ((), ())), preferred_element_type=jnp.float32)


def dot_nt(left, right):
    return lax.dot_general(left, right, (((1,), (1,)), ((), ())), preferred_element_type=jnp.float32)


def dot_tn(left, right):
    return lax.dot_general(left, right, (((0,), (0,)), ((), ())), preferred_element_type=jnp.float32)


def shifted(block, axis, distance):
    devices = range(lax.axis_size(axis))
    route = [(i - distance, i) for i in devices if i - distance in devices]
    return lax.ppermute(block, axis, route)


def rotary_tables(positions, head_dim):
    half_dim = head_dim // 2
    freqs = jnp.exp(-math.log(1000000.0) * 2.0 * jnp.arange(half_dim, dtype=jnp.float32) / head_dim)
    angles = wide(positions)[..., None] * freqs
    return (jnp.cos(angles), jnp.sin(angles))


def rotate(values, cosine, sine):
    half_dim = values.shape[-1] // 2
    first, second = values[..., :half_dim], values[..., half_dim:]
    return jnp.concatenate([first * cosine - second * sine, second * cosine + first * sine], -1)


def column_blocks(weight, count, width):
    rows, columns = weight.shape
    weight = jnp.pad(weight, ((0, 0), (0, count * width - columns)))
    return weight.reshape(rows, count, width).transpose(1, 0, 2)


def spread_weights(blocks, number):
    mine = swap_blocks(blocks, number)
    whole = lax.all_gather(mine, "ctx", axis=0, tiled=False)
    return whole.reshape(-1, whole.shape[-1])


def collect_grads(grad):
    ctx, count = lax.axis_size("ctx"), lax.axis_size("dp")
    grad = low(grad).reshape(ctx, -1, grad.shape[-1])
    summed = lax.psum_scatter(grad, "ctx", scatter_dimension=0, tiled=False)
    return summed.reshape(count, -1, summed.shape[-1])


def finish_grads(summed):
    return wide(return_blocks(summed))


def feed_forward(normed, weights, width):
    both = dot_nn(normed, weights[:, : 2 * width])
    gate, lift = both[:, :width], both[:, width:]
    hidden = low(jax.nn.silu(gate) * lift)
    partial = dot_nt(hidden, weights[:, 2 * width :])
    return partial, (gate, lift, hidden)


def feed_backward(grad_all, normed, weights, width, saved):
    gate, lift, hidden = saved
    down_grad = low(dot_tn(grad_all, hidden))
    hidden_grad = dot_nn(grad_all, after(weights[:, 2 * width :], down_grad))
    sig = jax.nn.sigmoid(gate)
    gate_grad = low(hidden_grad * lift * sig * (1.0 + gate * (1.0 - sig)))
    lift_grad = low(hidden_grad * gate * sig)
    gate_weight_grad = low(dot_tn(normed, gate_grad))
    lift_weight_grad = low(dot_tn(normed, lift_grad))
    gate_low, lift_low = lax.optimization_barrier(
        (gate_grad, lift_grad, gate_weight_grad, lift_weight_grad)
    )[:2]
    partial = dot_nt(gate_low, weights[:, :width]) + dot_nt(
        lift_low, weights[:, width : 2 * width]
    )
    return partial, (gate_weight_grad, lift_weight_grad, down_grad)


def shards(
    hidden_in,
    doc_pos,
    mixer_gain,
    mixer_in,
    conv_taps,
    mixer_out,
    feed_first,
    gate_first,
    lift_first,
    down_first,
    attend_gain,
    query_proj,
    key_proj,
    value_proj,
    query_gain,
    key_gain,
    attend_out,
    feed_second,
    gate_second,
    lift_second,
    down_second,
    output_grad,
):
    dp, ten, ctx = (lax.axis_index(name) for name in ("dp", "tensor", "ctx"))
    seqs, tens, ctxs = (lax.axis_size(name) for name in ("dp", "tensor", "ctx"))
    rows, width = hidden_in.shape[1], hidden_in.shape[2]
    own_rows = rows // tens
    part = mixer_gain.shape[0]
    channels = mixer_in.shape[2] // seqs
    units = gate_first.shape[1]
    feed_width = -(-units // (seqs * LANES)) * LANES

    def regroup(values):
        lead = values.shape[:-1]
        return values.reshape(lead + (seqs, ctxs, part)).swapaxes(-3, -2).reshape(lead + (width,))

    def restore(values):
        lead = values.shape[:-1]
        return values.reshape(lead + (ctxs, seqs, part)).swapaxes(-3, -2).reshape(lead + (width,))

    mixer_blocks = jnp.concatenate(
        [column_blocks(mixer_in[k], seqs, channels) for k in range(3)]
        + [column_blocks(mixer_out.T, seqs, channels)],
        -1,
    )
    own_gains = jnp.stack([mixer_gain, feed_first, attend_gain, feed_second], 1)
    own_gains = jnp.pad(own_gains, ((0, 0), (0, LANES - 4)))
    own_gains = jnp.broadcast_to(own_gains, (seqs, part, LANES))
    mixer_w = spread_weights(jnp.concatenate([mixer_blocks, own_gains], -1), 3)
    gains = wide(mixer_w[:, 4 * channels : 4 * channels + 4]).T
    first_blocks = jnp.concatenate(
        [column_blocks(w, seqs, feed_width) for w in (gate_first, lift_first, down_first.T)], -1
    )
    first_w = spread_weights(first_blocks, 4)
    q_cols, kv_cols = query_proj.shape[1] // seqs, key_proj.shape[1] // seqs
    attend_blocks = jnp.concatenate(
        [
            column_blocks(query_proj, seqs, q_cols),
            column_blocks(key_proj, seqs, kv_cols),
            column_blocks(value_proj, seqs, kv_cols),
            column_blocks(attend_out.T, seqs, q_cols),
        ],
        -1,
    )
    attend_w = spread_weights(attend_blocks, 6)
    second_blocks = jnp.concatenate(
        [column_blocks(w, seqs, feed_width) for w in (gate_second, lift_second, down_second.T)], -1
    )
    second_w = spread_weights(second_blocks, 4)

    positions = from_all_dp(doc_pos)
    own_taps = wide(lax.dynamic_slice_in_dim(conv_taps, dp * channels, channels, 1))

    def own_half(values):
        return regroup(lax.dynamic_slice_in_dim(values[0], ten * own_rows, own_rows, 0))

    stream_zero = wide(own_half(hidden_in))
    upstream = wide(own_half(output_grad))

    def norm_rows(stream, gain):
        return low(stream * rms_scale(stream) * gain)

    mixer_norm = plane_gather(norm_rows(stream_zero, gains[0]))
    mixer_in_w, mixer_out_w = mixer_w[:, : 3 * channels], mixer_w[:, 3 * channels : 4 * channels]
    projected = dot_nn(mixer_norm, mixer_in_w).reshape(seqs, rows, 3 * channels)
    gate_b = projected[..., :channels]
    gate_c = projected[..., channels : 2 * channels]
    conv_input = projected[..., 2 * channels :]
    conv_src = low(gate_b * conv_input)
    earlier = shifted(conv_src[:, -2:], "ctx", 1)
    extended = wide(jnp.concatenate([earlier, conv_src], 1))
    in_doc = [wide(positions >= offset)[..., None] for offset in range(3)]
    conv_sum = sum(
        own_taps[j] * extended[:, 2 - j : 2 - j + rows] * in_doc[j] for j in range(3)
    )
    conv_gated = low(gate_c * conv_sum).reshape(seqs * rows, channels)
    stream_one = stream_zero + plane_scatter(dot_nt(conv_gated, mixer_out_w))

    first_norm = plane_gather(norm_rows(stream_one, gains[1]))
    partial, first_saved = feed_forward(first_norm, first_w, feed_width)
    stream_two = stream_one + plane_scatter(partial)

    attend_norm = plane_gather(norm_rows(stream_two, gains[2]))
    qkv_w = attend_w[:, : q_cols + 2 * kv_cols]
    attend_out_w = attend_w[:, q_cols + 2 * kv_cols :]
    qkv = dot_nn(attend_norm, qkv_w).reshape(seqs, rows, -1)
    queries = qkv[..., :q_cols].reshape(seqs, rows, -1, HD)
    keys = qkv[..., q_cols : q_cols + kv_cols].reshape(seqs, rows, -1, HD)
    values = qkv[..., q_cols + kv_cols :].reshape(seqs, rows, -1, HD)
    cosine, sine = (table[:, :, None] for table in rotary_tables(positions, HD))
    query_scale, key_scale = rms_scale(queries), rms_scale(keys)
    q_gain, k_gain = wide(query_gain), wide(key_gain)
    query_rot = low(rotate(queries * query_scale * q_gain, cosine, sine))
    key_rot = low(rotate(keys * key_scale * k_gain, cosine, sine))
    kv_own = jnp.stack([key_rot, low(values)])
    kv_all = jnp.concatenate(
        [shifted(kv_own, "ctx", distance) for distance in range(ctxs - 1, 0, -1)] + [kv_own], 2
    )
    key_all, value_all = kv_all[0], kv_all[1]
    key_rows = key_all.shape[1]
    heads = kv_cols // HD
    query_g = query_rot.reshape(seqs, rows, heads, GROUPS, HD)
    query_at = jnp.arange(rows, dtype=jnp.int32) + (key_rows - rows)
    query_from = query_at[None] - positions
    key_at = jnp.arange(key_rows, dtype=jnp.int32)
    allowed = (key_at <= query_at[None, :, None]) & (key_at >= query_from[..., None])
    allowed = allowed[:, None, None]
    root = 1.0 / math.sqrt(HD)
    scores = (
        jnp.einsum("sthgd,suhd->shgtu", query_g, key_all, preferred_element_type=jnp.float32) * root
    )
    scores = jnp.where(allowed, scores, -1e30)
    top = jnp.max(scores, -1, keepdims=True)
    weights = jnp.exp(scores - top)
    probs = weights / jnp.sum(weights, -1, keepdims=True)
    probs_low = low(probs)
    context = low(
        jnp.einsum("shgtu,suhd->sthgd", probs_low, value_all, preferred_element_type=jnp.float32)
    ).reshape(seqs * rows, q_cols)
    stream_three = stream_two + plane_scatter(dot_nt(context, attend_out_w))

    second_norm = plane_gather(norm_rows(stream_three, gains[3]))
    partial, second_saved = feed_forward(second_norm, second_w, feed_width)
    stream_four = stream_three + plane_scatter(partial)

    def both_halves(values):
        values = low(restore(values))
        other = lax.ppermute(values, "tensor", [(i, 1 - i) for i in range(tens)])
        lower = lax.select_n(ten, values, other)
        upper = lax.select_n(ten, other, values)
        return jnp.concatenate([lower, upper], 0)[None]

    hidden_out = both_halves(stream_four)

    def norm_step(upstream, stream, gain, normed_grad):
        gain_grad = jnp.sum(normed_grad * stream * rms_scale(stream), 0)
        return upstream + rms_back(stream, normed_grad * gain), gain_grad

    grad_all = plane_gather(low(upstream))
    partial, second_grads = feed_backward(grad_all, second_norm, second_w, feed_width, second_saved)
    second_sums = [collect_grads(g) for g in second_grads]
    grad_three, second_gain_grad = norm_step(
        upstream, stream_three, gains[3], plane_scatter(partial)
    )
    grad_three = after(grad_three, second_sums[2])

    grad_all = plane_gather(low(grad_three))
    attend_out_grad = dot_tn(grad_all, context)
    context_grad = low(dot_nn(grad_all, attend_out_w)).reshape(seqs, rows, heads, GROUPS, HD)
    prob_grad = jnp.einsum(
        "sthgd,suhd->shgtu", context_grad, value_all, preferred_element_type=jnp.float32
    )
    delta = jnp.sum(probs * prob_grad, -1, keepdims=True)
    score_grad = low(probs * (prob_grad - delta))
    query_acc = (
        jnp.einsum("shgtu,suhd->sthgd", score_grad, key_all, preferred_element_type=jnp.float32)
        * root
    ).reshape(seqs, rows, -1, HD)
    key_acc = (
        jnp.einsum("shgtu,sthgd->suhd", score_grad, query_g, preferred_element_type=jnp.float32)
        * root
    )
    value_acc = jnp.einsum(
        "shgtu,sthgd->suhd", probs_low, context_grad, preferred_element_type=jnp.float32
    )
    kv_acc = low(jnp.stack([key_acc, value_acc])).reshape(2, seqs, ctxs, rows, heads, HD)
    kv_mine = wide(kv_acc[:, :, ctxs - 1])
    for distance in range(1, ctxs):
        kv_mine = kv_mine + wide(shifted(kv_acc[:, :, ctxs - 1 - distance], "ctx", -distance))
    query_norm_grad = rotate(query_acc, cosine, -sine)
    key_norm_grad = rotate(kv_mine[0], cosine, -sine)
    query_gain_part = jnp.sum(query_norm_grad * queries * query_scale, (0, 1, 2))
    key_gain_part = jnp.sum(key_norm_grad * keys * key_scale, (0, 1, 2))
    query_grad = low(rms_back(queries, query_norm_grad * q_gain)).reshape(seqs * rows, -1)
    key_grad = low(rms_back(keys, key_norm_grad * k_gain)).reshape(seqs * rows, -1)
    value_grad = low(kv_mine[1]).reshape(seqs * rows, -1)
    qkv_grad = jnp.concatenate([query_grad, key_grad, value_grad], -1)
    qkv_weight_grad = dot_tn(attend_norm, qkv_grad)
    attend_grads = low(jnp.concatenate([qkv_weight_grad, attend_out_grad], -1))
    attend_sums = collect_grads(attend_grads)
    grad_two, attend_gain_grad = norm_step(
        grad_three,
        stream_two,
        gains[2],
        plane_scatter(after(low(dot_nt(qkv_grad, qkv_w)), attend_grads)),
    )
    grad_two = after(grad_two, second_sums[0], second_sums[1])

    grad_all = plane_gather(low(grad_two))
    partial, first_grads = feed_backward(grad_all, first_norm, first_w, feed_width, first_saved)
    first_sums = [collect_grads(g) for g in first_grads]
    grad_one, first_gain_grad = norm_step(grad_two, stream_one, gains[1], plane_scatter(partial))
    grad_one = after(grad_one, attend_sums)
    second_done, first_done = (
        [finish_grads(total).reshape(part, -1)[:, :units] for total in sums]
        for sums in (second_sums, first_sums)
    )
    attend_done = finish_grads(attend_sums)

    grad_all = plane_gather(low(grad_one))
    mixer_out_grad = dot_tn(grad_all, conv_gated)
    gated_grad = dot_nn(grad_all, mixer_out_w).reshape(seqs, rows, channels)
    gate_c_grad = low(gated_grad * conv_sum)
    sum_grad = gated_grad * gate_c
    tap_rows = []
    spread = jnp.zeros_like(extended)
    for j in range(3):
        masked = sum_grad * in_doc[j]
        tap_rows.append(jnp.sum(masked * extended[:, 2 - j : 2 - j + rows], (0, 1)))
        spread = spread + jnp.pad(own_taps[j] * masked, ((0, 0), (2 - j, j), (0, 0)))
    returned = shifted(spread[:, :2], "ctx", -1)
    src_grad = spread[:, 2:] + jnp.pad(returned, ((0, 0), (rows - 2, 0), (0, 0)))
    proj_grad = jnp.concatenate(
        [low(src_grad * conv_input), gate_c_grad, low(src_grad * gate_b)], -1
    ).reshape(seqs * rows, 3 * channels)
    mixer_in_grad = dot_tn(mixer_norm, proj_grad)
    mixer_grads = low(jnp.concatenate([mixer_in_grad, mixer_out_grad], -1))
    mixer_done = finish_grads(collect_grads(mixer_grads))
    grad_zero, mixer_gain_grad = norm_step(
        grad_one,
        stream_zero,
        gains[0],
        plane_scatter(after(low(dot_nt(proj_grad, mixer_in_w)), mixer_grads)),
    )
    hidden_grad = both_halves(grad_zero)

    gain_rows = restore(
        jnp.stack([mixer_gain_grad, first_gain_grad, attend_gain_grad, second_gain_grad])
    )
    taps_part = lax.dynamic_update_slice(
        jnp.zeros((tens, 3, channels * seqs), jnp.float32),
        jnp.stack(tap_rows)[None],
        (ten, 0, dp * channels),
    )
    small = jnp.concatenate(
        [gain_rows.reshape(-1), query_gain_part, key_gain_part, taps_part.reshape(-1)]
    )
    small = small_sum(small, 5)
    gain_sums = lax.dynamic_slice_in_dim(
        small[: 4 * width].reshape(4, width), (dp * ctxs + ctx) * part, part, 1
    )
    query_gain_grad = small[4 * width : 4 * width + HD]
    key_gain_grad = small[4 * width + HD : 4 * width + 2 * HD]
    taps_grad = lax.dynamic_index_in_dim(
        small[4 * width + 2 * HD :].reshape(tens, 3, channels * seqs), ten, 0, keepdims=False
    )

    def columns(done, start, count):
        return done[:, :, start : start + count].reshape(part, -1)

    return (
        hidden_out,
        hidden_grad,
        gain_sums[0],
        jnp.stack([columns(mixer_done, k * channels, channels) for k in range(3)]),
        taps_grad,
        columns(mixer_done, 3 * channels, channels).T,
        gain_sums[1],
        first_done[0],
        first_done[1],
        first_done[2].T,
        gain_sums[2],
        columns(attend_done, 0, q_cols),
        columns(attend_done, q_cols, kv_cols),
        columns(attend_done, q_cols + kv_cols, kv_cols),
        query_gain_grad,
        key_gain_grad,
        columns(attend_done, q_cols + 2 * kv_cols, q_cols).T,
        gain_sums[3],
        second_done[0],
        second_done[1],
        second_done[2].T,
    )


def solution(mesh):
    rows = P("dp", "ctx", None)
    gain = P(("dp", "ctx"))
    into = P(("dp", "ctx"), "tensor")
    out = P("tensor", ("dp", "ctx"))
    thrice = P(None, ("dp", "ctx"), "tensor")
    taps = P(None, "tensor")
    weights = (
        (gain, thrice, taps, out, gain, into, into, out)
        + (gain, into, into, into, P(), P(), out)
        + (gain, into, into, out)
    )
    return jax.shard_map(
        shards,
        mesh=mesh,
        in_specs=(rows, P("dp", "ctx")) + weights + (rows,),
        out_specs=(rows, rows) + weights,
        check_vma=False,
    )
```

time: 4280 us -> 986 us (0.23)
  waiting for transfers between devices: 2920 us -> 194 us
  local copies, waits for them, and re-layouts: 795 us -> 106 us
  Pallas kernels: 0 us -> 385 us
  blocking collectives: 257 us -> 0 us
  matrix products: 221 us -> 157 us
    unnamed x22 -> x12, waiting for transfers between devices: 2130 us -> 0.2 us
    all_gather x10 -> x4, waiting for transfers between devices: 527 us -> 71.9 us  [spread_weights(): whole = lax.all_gather(mine, 'ctx', axis=0, tiled=False)]
    pallas_call x0 -> x21, Pallas kernels: none -> 385 us  [the longest x8 159 us: plane_gather(): pl.pallas_call(gather_kernel, out_shape=jax.ShapeDtypeStruct((slots, rows...]
    unnamed x286 -> x344, local copies, waits for them, and re-layouts: 360 us -> 31.4 us
    psum x7 -> x0, waiting for transfers between devices: 218 us -> none  [the longest x6 185 us: tensor_total(): return lax.psum(term_sum, 'tensor')]
    reshape x19 -> x25, local copies, waits for them, and re-layouts: 166 us -> 14.7 us  [the longest x2 3.68 us: shards(): proj_grad = jnp.concatenate([low(src_grad * conv_input), gate_c_grad, low...]
    all_gather x4 -> x0, blocking collectives: 124 us -> none  [the longest x1 41.6 us: gather_attend(): lax.all_gather(value_proj, ('dp', 'ctx'), axis=0, tiled=True)]
    concatenate x3 -> x4, local copies, waits for them, and re-layouts: 119 us -> 4.26 us  [the longest x1 3.2 us: shards(): jnp.concatenate([low(src_grad * conv_input), gate_c_grad, low(src_grad *...]
  transfers between devices with their start and end apart: 22 -> 49, of which waited for: 17 -> 24; matrix products, arithmetic and copies ran while one was open for 21% -> 30% of each run, Pallas kernels for 0% -> 38%
where the time goes in v1:
time: 986 us; the launch traced here: 975 us
  Pallas kernels  385 us (39%)
  waiting for transfers between devices  194 us (20%)
  matrix products  157 us (16%)
  local copies, waits for them, and re-layouts  106 us (11%)
  other arithmetic  74.3 us (8%)
  starting transfers between devices  40.2 us (4%)
  between operations  17.8 us (2%)
    pallas_call x8, Pallas kernels, plane_gather(): pl.pallas_call(gather_kernel, out_shape=jax.ShapeDtypeStruct((slots, rows...  159 us
    pallas_call x8, Pallas kernels, plane_scatter(): pl.pallas_call(scatter_kernel, out_shape=jax.ShapeDtypeStruct(block, jnp....  143 us
    ppermute x8, waiting for transfers between devices, shifted(): return lax.ppermute(block, axis, route)  82.3 us
    all_gather x4, waiting for transfers between devices, spread_weights(): whole = lax.all_gather(mine, 'ctx', axis=0, tiled=False)  71.9 us
    pallas_call x4, Pallas kernels, swap_blocks(): pl.pallas_call(swap_kernel, out_shape=jax.ShapeDtypeStruct(blocks.shape,...  69 us
    dot_general x10, matrix products, dot_tn(): lax.dot_general(left, right, (((0,), (0,)), ((), ())), preferred_element_...  42.7 us
    dot_general x8, matrix products, dot_nn(): lax.dot_general(left, right, (((1,), (0,)), ((), ())), preferred_element_...  42.7 us
    dot_general x10, matrix products, dot_nt(): lax.dot_general(left, right, (((1,), (1,)), ((), ())), preferred_element_...  37.1 us
  transfers between devices with their start and end apart: 49, of which 24 were waited for; matrix products, arithmetic and copies ran while one was open for 30% of the time, Pallas kernels for 38%

profile of v1, /device:TPU:0, one launch (start us, length us, event | category | flops | bytes accessed | tf_op | source)
XLA Modules:
  0.0 974.8 jit_solution(3472365865529095604)
XLA Ops:
  11.6 11.7 %shard_map.373 = bf16[4,96,896]{2,1,0:T(8,128)(2,1)} custom-call(bf16[4,96,896]{2,1,0:T(8,128)(2,1)S(1)} %concatenate.117.x_ref), custom_call_target="tpu_custom_call" | custom-call | tf_op jit(solution)/shard_map/pallas_call | solution.py:240
  23.9 24.9 %shard_map.377 = bf16[4,96,2688]{2,1,0:T(8,128)(2,1)} custom-call(bf16[4,96,2688]{2,1,0:T(8,128)(2,1)S(1)} %pad_maximum_fusion.1.x_ref), custom_call_target="tpu_custom_call" | custom-call | tf_op jit(solution)/shard_map/pallas_call | solution.py:240
  50.1 7.2 shard_map.380
  60.1 25.2 %shard_map.383 = bf16[4,96,2688]{2,1,0:T(8,128)(2,1)} custom-call(bf16[4,96,2688]{2,1,0:T(8,128)(2,1)S(1)} %pad_maximum_fusion.2.x_ref), custom_call_target="tpu_custom_call" | custom-call | tf_op jit(solution)/shard_map/pallas_call | solution.py:240
  88.9 20.0 %shard_map.385 = bf16[8,128,1536]{2,1,0:T(8,128)(2,1)S(1)} custom-call(bf16[128,1536]{1,0:T(8,128)(2,1)S(1)} %copy.399.x_ref), custom_call_target="tpu_custom_call" | custom-call | tf_op jit(solution)/shard_map/pallas_call | solution.py:99
  116.6 20.2 %shard_map.374 = bf16[8,128,1536]{2,1,0:T(8,128)(2,1)S(1)} custom-call(bf16[128,1536]{1,0:T(8,128)(2,1)S(1)} %multiply_convert_fusion.15.x_ref), custom_call_target="tpu_custom_call" | custom-call | tf_op jit(solution)/shard_map/pallas_call | solution.py:99
  139.1 3.2 collective-permute-start
  142.3 9.2 collective-permute-done
  155.4 17.6 %shard_map.375 = f32[128,1536]{1,0:T(8,128)S(1)} custom-call(bf16[8,128,1536]{2,1,0:T(8,128)(2,1)S(1)} %bitcast.717), custom_call_target="tpu_custom_call" | custom-call | tf_op jit(solution)/shard_map/pallas_call | solution.py:188
  174.2 19.2 %shard_map.376 = bf16[8,128,1536]{2,1,0:T(8,128)(2,1)S(1)} custom-call(bf16[128,1536]{1,0:T(8,128)(2,1)S(1)} %multiply_convert_fusion.12.x_ref), custom_call_target="tpu_custom_call" | custom-call | tf_op jit(solution)/shard_map/pallas_call | solution.py:99
  193.5 36.0 %all-gather.11.cloned.1.call-done = bf16[16,96,2688]{2,1,0:T(8,128)(2,1)} async-done(((bf16[4,96,2688]{2,1,0:T(8,128)(2,1)}), bf16[16,96,2688]{2,1,0:T(8,128)(2,1)}) %all-gather.11.cloned.1.call-update) | async-done | bytes 8257552 | tf_op jit(solution)/shard_map/all_gather | solution.py:412
  229.5 8.4 fusion.13
  242.0 6.1 convolution_convert_fusion.5
  248.1 18.7 %shard_map.378 = f32[128,1536]{1,0:T(8,128)S(1)} custom-call(bf16[8,128,1536]{2,1,0:T(8,128)(2,1)S(1)} %bitcast.734), custom_call_target="tpu_custom_call" | custom-call | tf_op jit(solution)/shard_map/pallas_call | solution.py:188
  268.1 19.2 %shard_map.379 = bf16[8,128,1536]{2,1,0:T(8,128)(2,1)S(1)} custom-call(bf16[128,1536]{1,0:T(8,128)(2,1)S(1)} %multiply_convert_fusion.11.x_ref), custom_call_target="tpu_custom_call" | custom-call | tf_op jit(solution)/shard_map/pallas_call | solution.py:99
  290.8 6.5 collective-permute-start.4
  301.5 8.0 collective-permute-done.4
  309.5 11.2 %collective-permute-done.5 = bf16[2,4,256,1,64]{2,4,1,3,0:T(8,128)(2,1)S(1)} collective-permute-done((bf16[2,4,256,1,64]{2,4,1,3,0:T(8,128)(2,1)S(1)}, bf16[2,4,256,1,64]{2,4,1,3,0:T(8,128)(2,1)S(1)}, u32[]{:S(2)}, u32[]{:S(2)}) %collective-permute-start.5) | collective-permute-done | bytes 262176 | tf_op jit(solution)/shard_map/ppermute | solution.py:388
  320.7 11.1 %collective-permute-done.6 = bf16[2,4,256,1,64]{2,4,1,3,0:T(8,128)(2,1)S(1)} collective-permute-done((bf16[2,4,256,1,64]{2,4,1,3,0:T(8,128)(2,1)S(1)}, bf16[2,4,256,1,64]{2,4,1,3,0:T(8,128)(2,1)S(1)}, u32[]{:S(2)}, u32[]{:S(2)}) %collective-permute-start.6) | collective-permute-done | bytes 262176 | tf_op jit(solution)/shard_map/ppermute | solution.py:388
  331.9 6.3 fusion.5
  338.2 7.3 fusion.4
  345.6 6.8 fusion.43
  354.8 17.6 %shard_map.381 = f32[128,1536]{1,0:T(8,128)S(1)} custom-call(bf16[8,128,1536]{2,1,0:T(8,128)(2,1)S(1)} %bitcast.718), custom_call_target="tpu_custom_call" | custom-call | tf_op jit(solution)/shard_map/pallas_call | solution.py:188
  373.6 19.5 %shard_map.382 = bf16[8,128,1536]{2,1,0:T(8,128)(2,1)S(1)} custom-call(bf16[128,1536]{1,0:T(8,128)(2,1)S(1)} %multiply_convert_fusion.10.x_ref), custom_call_target="tpu_custom_call" | custom-call | tf_op jit(solution)/shard_map/pallas_call | solution.py:99
  394.9 35.9 %all-gather.15.cloned.1.call-done = bf16[16,96,2688]{2,1,0:T(8,128)(2,1)} async-done(((bf16[4,96,2688]{2,1,0:T(8,128)(2,1)}), bf16[16,96,2688]{2,1,0:T(8,128)(2,1)}) %all-gather.15.cloned.1.call-update) | async-done | bytes 8257552 | tf_op jit(solution)/shard_map/all_gather | solution.py:412
  430.8 9.4 fusion.11
  444.4 4.8 convolution_convert_fusion.11
  452.0 7.7 multiply_convert_fusion.2
  459.6 4.8 convolution_convert_fusion.9
  473.3 7.6 convolution_convert_fusion.10
  481.0 5.4 fusion.21
  486.4 5.5 add_convert_fusion.1
  492.0 18.8 %shard_map.386 = f32[128,1536]{1,0:T(8,128)S(1)} custom-call(bf16[8,128,1536]{2,1,0:T(8,128)(2,1)S(1)} %bitcast.731), custom_call_target="tpu_custom_call" | custom-call | tf_op jit(solution)/shard_map/pallas_call | solution.py:188
  510.7 5.5 convolution_convert_fusion.4
  516.3 17.6 %shard_map.384 = f32[128,1536]{1,0:T(8,128)S(1)} custom-call(bf16[8,128,1536]{2,1,0:T(8,128)(2,1)S(1)} %bitcast.732), custom_call_target="tpu_custom_call" | custom-call | tf_op jit(solution)/shard_map/pallas_call | solution.py:188
  538.0 19.4 %shard_map.387 = bf16[8,128,1536]{2,1,0:T(8,128)(2,1)S(1)} custom-call(bf16[128,1536]{1,0:T(8,128)(2,1)S(1)} %convert_element_type.363.x_ref), custom_call_target="tpu_custom_call" | custom-call | tf_op jit(solution)/shard_map/pallas_call | solution.py:99
  560.9 10.1 %fusion = (f32[4,3,256]{2,1,0:T(4,128)S(1)}, f32[4,1024,256,3]{2,1,3,0:T(8,128)}) fusion(f32[4,3,256]{2,1,0:T(4,128)} %copy-done.107, f32[4,3,256]{2,1,0:T(4,128)} %copy-done.105, f32[4,1024,256,3]{2,1,3,0:T(8,128)} %get-tuple-element.291, pred[4,256,1024]{1,2,0:T(8,128)(4,1)} %fusion.15, bf16[4,256,3,64]{1,0,3,2:T(4,128)(2,1)S(1)} %reshape.841, ...), kind=kOutput, calls=%fused_computation.3 | convolution fusion | flops 421524480 | bytes 27176960 | tf_op jit(solution)/shard_map/sthgd,suhd->shgtu/dot_general | solution.py:623
  571.1 10.8 %fusion.6 = bf16[4,3,256,1024]{2,3,1,0:T(8,128)(2,1)S(1)} fusion(f32[4,1024,256,3]{2,1,3,0:T(8,128)} %get-tuple-element.293, f32[4,3,256]{2,1,0:T(4,128)S(1)} %get-tuple-element.292, f32[4,3,256]{2,1,0:T(4,128)S(1)} %copy-done.108, f32[4,3,256]{2,1,0:T(4,128)S(1)} %copy-done.106, f32[4,1024,256,3]{2,1,3,0:T(8,128)} %get-tuple-element.291, ...), kind=kLoop, calls=%fused_computation.10 | loop fusion | flops 22020096 | bytes 32542720 | tf_op jit(solution)/shard_map/reshape.25
  591.9 4.7 fusion.39
  599.0 5.6 fusion.42
  618.0 3.2 convolution_convert_fusion.15
  621.5 8.4 collective-permute-done.10
  629.9 3.8 collective-permute-done.8
  633.8 12.3 %collective-permute-done.9 = bf16[2,4,256,1,64]{2,4,1,0,3:T(8,128)(2,1)} collective-permute-done((bf16[2,4,256,1,64]{2,4,1,0,3:T(8,128)(2,1)}, bf16[2,4,256,1,64]{2,4,1,0,3:T(8,128)(2,1)}, u32[]{:S(2)}, u32[]{:S(2)}) %collective-permute-start.9) | collective-permute-done | bytes 262176 | tf_op jit(solution)/shard_map/ppermute | solution.py:388
  656.1 17.8 %shard_map.388 = f32[128,1536]{1,0:T(8,128)S(1)} custom-call(bf16[8,128,1536]{2,1,0:T(8,128)(2,1)S(1)} %bitcast.729), custom_call_target="tpu_custom_call" | custom-call | tf_op jit(solution)/shard_map/pallas_call | solution.py:188
  675.2 19.4 %shard_map.389 = bf16[8,128,1536]{2,1,0:T(8,128)(2,1)S(1)} custom-call(bf16[128,1536]{1,0:T(8,128)(2,1)S(1)} %convert_element_type.375.x_ref), custom_call_target="tpu_custom_call" | custom-call | tf_op jit(solution)/shard_map/pallas_call | solution.py:99
  694.6 4.8 convolution_convert_fusion.8
  707.7 3.5 slice.370
  738.3 7.7 multiply_convert_fusion
  746.0 4.8 convolution_convert_fusion.6
  754.8 5.0 convolution_convert_fusion.7
  759.8 3.4 fusion.18
  763.3 3.7 add_convert_fusion
  767.1 17.6 %shard_map.390 = f32[128,1536]{1,0:T(8,128)S(1)} custom-call(bf16[8,128,1536]{2,1,0:T(8,128)(2,1)S(1)} %bitcast.730), custom_call_target="tpu_custom_call" | custom-call | tf_op jit(solution)/shard_map/pallas_call | solution.py:188
  790.2 22.4 %shard_map.391 = bf16[8,128,1536]{2,1,0:T(8,128)(2,1)S(1)} custom-call(bf16[128,1536]{1,0:T(8,128)(2,1)S(1)} %convert_element_type.382.x_ref), custom_call_target="tpu_custom_call" | custom-call | tf_op jit(solution)/shard_map/pallas_call | solution.py:99
  822.0 3.4 copy.424
  834.1 18.2 %collective-permute-done.11 = f32[4,2,192]{1,2,0:T(8,128)} collective-permute-done((f32[4,2,192]{1,2,0:T(8,128)}, f32[4,2,192]{1,2,0:T(8,128)}, u32[]{:S(2)}, u32[]{:S(2)}) %collective-permute-start.11) | collective-permute-done | bytes 6176 | tf_op jit(solution)/shard_map/ppermute | solution.py:388
  858.9 17.6 %shard_map.392 = f32[128,1536]{1,0:T(8,128)S(1)} custom-call(bf16[8,128,1536]{2,1,0:T(8,128)(2,1)S(1)} %bitcast.733), custom_call_target="tpu_custom_call" | custom-call | tf_op jit(solution)/shard_map/pallas_call | solution.py:188
  877.2 13.0 %shard_map.393 = f32[88,128]{1,0:T(8,128)S(1)} custom-call(f32[88,128]{1,0:T(8,128)S(1)} %pad_bitcast_fusion.x_ref), custom_call_target="tpu_custom_call" | custom-call | tf_op jit(solution)/shard_map/pallas_call | solution.py:334
  893.4 3.5 reshape.888
  897.7 4.3 convolution_convert_fusion.12
  932.3 3.8 collective-permute-done.17
  941.6 11.5 %reduce-scatter.17.cloned.1.call-done = bf16[1,384,768]{1,2,0:T(8,128)(2,1)} async-done(((bf16[4,384,768]{1,2,0:T(8,128)(2,1)}), bf16[1,384,768]{1,2,0:T(8,128)(2,1)}) %reduce-scatter.17.cloned.1.call-update) | async-done | bytes 589840 | tf_op jit(solution)/shard_map/reduce_scatter | solution.py:419
  957.5 3.7 collective-permute-done.14
  (682 shorter events, 225.0 us)
Async XLA Ops:
  7.2 106.6 %all-gather.9.cloned.1.call-start = ((), (), s32[]{:S(2)}) async-start(), calls=%async_computation.16 | async-start | bytes 3440640 | tf_op jit(solution)/shard_map/all_gather | solution.py:412
  23.3 206.2 %all-gather.11.cloned.1.call-start = ((), (), s32[]{:S(2)}) async-start(), calls=%async_computation.17 | async-start | bytes 10321920 | tf_op jit(solution)/shard_map/all_gather | solution.py:412
  48.9 238.4 %all-gather.13.cloned.1.call-start = ((), (), s32[]{:S(2)}) async-start(), calls=%async_computation.18 | async-start | bytes 1966080 | tf_op jit(solution)/shard_map/all_gather | solution.py:412
  57.4 373.4 %all-gather.15.cloned.1.call-start = ((), (), s32[]{:S(2)}) async-start(), calls=%async_computation.19 | async-start | bytes 10321920 | tf_op jit(solution)/shard_map/all_gather | solution.py:412
  57.4 53.2 %collective-permute-start.1 = (s32[1,256]{1,0:T(1,128)S(1)}, s32[1,256]{1,0:T(1,128)S(1)}, u32[]{:S(2)}, u32[]{:S(2)}) collective-permute-start(s32[1,256]{1,0:T(1,128)S(1)} %copy-done.150), channel_id=1, source_target_pairs={{0,8},{8,0},{16,24},{24,16},{1,9},{9,1},{17,25},{25,17},{2,10},{10... | collective-permute-start | bytes 3080 | tf_op jit(solution)/shard_map/ppermute | solution.py:271
  58.1 52.6 %collective-permute-start.2 = (s32[1,256]{1,0:T(1,128)S(1)}, s32[1,256]{1,0:T(1,128)S(1)}, u32[]{:S(2)}, u32[]{:S(2)}) collective-permute-start(s32[1,256]{1,0:T(1,128)S(1)} %copy-done.150), channel_id=1, source_target_pairs={{0,16},{8,24},{16,0},{24,8},{1,17},{9,25},{17,1},{25,9},{2,18},{10... | collective-permute-start | bytes 3080 | tf_op jit(solution)/shard_map/ppermute | solution.py:271
  59.5 51.2 %collective-permute-start.3 = (s32[1,256]{1,0:T(1,128)S(1)}, s32[1,256]{1,0:T(1,128)S(1)}, u32[]{:S(2)}, u32[]{:S(2)}) collective-permute-start(s32[1,256]{1,0:T(1,128)S(1)} %copy-done.150), channel_id=1, source_target_pairs={{0,24},{8,16},{16,8},{24,0},{1,25},{9,17},{17,9},{25,1},{2,26},{10... | collective-permute-start | bytes 3080 | tf_op jit(solution)/shard_map/ppermute | solution.py:271
  85.3 451.8 %reduce-scatter.9.cloned.1.call-start = ((), (), s32[]{:S(2)}) async-start(), calls=%async_computation.8 | async-start | bytes 3440640 | tf_op jit(solution)/shard_map/reduce_scatter | solution.py:419
  86.0 204.1 %copy-start.134 = (f32[32]{0:T(128)}, f32[32]{0:T(128)S(1)}, u32[]{:S(2)}) copy-start(f32[32]{0:T(128)S(1)} %multiply_exponential_fusion) | copy-start | bytes 388
  86.0 30.4 %copy-start.130 = (f32[128]{0:T(128)}, f32[128]{0:T(128)S(1)}, u32[]{:S(2)}) copy-start(f32[128]{0:T(128)S(1)} %add_rsqrt_fusion.5) | copy-start | bytes 1540
  86.8 65.0 %copy-start.124 = (f32[1,192]{1,0:T(1,128)}, f32[1,192]{1,0:T(1,128)S(1)}, u32[]{:S(2)}) copy-start(f32[1,192]{1,0:T(1,128)S(1)} %get-tuple-element.277) | copy-start | bytes 2308
  86.8 65.0 %copy-start.126 = (f32[1,192]{1,0:T(1,128)}, f32[1,192]{1,0:T(1,128)S(1)}, u32[]{:S(2)}) copy-start(f32[1,192]{1,0:T(1,128)S(1)} %get-tuple-element.278) | copy-start | bytes 2308
  86.8 65.0 %copy-start.128 = (f32[1,192]{1,0:T(1,128)}, f32[1,192]{1,0:T(1,128)S(1)}, u32[]{:S(2)}) copy-start(f32[1,192]{1,0:T(1,128)S(1)} %get-tuple-element.279) | copy-start | bytes 2308
  87.4 85.6 %copy-start.14 = (f32[128,1536]{1,0:T(8,128)}, f32[128,1536]{1,0:T(8,128)S(1)}, u32[]{:S(2)}) copy-start(f32[128,1536]{1,0:T(8,128)S(1)} %copy.379) | copy-start | bytes 2359300
  110.7 41.1 %copy-start.113 = (f32[4,256]{1,0:T(4,128)}, f32[4,256]{1,0:T(4,128)S(1)}, u32[]{:S(2)}) copy-start(f32[4,256]{1,0:T(4,128)S(1)} %get-tuple-element.280) | copy-start | bytes 12292
  110.7 41.1 %copy-start.115 = (f32[4,256]{1,0:T(4,128)}, f32[4,256]{1,0:T(4,128)S(1)}, u32[]{:S(2)}) copy-start(f32[4,256]{1,0:T(4,128)S(1)} %get-tuple-element.281) | copy-start | bytes 12292
  110.7 179.4 %copy-start.109 = (f32[4,256]{1,0:T(4,128)}, f32[4,256]{1,0:T(4,128)S(1)}, u32[]{:S(2)}) copy-start(f32[4,256]{1,0:T(4,128)S(1)} %get-tuple-element.276) | copy-start | bytes 12292
  116.4 56.8 %copy-start.98 = (f32[1536]{0:T(1024)}, f32[1536]{0:T(1024)S(1)}, u32[]{:S(2)}) copy-start(f32[1536]{0:T(1024)S(1)} %get-tuple-element.159) | copy-start | bytes 18436
  116.4 150.7 %copy-start.100 = (f32[1536]{0:T(1024)}, f32[1536]{0:T(1024)S(1)}, u32[]{:S(2)}) copy-start(f32[1536]{0:T(1024)S(1)} %get-tuple-element.158) | copy-start | bytes 18436
  139.1 12.5 %collective-permute-start = (bf16[4,2,192]{1,2,0:T(8,128)(2,1)S(1)}, bf16[4,2,192]{1,2,0:T(8,128)(2,1)S(1)}, u32[]{:S(2)}, u32[]{:S(2)}) collective-permute-start(bf16[4,2,192]{1,2,0:T(8,128)(2,1)S(1)} %slice.359), channel_id=1, source_target_pairs={{0,2},{2,4},{4,6},{1,3},{3,5},{5,7},{8,10},{10,12},{12,14},{9,11},... | collective-permute-start | bytes 9224 | tf_op jit(solution)/shard_map/ppermute | solution.py:388
  193.5 44.4 %copy-start.2 = (bf16[8,128,1536]{2,1,0:T(8,128)(2,1)}, bf16[8,128,1536]{2,1,0:T(8,128)(2,1)S(1)}, u32[]{:S(2)}) copy-start(bf16[8,128,1536]{2,1,0:T(8,128)(2,1)S(1)} %shard_map.376) | copy-start | bytes 9437188
  290.8 41.2 %copy-start.28 = (pred[4,256,1024]{1,2,0:T(8,128)(4,1)S(1)}, pred[4,256,1024]{1,2,0:T(8,128)(4,1)}, u32[]{:S(2)}) copy-start(pred[4,256,1024]{1,2,0:T(8,128)(4,1)} %fusion.15) | copy-start | bytes 3145732
  290.8 18.7 %collective-permute-start.4 = (bf16[2,4,256,1,64]{2,4,1,3,0:T(8,128)(2,1)S(1)}, bf16[2,4,256,1,64]{2,4,1,3,0:T(8,128)(2,1)S(1)}, u32[]{:S(2)}, u32[]{:S(2)}) collective-permute-start(bf16[2,4,256,1,64]{2,4,1,3,0:T(8,128)(2,1)S(1)} %pad_maximum_fusion.12), channel_id=1, source_target_pairs={{0,6},{1,7},{8,14},{9,15},{16,22},{17,23},{24,30},{25,31}} | collective-permute-start | bytes 786440 | tf_op jit(solution)/shard_map/ppermute | solution.py:388
  297.3 23.5 %collective-permute-start.5 = (bf16[2,4,256,1,64]{2,4,1,3,0:T(8,128)(2,1)S(1)}, bf16[2,4,256,1,64]{2,4,1,3,0:T(8,128)(2,1)S(1)}, u32[]{:S(2)}, u32[]{:S(2)}) collective-permute-start(bf16[2,4,256,1,64]{2,4,1,3,0:T(8,128)(2,1)S(1)} %pad_maximum_fusion.12), channel_id=1, source_target_pairs={{0,4},{2,6},{1,5},{3,7},{8,12},{10,14},{9,13},{11,15},{16,20},{18,... | collective-permute-start | bytes 786440 | tf_op jit(solution)/shard_map/ppermute | solution.py:388
  298.6 33.2 %collective-permute-start.6 = (bf16[2,4,256,1,64]{2,4,1,3,0:T(8,128)(2,1)S(1)}, bf16[2,4,256,1,64]{2,4,1,3,0:T(8,128)(2,1)S(1)}, u32[]{:S(2)}, u32[]{:S(2)}) collective-permute-start(bf16[2,4,256,1,64]{2,4,1,3,0:T(8,128)(2,1)S(1)} %pad_maximum_fusion.12), channel_id=1, source_target_pairs={{0,2},{2,4},{4,6},{1,3},{3,5},{5,7},{8,10},{10,12},{12,14},{9,11},... | collective-permute-start | bytes 786440 | tf_op jit(solution)/shard_map/ppermute | solution.py:388
  301.5 36.7 %copy-start.70 = (bf16[4,256,3,32]{1,3,2,0:T(8,128)(2,1)}, bf16[4,256,3,32]{1,3,2,0:T(8,128)(2,1)S(1)}, u32[]{:S(2)}) copy-start(bf16[4,256,3,32]{1,3,2,0:T(8,128)(2,1)S(1)} %get-tuple-element.213) | copy-start | bytes 589828
  301.5 36.7 %copy-start.72 = (bf16[4,256,3,32]{1,3,2,0:T(8,128)(2,1)}, bf16[4,256,3,32]{1,3,2,0:T(8,128)(2,1)S(1)}, u32[]{:S(2)}) copy-start(bf16[4,256,3,32]{1,3,2,0:T(8,128)(2,1)S(1)} %get-tuple-element.214) | copy-start | bytes 589828
  449.2 225.9 %reduce-scatter.13.cloned.1.call-start = ((), (), s32[]{:S(2)}) async-start(), calls=%async_computation.10 | async-start | bytes 3440640 | tf_op jit(solution)/shard_map/reduce_scatter | solution.py:419
  464.5 210.6 %reduce-scatter.11.cloned.1.call-start = ((), (), s32[]{:S(2)}) async-start(), calls=%async_computation.9 | async-start | bytes 3440640 | tf_op jit(solution)/shard_map/reduce_scatter | solution.py:419
  535.3 250.2 %reduce-scatter.15.cloned.1.call-start = ((), (), s32[]{:S(2)}) async-start(), calls=%async_computation.11 | async-start | bytes 1966080 | tf_op jit(solution)/shard_map/reduce_scatter | solution.py:419
  610.9 19.0 %collective-permute-start.10 = (bf16[2,4,256,1,64]{2,4,1,3,0:T(8,128)(2,1)}, bf16[2,4,256,1,64]{2,4,1,3,0:T(8,128)(2,1)}, u32[]{:S(2)}, u32[]{:S(2)}) collective-permute-start(bf16[2,4,256,1,64]{2,4,1,3,0:T(8,128)(2,1)} %get-tuple-element.211), channel_id=1, source_target_pairs={{6,0},{7,1},{14,8},{15,9},{22,16},{23,17},{30,24},{31,25}} | collective-permute-start | bytes 786440 | tf_op jit(solution)/shard_map/ppermute | solution.py:388
  612.2 21.6 %collective-permute-start.8 = (bf16[2,4,256,1,64]{2,4,1,0,3:T(8,128)(2,1)}, bf16[2,4,256,1,64]{2,4,1,0,3:T(8,128)(2,1)}, u32[]{:S(2)}, u32[]{:S(2)}) collective-permute-start(bf16[2,4,256,1,64]{2,4,1,0,3:T(8,128)(2,1)} %get-tuple-element.210), channel_id=1, source_target_pairs={{2,0},{4,2},{6,4},{3,1},{5,3},{7,5},{10,8},{12,10},{14,12},{11,9},... | collective-permute-start | bytes 786440 | tf_op jit(solution)/shard_map/ppermute | solution.py:388
  613.5 32.6 %collective-permute-start.9 = (bf16[2,4,256,1,64]{2,4,1,0,3:T(8,128)(2,1)}, bf16[2,4,256,1,64]{2,4,1,0,3:T(8,128)(2,1)}, u32[]{:S(2)}, u32[]{:S(2)}) collective-permute-start(bf16[2,4,256,1,64]{2,4,1,0,3:T(8,128)(2,1)} %get-tuple-element.212), channel_id=1, source_target_pairs={{4,0},{6,2},{5,1},{7,3},{12,8},{14,10},{13,9},{15,11},{20,16},{22,... | collective-permute-start | bytes 786440 | tf_op jit(solution)/shard_map/ppermute | solution.py:388
  653.6 258.8 %reduce-scatter.23.cloned.1.call-start = ((), (), s32[]{:S(2)}) async-start(), calls=%async_computation.15 | async-start | bytes 3440640 | tf_op jit(solution)/shard_map/reduce_scatter | solution.py:419
  699.5 216.1 %reduce-scatter.21.cloned.1.call-start = ((), (), s32[]{:S(2)}) async-start(), calls=%async_computation.14 | async-start | bytes 3440640 | tf_op jit(solution)/shard_map/reduce_scatter | solution.py:419
  702.3 11.7 %collective-permute-start.7 = (bf16[128,1536]{0,1:T(8,128)(2,1)}, bf16[128,1536]{0,1:T(8,128)(2,1)}, u32[]{:S(2)}, u32[]{:S(2)}) collective-permute-start(bf16[128,1536]{0,1:T(8,128)(2,1)} %bitcast.63), channel_id=1, source_target_pairs={{0,1},{1,0},{2,3},{3,2},{4,5},{5,4},{6,7},{7,6},{8,9},{9,8},{10,11... | collective-permute-start | bytes 1179656 | tf_op jit(solution)/shard_map/ppermute | solution.py:601
  718.3 5.4 collective-permute-start.34
  718.3 7.5 collective-permute-start.35
  719.3 9.4 collective-permute-start.36
  720.9 10.2 %collective-permute-start.31 = (bf16[96,896]{1,0:T(8,128)(2,1)}, bf16[96,896]{1,0:T(8,128)(2,1)S(1)}, u32[]{:S(2)}, u32[]{:S(2)}) collective-permute-start(bf16[96,896]{1,0:T(8,128)(2,1)} %get-tuple-element.240), channel_id=1, source_target_pairs={{0,8},{8,0},{16,24},{24,16},{1,9},{9,1},{17,25},{25,17},{2,10},{10... | collective-permute-start | bytes 516104 | tf_op jit(solution)/shard_map/ppermute | solution.py:262
  721.2 11.9 %collective-permute-start.32 = (bf16[96,896]{1,0:T(8,128)(2,1)S(1)}, bf16[96,896]{1,0:T(8,128)(2,1)S(1)}, u32[]{:S(2)}, u32[]{:S(2)}) collective-permute-start(bf16[96,896]{1,0:T(8,128)(2,1)S(1)} %get-tuple-element.238), channel_id=1, source_target_pairs={{0,16},{8,24},{16,0},{24,8},{1,17},{9,25},{17,1},{25,9},{2,18},{10... | collective-permute-start | bytes 516104 | tf_op jit(solution)/shard_map/ppermute | solution.py:262
  723.7 12.3 %collective-permute-start.33 = (bf16[96,896]{1,0:T(8,128)(2,1)S(1)}, bf16[96,896]{1,0:T(8,128)(2,1)S(1)}, u32[]{:S(2)}, u32[]{:S(2)}) collective-permute-start(bf16[96,896]{1,0:T(8,128)(2,1)S(1)} %get-tuple-element.239), channel_id=1, source_target_pairs={{0,24},{8,16},{16,8},{24,0},{1,25},{9,17},{17,9},{25,1},{2,26},{10... | collective-permute-start | bytes 516104 | tf_op jit(solution)/shard_map/ppermute | solution.py:262
  725.8 25.1 %collective-permute-start.28 = (bf16[96,896]{1,0:T(8,128)(2,1)}, bf16[96,896]{1,0:T(8,128)(2,1)}, u32[]{:S(2)}, u32[]{:S(2)}) collective-permute-start(bf16[96,896]{1,0:T(8,128)(2,1)} %get-tuple-element.243), channel_id=1, source_target_pairs={{0,8},{8,0},{16,24},{24,16},{1,9},{9,1},{17,25},{25,17},{2,10},{10... | collective-permute-start | bytes 516104 | tf_op jit(solution)/shard_map/ppermute | solution.py:262
  728.7 22.1 %collective-permute-start.29 = (bf16[96,896]{1,0:T(8,128)(2,1)S(1)}, bf16[96,896]{1,0:T(8,128)(2,1)}, u32[]{:S(2)}, u32[]{:S(2)}) collective-permute-start(bf16[96,896]{1,0:T(8,128)(2,1)S(1)} %get-tuple-element.241), channel_id=1, source_target_pairs={{0,16},{8,24},{16,0},{24,8},{1,17},{9,25},{17,1},{25,9},{2,18},{10... | collective-permute-start | bytes 516104 | tf_op jit(solution)/shard_map/ppermute | solution.py:262
  731.1 19.8 %collective-permute-start.30 = (bf16[96,896]{1,0:T(8,128)(2,1)S(1)}, bf16[96,896]{1,0:T(8,128)(2,1)}, u32[]{:S(2)}, u32[]{:S(2)}) collective-permute-start(bf16[96,896]{1,0:T(8,128)(2,1)S(1)} %get-tuple-element.242), channel_id=1, source_target_pairs={{0,24},{8,16},{16,8},{24,0},{1,25},{9,17},{17,9},{25,1},{2,26},{10... | collective-permute-start | bytes 516104 | tf_op jit(solution)/shard_map/ppermute | solution.py:262
  750.8 167.6 %reduce-scatter.19.cloned.1.call-start = ((), (), s32[]{:S(2)}) async-start(), calls=%async_computation.13 | async-start | bytes 3440640 | tf_op jit(solution)/shard_map/reduce_scatter | solution.py:419
  785.5 167.6 %reduce-scatter.17.cloned.1.call-start = ((), (), s32[]{:S(2)}) async-start(), calls=%async_computation.12 | async-start | bytes 2949120 | tf_op jit(solution)/shard_map/reduce_scatter | solution.py:419
  787.7 117.8 %collective-permute-start.25 = (bf16[96,512]{1,0:T(8,128)(2,1)}, bf16[96,512]{1,0:T(8,128)(2,1)}, u32[]{:S(2)}, u32[]{:S(2)}) collective-permute-start(bf16[96,512]{1,0:T(8,128)(2,1)} %get-tuple-element.265), channel_id=1, source_target_pairs={{0,8},{8,0},{16,24},{24,16},{1,9},{9,1},{17,25},{25,17},{2,10},{10... | collective-permute-start | bytes 294920 | tf_op jit(solution)/shard_map/ppermute | solution.py:262
  788.8 116.7 %collective-permute-start.26 = (bf16[96,512]{1,0:T(8,128)(2,1)}, bf16[96,512]{1,0:T(8,128)(2,1)}, u32[]{:S(2)}, u32[]{:S(2)}) collective-permute-start(bf16[96,512]{1,0:T(8,128)(2,1)} %get-tuple-element.263), channel_id=1, source_target_pairs={{0,16},{8,24},{16,0},{24,8},{1,17},{9,25},{17,1},{25,9},{2,18},{10... | collective-permute-start | bytes 294920 | tf_op jit(solution)/shard_map/ppermute | solution.py:262
  789.8 115.7 %collective-permute-start.27 = (bf16[96,512]{1,0:T(8,128)(2,1)}, bf16[96,512]{1,0:T(8,128)(2,1)}, u32[]{:S(2)}, u32[]{:S(2)}) collective-permute-start(bf16[96,512]{1,0:T(8,128)(2,1)} %get-tuple-element.264), channel_id=1, source_target_pairs={{0,24},{8,16},{16,8},{24,0},{1,25},{9,17},{17,9},{25,1},{2,26},{10... | collective-permute-start | bytes 294920 | tf_op jit(solution)/shard_map/ppermute | solution.py:262
  820.7 31.6 %collective-permute-start.11 = (f32[4,2,192]{1,2,0:T(8,128)}, f32[4,2,192]{1,2,0:T(8,128)}, u32[]{:S(2)}, u32[]{:S(2)}) collective-permute-start(f32[4,2,192]{1,2,0:T(8,128)} %pad_add_fusion.1), channel_id=1, source_target_pairs={{2,0},{4,2},{6,4},{3,1},{5,3},{7,5},{10,8},{12,10},{14,12},{11,9},... | collective-permute-start | bytes 18440 | tf_op jit(solution)/shard_map/ppermute | solution.py:388
  897.6 13.6 %collective-permute-start.12 = (bf16[128,1536]{0,1:T(8,128)(2,1)S(1)}, bf16[128,1536]{0,1:T(8,128)(2,1)S(1)}, u32[]{:S(2)}, u32[]{:S(2)}) collective-permute-start(bf16[128,1536]{0,1:T(8,128)(2,1)S(1)} %bitcast.786), channel_id=1, source_target_pairs={{0,1},{1,0},{2,3},{3,2},{4,5},{5,4},{6,7},{7,6},{8,9},{9,8},{10,11... | collective-permute-start | bytes 1179656 | tf_op jit(solution)/shard_map/ppermute | solution.py:601
  913.6 6.0 collective-permute-start.22
  914.2 7.2 collective-permute-start.23
  915.1 8.4 collective-permute-start.24
  916.7 8.9 collective-permute-start.19
  917.5 11.3 %collective-permute-start.20 = (bf16[96,896]{1,0:T(8,128)(2,1)S(1)}, bf16[96,896]{1,0:T(8,128)(2,1)S(1)}, u32[]{:S(2)}, u32[]{:S(2)}) collective-permute-start(bf16[96,896]{1,0:T(8,128)(2,1)S(1)} %get-tuple-element.251), channel_id=1, source_target_pairs={{0,16},{8,24},{16,0},{24,8},{1,17},{9,25},{17,1},{25,9},{2,18},{10... | collective-permute-start | bytes 516104 | tf_op jit(solution)/shard_map/ppermute | solution.py:262
  919.6 11.3 %collective-permute-start.21 = (bf16[96,896]{1,0:T(8,128)(2,1)S(1)}, bf16[96,896]{1,0:T(8,128)(2,1)S(1)}, u32[]{:S(2)}, u32[]{:S(2)}) collective-permute-start(bf16[96,896]{1,0:T(8,128)(2,1)S(1)} %get-tuple-element.252), channel_id=1, source_target_pairs={{0,24},{8,16},{16,8},{24,0},{1,25},{9,17},{17,9},{25,1},{2,26},{10... | collective-permute-start | bytes 516104 | tf_op jit(solution)/shard_map/ppermute | solution.py:262
  921.4 10.9 %collective-permute-start.16 = (bf16[96,896]{1,0:T(8,128)(2,1)S(1)}, bf16[96,896]{1,0:T(8,128)(2,1)S(1)}, u32[]{:S(2)}, u32[]{:S(2)}) collective-permute-start(bf16[96,896]{1,0:T(8,128)(2,1)S(1)} %get-tuple-element.256), channel_id=1, source_target_pairs={{0,8},{8,0},{16,24},{24,16},{1,9},{9,1},{17,25},{25,17},{2,10},{10... | collective-permute-start | bytes 516104 | tf_op jit(solution)/shard_map/ppermute | solution.py:262
  923.5 12.6 %collective-permute-start.17 = (bf16[96,896]{1,0:T(8,128)(2,1)S(1)}, bf16[96,896]{1,0:T(8,128)(2,1)S(1)}, u32[]{:S(2)}, u32[]{:S(2)}) collective-permute-start(bf16[96,896]{1,0:T(8,128)(2,1)S(1)} %get-tuple-element.254), channel_id=1, source_target_pairs={{0,16},{8,24},{16,0},{24,8},{1,17},{9,25},{17,1},{25,9},{2,18},{10... | collective-permute-start | bytes 516104 | tf_op jit(solution)/shard_map/ppermute | solution.py:262
  925.7 12.4 %collective-permute-start.18 = (bf16[96,896]{1,0:T(8,128)(2,1)S(1)}, bf16[96,896]{1,0:T(8,128)(2,1)S(1)}, u32[]{:S(2)}, u32[]{:S(2)}) collective-permute-start(bf16[96,896]{1,0:T(8,128)(2,1)S(1)} %get-tuple-element.255), channel_id=1, source_target_pairs={{0,24},{8,16},{16,8},{24,0},{1,25},{9,17},{17,9},{25,1},{2,26},{10... | collective-permute-start | bytes 516104 | tf_op jit(solution)/shard_map/ppermute | solution.py:262
  954.4 3.1 collective-permute-start.13
  954.5 6.7 collective-permute-start.14
  956.1 7.4 collective-permute-start.15
  (149 other events, 1457.2 us)
Sparse Core Ops, SparseCore 0:
  23.4 58.1 all-gather.8
  83.2 146.2 all-gather.10
  231.0 39.2 all-gather.12
  271.8 158.9 all-gather.14
  449.3 61.9 reduce-scatter.8
  513.4 53.9 reduce-scatter.12
  569.7 53.9 reduce-scatter.10
  653.7 32.6 reduce-scatter.14
  699.6 51.4 reduce-scatter.22
  753.2 53.9 reduce-scatter.20
  809.5 62.2 reduce-scatter.18
  905.0 48.0 reduce-scatter.16

commit v2 on v1

--- a/solution.py
+++ b/solution.py
@@ -236,6 +236,55 @@
     local.wait()
 
 
+def turn_kernel(x_ref, o_ref, own_sem, send, recv):
+    dp = lax.axis_index("dp")
+    ten = lax.axis_index("tensor")
+    barrier = pltpu.get_barrier_semaphore()
+    for step in (1, 2, 3):
+        pl.semaphore_signal(
+            barrier,
+            1,
+            device_id={"dp": lax.rem(dp + step, 4), "tensor": ten},
+            device_id_type=MESH,
+        )
+    pl.semaphore_wait(barrier, 3)
+    copies = []
+    for step in (2, 1, 3):
+        there = lax.rem(dp + step, 4)
+        copy = remote(
+            x_ref.at[there],
+            o_ref.at[:, dp],
+            send.at[step],
+            recv.at[step],
+            {"dp": there, "tensor": ten},
+        )
+        copy.start()
+        copies.append(copy)
+    local = pltpu.make_async_copy(x_ref.at[dp], o_ref.at[:, dp], own_sem)
+    local.start()
+    for copy in copies:
+        copy.wait()
+    local.wait()
+
+
+def turn_blocks(blocks, number):
+    shape = (blocks.shape[1], blocks.shape[0]) + blocks.shape[2:]
+    return pl.pallas_call(
+        turn_kernel,
+        out_shape=jax.ShapeDtypeStruct(shape, blocks.dtype),
+        in_specs=[pl.BlockSpec(memory_space=pltpu.VMEM)],
+        out_specs=pl.BlockSpec(memory_space=pl.ANY),
+        scratch_shapes=[
+            pltpu.SemaphoreType.DMA,
+            pltpu.SemaphoreType.DMA((4,)),
+            pltpu.SemaphoreType.DMA((4,)),
+        ],
+        compiler_params=pltpu.CompilerParams(
+            collective_id=number, has_side_effects=True, vmem_limit_bytes=16 << 20
+        ),
+    )(blocks)
+
+
 def swap_blocks(blocks, number):
     return pl.pallas_call(
         swap_kernel,
@@ -253,15 +302,20 @@
     )(blocks)
 
 
-def return_blocks(blocks):
+def send_back(blocks):
     dp = lax.axis_index("dp")
     devices = range(lax.axis_size("dp"))
     parts = [lax.dynamic_index_in_dim(blocks, dp, 0, keepdims=False)]
     for flip in (1, 2, 3):
         sent = lax.dynamic_index_in_dim(blocks, dp ^ flip, 0, keepdims=False)
         parts.append(lax.ppermute(sent, "dp", [(i, i ^ flip) for i in devices]))
-    ordered = [lax.select_n(dp, *(parts[j ^ i] for i in devices)) for j in devices]
-    return jnp.stack(ordered, 1)
+    return parts
+
+
+def by_source(parts):
+    dp = lax.axis_index("dp")
+    devices = range(lax.axis_size("dp"))
+    return jnp.stack([wide(lax.select_n(dp, *(parts[j ^ i] for i in devices))) for j in devices], 1)
 
 
 def from_all_dp(block):
@@ -273,8 +327,8 @@
     return jnp.concatenate([lax.select_n(dp, *(parts[j ^ i] for i in devices)) for j in devices], 0)
 
 
-def after(values, *others):
-    return lax.optimization_barrier((values,) + others)[0]
+def together(*values):
+    return lax.optimization_barrier(values)
 
 
 def small_sum_kernel(x_ref, o_ref, plane_box, plane_sum, line_box, send, recv, line_send, line_recv):
@@ -325,6 +379,63 @@
         copy.wait_send()
 
 
+def small_gather_kernel(x_ref, o_ref, own_sem, send, recv, line_send, line_recv):
+    dp, ten, ctx = (lax.axis_index(name) for name in ("dp", "tensor", "ctx"))
+    dps, ctxs = (lax.axis_size(name) for name in ("dp", "ctx"))
+    barrier = pltpu.get_barrier_semaphore()
+
+    def dp_peer(step):
+        return {"dp": lax.rem(dp + step, dps), "tensor": ten, "ctx": ctx}
+
+    def ctx_peer(step):
+        return {"dp": dp, "tensor": ten, "ctx": lax.rem(ctx + step, ctxs)}
+
+    for step in range(1, dps):
+        pl.semaphore_signal(barrier, 1, device_id=dp_peer(step), device_id_type=MESH)
+    for step in range(1, ctxs):
+        pl.semaphore_signal(barrier, 1, device_id=ctx_peer(step), device_id_type=MESH)
+    pl.semaphore_wait(barrier, dps + ctxs - 2)
+    copies = []
+    for step in range(1, dps):
+        copy = remote(x_ref, o_ref.at[ctx, dp], send.at[step], recv.at[step], dp_peer(step))
+        copy.start()
+        copies.append(copy)
+    local = pltpu.make_async_copy(x_ref, o_ref.at[ctx, dp], own_sem)
+    local.start()
+    local.wait()
+    for copy in copies:
+        copy.wait()
+    lines = []
+    for step in range(1, ctxs):
+        copy = remote(
+            o_ref.at[ctx], o_ref.at[ctx], line_send.at[step], line_recv.at[step], ctx_peer(step)
+        )
+        copy.start()
+        lines.append(copy)
+    for copy in lines:
+        copy.wait()
+
+
+def small_gather(block, number):
+    dps, ctxs = lax.axis_size("dp"), lax.axis_size("ctx")
+    return pl.pallas_call(
+        small_gather_kernel,
+        out_shape=jax.ShapeDtypeStruct((ctxs, dps) + block.shape, block.dtype),
+        in_specs=[pl.BlockSpec(memory_space=pltpu.VMEM)],
+        out_specs=pl.BlockSpec(memory_space=pltpu.VMEM),
+        scratch_shapes=[
+            pltpu.SemaphoreType.DMA,
+            pltpu.SemaphoreType.DMA((dps,)),
+            pltpu.SemaphoreType.DMA((dps,)),
+            pltpu.SemaphoreType.DMA((ctxs,)),
+            pltpu.SemaphoreType.DMA((ctxs,)),
+        ],
+        compiler_params=pltpu.CompilerParams(
+            collective_id=number, has_side_effects=True, vmem_limit_bytes=16 << 20
+        ),
+    )(block)
+
+
 def small_sum(values, number):
     count = values.size
     rows = -(-count // (8 * LANES)) * 8
@@ -401,6 +512,95 @@
     return jnp.concatenate([first * cosine - second * sine, second * cosine + first * sine], -1)
 
 
+def visible(pos_ref, rows, key_rows):
+    query_at = lax.broadcasted_iota(jnp.int32, (rows, key_rows), 0) + (key_rows - rows)
+    key_at = lax.broadcasted_iota(jnp.int32, (rows, key_rows), 1)
+    return (key_at <= query_at) & (key_at >= query_at - pos_ref[0])
+
+
+def attend_kernel(q_ref, kv_ref, pos_ref, context_ref, lse_ref):
+    rows = q_ref.shape[1]
+    key_rows = kv_ref.shape[0] * rows
+    both = kv_ref[...].reshape(key_rows, 2 * HD)
+    keys, values = both[:, :HD], both[:, HD:]
+    allowed = visible(pos_ref, rows, key_rows)
+    contexts, totals = [], []
+    for head in range(GROUPS):
+        query = q_ref[0, :, head * HD : (head + 1) * HD]
+        scores = jnp.where(allowed, dot_nt(query, keys) * (1.0 / math.sqrt(HD)), -1e30)
+        top = jnp.max(scores, -1, keepdims=True)
+        weights = jnp.exp(scores - top)
+        total = jnp.sum(weights, -1, keepdims=True)
+        contexts.append(low(dot_nn(low(weights * (1.0 / total)), values)))
+        totals.append(top + jnp.log(total))
+    context_ref[0] = jnp.concatenate(contexts, -1)
+    lse_ref[0] = jnp.concatenate(totals + [jnp.zeros_like(totals[0])] * (8 - GROUPS), -1)
+
+
+def attend_back_kernel(q_ref, kv_ref, pos_ref, lse_ref, grad_ref, dq_ref, dkv_ref):
+    rows = q_ref.shape[1]
+    key_rows = kv_ref.shape[0] * rows
+    both = kv_ref[...].reshape(key_rows, 2 * HD)
+    keys, values = both[:, :HD], both[:, HD:]
+    allowed = visible(pos_ref, rows, key_rows)
+    root = 1.0 / math.sqrt(HD)
+    query_grads = []
+    key_grad = jnp.zeros((key_rows, HD), jnp.float32)
+    value_grad = jnp.zeros((key_rows, HD), jnp.float32)
+    for head in range(GROUPS):
+        query = q_ref[0, :, head * HD : (head + 1) * HD]
+        grad = grad_ref[0, :, head * HD : (head + 1) * HD]
+        scores = dot_nt(query, keys) * root - lse_ref[0, :, head : head + 1]
+        probs = jnp.where(allowed, jnp.exp(jnp.where(allowed, scores, 0.0)), 0.0)
+        prob_grad = dot_nt(grad, values)
+        delta = jnp.sum(probs * prob_grad, -1, keepdims=True)
+        score_grad = low(probs * (prob_grad - delta))
+        query_grads.append(dot_nn(score_grad, keys) * root)
+        key_grad = key_grad + dot_tn(score_grad, query)
+        value_grad = value_grad + dot_tn(low(probs), grad)
+    dq_ref[0] = jnp.concatenate(query_grads, -1)
+    whole = low(jnp.concatenate([key_grad * root, value_grad], -1))
+    dkv_ref[...] = whole.reshape(dkv_ref.shape)
+
+
+def attend_specs(seqs, rows, parts):
+    by_seq = lambda width: pl.BlockSpec((1, rows, width), lambda s: (s, 0, 0))
+    over_keys = pl.BlockSpec((parts, 1, rows, 2 * HD), lambda s: (0, s, 0, 0))
+    return by_seq, over_keys
+
+
+def attend(queries, kv_all, positions):
+    seqs, rows, width = queries.shape
+    by_seq, over_keys = attend_specs(seqs, rows, kv_all.shape[0])
+    return pl.pallas_call(
+        attend_kernel,
+        grid=(seqs,),
+        out_shape=(
+            jax.ShapeDtypeStruct(queries.shape, jnp.bfloat16),
+            jax.ShapeDtypeStruct((seqs, rows, 8), jnp.float32),
+        ),
+        in_specs=[by_seq(width), over_keys, by_seq(1)],
+        out_specs=(by_seq(width), by_seq(8)),
+        compiler_params=pltpu.CompilerParams(vmem_limit_bytes=56 << 20),
+    )(queries, kv_all, positions[..., None])
+
+
+def attend_back(queries, kv_all, positions, totals, grads):
+    seqs, rows, width = queries.shape
+    by_seq, over_keys = attend_specs(seqs, rows, kv_all.shape[0])
+    return pl.pallas_call(
+        attend_back_kernel,
+        grid=(seqs,),
+        out_shape=(
+            jax.ShapeDtypeStruct(queries.shape, jnp.float32),
+            jax.ShapeDtypeStruct(kv_all.shape, jnp.bfloat16),
+        ),
+        in_specs=[by_seq(width), over_keys, by_seq(1), by_seq(8), by_seq(width)],
+        out_specs=(by_seq(width), over_keys),
+        compiler_params=pltpu.CompilerParams(vmem_limit_bytes=56 << 20),
+    )(queries, kv_all, positions[..., None], totals, grads)
+
+
 def column_blocks(weight, count, width):
     rows, columns = weight.shape
     weight = jnp.pad(weight, ((0, 0), (0, count * width - columns)))
@@ -420,32 +620,30 @@
     return summed.reshape(count, -1, summed.shape[-1])
 
 
-def finish_grads(summed):
-    return wide(return_blocks(summed))
-
-
-def feed_forward(normed, weights, width):
+def feed_hidden(normed, weights, width):
     both = dot_nn(normed, weights[:, : 2 * width])
     gate, lift = both[:, :width], both[:, width:]
-    hidden = low(jax.nn.silu(gate) * lift)
-    partial = dot_nt(hidden, weights[:, 2 * width :])
-    return partial, (gate, lift, hidden)
+    return gate, lift, low(jax.nn.silu(gate) * lift)
+
+
+def feed_down(hidden, weights, width):
+    return low(dot_nt(hidden, weights[:, 2 * width :]))
 
 
 def feed_backward(grad_all, normed, weights, width, saved):
     gate, lift, hidden = saved
-    down_grad = low(dot_tn(grad_all, hidden))
-    hidden_grad = dot_nn(grad_all, after(weights[:, 2 * width :], down_grad))
+    down_grad, grad_all = together(low(dot_tn(grad_all, hidden)), grad_all)
+    hidden_grad = dot_nn(grad_all, weights[:, 2 * width :])
     sig = jax.nn.sigmoid(gate)
     gate_grad = low(hidden_grad * lift * sig * (1.0 + gate * (1.0 - sig)))
     lift_grad = low(hidden_grad * gate * sig)
     gate_weight_grad = low(dot_tn(normed, gate_grad))
     lift_weight_grad = low(dot_tn(normed, lift_grad))
-    gate_low, lift_low = lax.optimization_barrier(
-        (gate_grad, lift_grad, gate_weight_grad, lift_weight_grad)
-    )[:2]
-    partial = dot_nt(gate_low, weights[:, :width]) + dot_nt(
-        lift_low, weights[:, width : 2 * width]
+    gate_grad, lift_grad, gate_weight_grad, lift_weight_grad = together(
+        gate_grad, lift_grad, gate_weight_grad, lift_weight_grad
+    )
+    partial = dot_nt(gate_grad, weights[:, :width]) + dot_nt(
+        lift_grad, weights[:, width : 2 * width]
     )
     return partial, (gate_weight_grad, lift_weight_grad, down_grad)
 
@@ -491,16 +689,26 @@
         lead = values.shape[:-1]
         return values.reshape(lead + (ctxs, seqs, part)).swapaxes(-3, -2).reshape(lead + (width,))
 
+    def own_half(values):
+        return regroup(lax.dynamic_slice_in_dim(values[0], ten * own_rows, own_rows, 0))
+
+    stream_zero = wide(own_half(hidden_in))
+    upstream = wide(own_half(output_grad))
+    last_grad_all = plane_gather(low(upstream))
+
+    def norm_rows(stream, gain):
+        return low(stream * rms_scale(stream) * gain)
+
     mixer_blocks = jnp.concatenate(
         [column_blocks(mixer_in[k], seqs, channels) for k in range(3)]
         + [column_blocks(mixer_out.T, seqs, channels)],
         -1,
     )
-    own_gains = jnp.stack([mixer_gain, feed_first, attend_gain, feed_second], 1)
-    own_gains = jnp.pad(own_gains, ((0, 0), (0, LANES - 4)))
-    own_gains = jnp.broadcast_to(own_gains, (seqs, part, LANES))
-    mixer_w = spread_weights(jnp.concatenate([mixer_blocks, own_gains], -1), 3)
-    gains = wide(mixer_w[:, 4 * channels : 4 * channels + 4]).T
+    mixer_w = spread_weights(mixer_blocks, 3)
+    own_gains = wide(jnp.stack([mixer_gain, feed_first, attend_gain, feed_second]))
+    own_gains = jnp.pad(own_gains, ((0, 4), (0, -part % LANES)))
+    gains = small_gather(own_gains, 8)[:, :, :4, :part]
+    gains = gains.transpose(2, 0, 1, 3).reshape(4, width)
     first_blocks = jnp.concatenate(
         [column_blocks(w, seqs, feed_width) for w in (gate_first, lift_first, down_first.T)], -1
     )
@@ -522,18 +730,10 @@
     second_w = spread_weights(second_blocks, 4)
 
     positions = from_all_dp(doc_pos)
+    mixer_norm = plane_gather(norm_rows(stream_zero, gains[0]))
+    mixer_w, mixer_norm, last_grad_all = together(mixer_w, mixer_norm, last_grad_all)
     own_taps = wide(lax.dynamic_slice_in_dim(conv_taps, dp * channels, channels, 1))
 
-    def own_half(values):
-        return regroup(lax.dynamic_slice_in_dim(values[0], ten * own_rows, own_rows, 0))
-
-    stream_zero = wide(own_half(hidden_in))
-    upstream = wide(own_half(output_grad))
-
-    def norm_rows(stream, gain):
-        return low(stream * rms_scale(stream) * gain)
-
-    mixer_norm = plane_gather(norm_rows(stream_zero, gains[0]))
     mixer_in_w, mixer_out_w = mixer_w[:, : 3 * channels], mixer_w[:, 3 * channels : 4 * channels]
     projected = dot_nn(mixer_norm, mixer_in_w).reshape(seqs, rows, 3 * channels)
     gate_b = projected[..., :channels]
@@ -550,8 +750,8 @@
     stream_one = stream_zero + plane_scatter(dot_nt(conv_gated, mixer_out_w))
 
     first_norm = plane_gather(norm_rows(stream_one, gains[1]))
-    partial, first_saved = feed_forward(first_norm, first_w, feed_width)
-    stream_two = stream_one + plane_scatter(partial)
+    first_saved = feed_hidden(first_norm, first_w, feed_width)
+    stream_two = stream_one + plane_scatter(feed_down(first_saved[2], first_w, feed_width))
 
     attend_norm = plane_gather(norm_rows(stream_two, gains[2]))
     qkv_w = attend_w[:, : q_cols + 2 * kv_cols]
@@ -565,36 +765,17 @@
     q_gain, k_gain = wide(query_gain), wide(key_gain)
     query_rot = low(rotate(queries * query_scale * q_gain, cosine, sine))
     key_rot = low(rotate(keys * key_scale * k_gain, cosine, sine))
-    kv_own = jnp.stack([key_rot, low(values)])
-    kv_all = jnp.concatenate(
-        [shifted(kv_own, "ctx", distance) for distance in range(ctxs - 1, 0, -1)] + [kv_own], 2
-    )
-    key_all, value_all = kv_all[0], kv_all[1]
-    key_rows = key_all.shape[1]
-    heads = kv_cols // HD
-    query_g = query_rot.reshape(seqs, rows, heads, GROUPS, HD)
-    query_at = jnp.arange(rows, dtype=jnp.int32) + (key_rows - rows)
-    query_from = query_at[None] - positions
-    key_at = jnp.arange(key_rows, dtype=jnp.int32)
-    allowed = (key_at <= query_at[None, :, None]) & (key_at >= query_from[..., None])
-    allowed = allowed[:, None, None]
-    root = 1.0 / math.sqrt(HD)
-    scores = (
-        jnp.einsum("sthgd,suhd->shgtu", query_g, key_all, preferred_element_type=jnp.float32) * root
-    )
-    scores = jnp.where(allowed, scores, -1e30)
-    top = jnp.max(scores, -1, keepdims=True)
-    weights = jnp.exp(scores - top)
-    probs = weights / jnp.sum(weights, -1, keepdims=True)
-    probs_low = low(probs)
-    context = low(
-        jnp.einsum("shgtu,suhd->sthgd", probs_low, value_all, preferred_element_type=jnp.float32)
-    ).reshape(seqs * rows, q_cols)
+    kv_own = jnp.concatenate([key_rot, low(values)], -1).reshape(seqs, rows, 2 * HD)
+    kv_all = jnp.stack(
+        [shifted(kv_own, "ctx", distance) for distance in range(ctxs - 1, 0, -1)] + [kv_own]
+    )
+    query_rows = query_rot.reshape(seqs, rows, q_cols)
+    context, totals = attend(query_rows, kv_all, positions)
+    context = context.reshape(seqs * rows, q_cols)
     stream_three = stream_two + plane_scatter(dot_nt(context, attend_out_w))
 
     second_norm = plane_gather(norm_rows(stream_three, gains[3]))
-    partial, second_saved = feed_forward(second_norm, second_w, feed_width)
-    stream_four = stream_three + plane_scatter(partial)
+    second_saved = feed_hidden(second_norm, second_w, feed_width)
 
     def both_halves(values):
         values = low(restore(values))
@@ -603,72 +784,56 @@
         upper = lax.select_n(ten, other, values)
         return jnp.concatenate([lower, upper], 0)[None]
 
-    hidden_out = both_halves(stream_four)
-
     def norm_step(upstream, stream, gain, normed_grad):
         gain_grad = jnp.sum(normed_grad * stream * rms_scale(stream), 0)
         return upstream + rms_back(stream, normed_grad * gain), gain_grad
 
-    grad_all = plane_gather(low(upstream))
-    partial, second_grads = feed_backward(grad_all, second_norm, second_w, feed_width, second_saved)
+    partial, second_grads = feed_backward(last_grad_all, second_norm, second_w, feed_width, second_saved)
     second_sums = [collect_grads(g) for g in second_grads]
     grad_three, second_gain_grad = norm_step(
         upstream, stream_three, gains[3], plane_scatter(partial)
     )
-    grad_three = after(grad_three, second_sums[2])
+    grad_three, second_sums[2] = together(grad_three, second_sums[2])
 
     grad_all = plane_gather(low(grad_three))
     attend_out_grad = dot_tn(grad_all, context)
-    context_grad = low(dot_nn(grad_all, attend_out_w)).reshape(seqs, rows, heads, GROUPS, HD)
-    prob_grad = jnp.einsum(
-        "sthgd,suhd->shgtu", context_grad, value_all, preferred_element_type=jnp.float32
-    )
-    delta = jnp.sum(probs * prob_grad, -1, keepdims=True)
-    score_grad = low(probs * (prob_grad - delta))
-    query_acc = (
-        jnp.einsum("shgtu,suhd->sthgd", score_grad, key_all, preferred_element_type=jnp.float32)
-        * root
-    ).reshape(seqs, rows, -1, HD)
-    key_acc = (
-        jnp.einsum("shgtu,sthgd->suhd", score_grad, query_g, preferred_element_type=jnp.float32)
-        * root
-    )
-    value_acc = jnp.einsum(
-        "shgtu,sthgd->suhd", probs_low, context_grad, preferred_element_type=jnp.float32
-    )
-    kv_acc = low(jnp.stack([key_acc, value_acc])).reshape(2, seqs, ctxs, rows, heads, HD)
-    kv_mine = wide(kv_acc[:, :, ctxs - 1])
-    for distance in range(1, ctxs):
-        kv_mine = kv_mine + wide(shifted(kv_acc[:, :, ctxs - 1 - distance], "ctx", -distance))
+    context_grad = low(dot_nn(grad_all, attend_out_w)).reshape(seqs, rows, q_cols)
+    query_acc, kv_acc = attend_back(query_rows, kv_all, positions, totals, context_grad)
+    query_acc = query_acc.reshape(seqs, rows, -1, HD)
+    late_hidden, kv_acc = together(second_saved[2], kv_acc)
+    kv_sent = [
+        shifted(kv_acc[ctxs - 1 - distance], "ctx", -distance) for distance in range(1, ctxs)
+    ]
+    last_branch = plane_scatter(feed_down(late_hidden, second_w, feed_width))
+    last_branch, *kv_sent = together(last_branch, *kv_sent)
+    kv_mine = wide(kv_acc[ctxs - 1]) + sum(wide(sent) for sent in kv_sent)
+    key_grads, value_grads = kv_mine[..., :HD], kv_mine[..., HD:]
     query_norm_grad = rotate(query_acc, cosine, -sine)
-    key_norm_grad = rotate(kv_mine[0], cosine, -sine)
+    key_norm_grad = rotate(key_grads[:, :, None], cosine, -sine)
     query_gain_part = jnp.sum(query_norm_grad * queries * query_scale, (0, 1, 2))
     key_gain_part = jnp.sum(key_norm_grad * keys * key_scale, (0, 1, 2))
     query_grad = low(rms_back(queries, query_norm_grad * q_gain)).reshape(seqs * rows, -1)
     key_grad = low(rms_back(keys, key_norm_grad * k_gain)).reshape(seqs * rows, -1)
-    value_grad = low(kv_mine[1]).reshape(seqs * rows, -1)
+    value_grad = low(value_grads).reshape(seqs * rows, -1)
     qkv_grad = jnp.concatenate([query_grad, key_grad, value_grad], -1)
     qkv_weight_grad = dot_tn(attend_norm, qkv_grad)
     attend_grads = low(jnp.concatenate([qkv_weight_grad, attend_out_grad], -1))
+    qkv_grad, attend_grads = together(qkv_grad, attend_grads)
     attend_sums = collect_grads(attend_grads)
     grad_two, attend_gain_grad = norm_step(
         grad_three,
         stream_two,
         gains[2],
-        plane_scatter(after(low(dot_nt(qkv_grad, qkv_w)), attend_grads)),
-    )
-    grad_two = after(grad_two, second_sums[0], second_sums[1])
+        plane_scatter(dot_nt(qkv_grad, qkv_w)),
+    )
+    grad_two, *second_sums[:2] = together(grad_two, *second_sums[:2])
 
     grad_all = plane_gather(low(grad_two))
     partial, first_grads = feed_backward(grad_all, first_norm, first_w, feed_width, first_saved)
     first_sums = [collect_grads(g) for g in first_grads]
     grad_one, first_gain_grad = norm_step(grad_two, stream_one, gains[1], plane_scatter(partial))
-    grad_one = after(grad_one, attend_sums)
-    second_done, first_done = (
-        [finish_grads(total).reshape(part, -1)[:, :units] for total in sums]
-        for sums in (second_sums, first_sums)
-    )
-    attend_done = finish_grads(attend_sums)
+    second_cat = jnp.concatenate(second_sums, -1)
+    grad_one, attend_sums, second_cat = together(grad_one, attend_sums, second_cat)
 
     grad_all = plane_gather(low(grad_one))
     mixer_out_grad = dot_tn(grad_all, conv_gated)
@@ -681,20 +846,28 @@
         masked = sum_grad * in_doc[j]
         tap_rows.append(jnp.sum(masked * extended[:, 2 - j : 2 - j + rows], (0, 1)))
         spread = spread + jnp.pad(own_taps[j] * masked, ((0, 0), (2 - j, j), (0, 0)))
+    spread, second_cat = together(spread, second_cat)
     returned = shifted(spread[:, :2], "ctx", -1)
+    second_done = by_source(send_back(second_cat))
+    returned, second_done = together(returned, second_done)
     src_grad = spread[:, 2:] + jnp.pad(returned, ((0, 0), (rows - 2, 0), (0, 0)))
     proj_grad = jnp.concatenate(
         [low(src_grad * conv_input), gate_c_grad, low(src_grad * gate_b)], -1
     ).reshape(seqs * rows, 3 * channels)
     mixer_in_grad = dot_tn(mixer_norm, proj_grad)
     mixer_grads = low(jnp.concatenate([mixer_in_grad, mixer_out_grad], -1))
-    mixer_done = finish_grads(collect_grads(mixer_grads))
+    mixer_grads = turn_blocks(
+        mixer_grads.reshape(ctxs, seqs, part, 4 * channels).swapaxes(0, 1), 7
+    ).reshape(ctxs, seqs * part, 4 * channels)
+    proj_grad, mixer_grads = together(proj_grad, mixer_grads)
+    mixer_sums = lax.psum_scatter(mixer_grads, "ctx", scatter_dimension=0, tiled=False)
     grad_zero, mixer_gain_grad = norm_step(
         grad_one,
         stream_zero,
         gains[0],
-        plane_scatter(after(low(dot_nt(proj_grad, mixer_in_w)), mixer_grads)),
-    )
+        plane_scatter(dot_nt(proj_grad, mixer_in_w)),
+    )
+    hidden_out = both_halves(stream_three + last_branch)
     hidden_grad = both_halves(grad_zero)
 
     gain_rows = restore(
@@ -708,6 +881,11 @@
     small = jnp.concatenate(
         [gain_rows.reshape(-1), query_gain_part, key_gain_part, taps_part.reshape(-1)]
     )
+    first_cat = jnp.concatenate(first_sums + [attend_sums], -1)
+    first_parts = send_back(first_cat)
+    small, mixer_sums, *first_parts = together(small, mixer_sums, *first_parts)
+    first_done = by_source(first_parts)
+    mixer_done = wide(mixer_sums).reshape(seqs, part, -1).swapaxes(0, 1)
     small = small_sum(small, 5)
     gain_sums = lax.dynamic_slice_in_dim(
         small[: 4 * width].reshape(4, width), (dp * ctxs + ctx) * part, part, 1
@@ -720,6 +898,11 @@
 
     def columns(done, start, count):
         return done[:, :, start : start + count].reshape(part, -1)
+
+    def feed_columns(done, number):
+        return columns(done, number * feed_width, feed_width)[:, :units]
+
+    attend_at = 3 * feed_width
 
     return (
         hidden_out,
@@ -729,20 +912,20 @@
         taps_grad,
         columns(mixer_done, 3 * channels, channels).T,
         gain_sums[1],
-        first_done[0],
-        first_done[1],
-        first_done[2].T,
+        feed_columns(first_done, 0),
+        feed_columns(first_done, 1),
+        feed_columns(first_done, 2).T,
         gain_sums[2],
-        columns(attend_done, 0, q_cols),
-        columns(attend_done, q_cols, kv_cols),
-        columns(attend_done, q_cols + kv_cols, kv_cols),
+        columns(first_done, attend_at, q_cols),
+        columns(first_done, attend_at + q_cols, kv_cols),
+        columns(first_done, attend_at + q_cols + kv_cols, kv_cols),
         query_gain_grad,
         key_gain_grad,
-        columns(attend_done, q_cols + 2 * kv_cols, q_cols).T,
+        columns(first_done, attend_at + q_cols + 2 * kv_cols, q_cols).T,
         gain_sums[3],
-        second_done[0],
-        second_done[1],
-        second_done[2].T,
+        feed_columns(second_done, 0),
+        feed_columns(second_done, 1),
+        feed_columns(second_done, 2).T,
     )
 
 

time: 986 us -> 957 us (0.971)
  Pallas kernels: 385 us -> 448 us
  waiting for transfers between devices: 194 us -> 164 us
  matrix products: 157 us -> 132 us
  other arithmetic: 74.3 us -> 61.3 us
  local copies, waits for them, and re-layouts: 106 us -> 95.6 us
    pallas_call x0 -> x4, Pallas kernels: none -> 65.9 us  [the longest x1 28.3 us: turn_blocks(): pl.pallas_call(turn_kernel, out_shape=jax.ShapeDtypeStruct(shape, blocks....]
    dot_general x6 -> x0, matrix products: 34.7 us -> none  [the longest x1 10.1 us: shards(): jnp.einsum('sthgd,suhd->shgtu', context_grad, value_all, preferred_elemen...]
    all_gather x4, waiting for transfers between devices: 71.9 us -> 45.5 us  [spread_weights(): whole = lax.all_gather(mine, 'ctx', axis=0, tiled=False)]
    ppermute x24 -> x6, starting transfers between devices: 17.9 us -> 3.72 us  [send_back(): parts.append(lax.ppermute(sent, 'dp', [(i, i ^ flip) for i in devices]))]
    ppermute x8, waiting for transfers between devices: 82.3 us -> 70.1 us  [shifted(): return lax.ppermute(block, axis, route)]
    ppermute x24 -> x6, waiting for transfers between devices: 26.2 us -> 33.7 us  [send_back(): parts.append(lax.ppermute(sent, 'dp', [(i, i ^ flip) for i in devices]))]
    unnamed x344 -> x312, local copies, waits for them, and re-layouts: 31.4 us -> 31.7 us
  transfers between devices with their start and end apart: 49 -> 31, of which waited for: 24 -> 13; matrix products, arithmetic and copies ran while one was open for 30% -> 24% of each run, Pallas kernels for 38% -> 45%
where the time goes in v2:
time: 957 us; the launch traced here: 948 us
  Pallas kernels  448 us (47%)
  waiting for transfers between devices  164 us (17%)
  matrix products  132 us (14%)
  local copies, waits for them, and re-layouts  95.6 us (10%)
  other arithmetic  61.3 us (6%)
  starting transfers between devices  30.9 us (3%)
  between operations  17.4 us (2%)
    pallas_call x8, Pallas kernels, plane_gather(): pl.pallas_call(gather_kernel, out_shape=jax.ShapeDtypeStruct((slots, rows...  157 us
    pallas_call x8, Pallas kernels, plane_scatter(): pl.pallas_call(scatter_kernel, out_shape=jax.ShapeDtypeStruct(block, jnp....  143 us
    ppermute x8, waiting for transfers between devices, shifted(): return lax.ppermute(block, axis, route)  70.1 us
    pallas_call x4, Pallas kernels, swap_blocks(): pl.pallas_call(swap_kernel, out_shape=jax.ShapeDtypeStruct(blocks.shape,...  67.9 us
    dot_general x8, matrix products, dot_nn(): lax.dot_general(left, right, (((1,), (0,)), ((), ())), preferred_element_...  46.6 us
    all_gather x4, waiting for transfers between devices, spread_weights(): whole = lax.all_gather(mine, 'ctx', axis=0, tiled=False)  45.5 us
    dot_general x10, matrix products, dot_nt(): lax.dot_general(left, right, (((1,), (1,)), ((), ())), preferred_element_...  43.4 us
    dot_general x10, matrix products, dot_tn(): lax.dot_general(left, right, (((0,), (0,)), ((), ())), preferred_element_...  41.5 us
  transfers between devices with their start and end apart: 31, of which 13 were waited for; matrix products, arithmetic and copies ran while one was open for 24% of the time, Pallas kernels for 45%

profile of v2, /device:TPU:0, one launch (start us, length us, event | category | flops | bytes accessed | tf_op | source)
XLA Modules:
  0.0 947.9 jit_solution(6656831245194310149)
XLA Ops:
  10.4 10.6 %shard_map.373 = bf16[4,96,768]{2,1,0:T(8,128)(2,1)} custom-call(bf16[4,96,768]{2,1,0:T(8,128)(2,1)S(1)} %pad_maximum_fusion.10.x_ref), custom_call_target="tpu_custom_call" | custom-call | tf_op jit(solution)/shard_map/pallas_call | solution.py:289
  21.8 24.9 %shard_map.379 = bf16[4,96,2688]{2,1,0:T(8,128)(2,1)} custom-call(bf16[4,96,2688]{2,1,0:T(8,128)(2,1)S(1)} %pad_maximum_fusion.1.x_ref), custom_call_target="tpu_custom_call" | custom-call | tf_op jit(solution)/shard_map/pallas_call | solution.py:289
  48.0 7.2 shard_map.382
  58.0 25.2 %shard_map.386 = bf16[4,96,2688]{2,1,0:T(8,128)(2,1)} custom-call(bf16[4,96,2688]{2,1,0:T(8,128)(2,1)S(1)} %pad_maximum_fusion.2.x_ref), custom_call_target="tpu_custom_call" | custom-call | tf_op jit(solution)/shard_map/pallas_call | solution.py:289
  83.3 11.1 %shard_map.374 = f32[4,4,8,128]{3,2,1,0:T(8,128)S(1)} custom-call(f32[8,128]{1,0:T(8,128)S(1)} %fusion.75.x_ref), custom_call_target="tpu_custom_call" | custom-call | tf_op jit(solution)/shard_map/pallas_call | solution.py:421
  98.2 20.0 %shard_map.375 = bf16[8,128,1536]{2,1,0:T(8,128)(2,1)S(1)} custom-call(bf16[128,1536]{1,0:T(8,128)(2,1)S(1)} %multiply_convert_fusion.15.x_ref), custom_call_target="tpu_custom_call" | custom-call | tf_op jit(solution)/shard_map/pallas_call | solution.py:99
  123.6 20.1 %shard_map.376 = bf16[8,128,1536]{2,1,0:T(8,128)(2,1)S(1)} custom-call(bf16[128,1536]{1,0:T(8,128)(2,1)S(1)} %copy.424.x_ref), custom_call_target="tpu_custom_call" | custom-call | tf_op jit(solution)/shard_map/pallas_call | solution.py:99
  154.3 5.0 fusion.24
  164.6 4.3 collective-permute-start
  171.3 2.9 copy.429
  174.2 3.1 collective-permute-done
  182.0 17.6 %shard_map.377 = f32[128,1536]{1,0:T(8,128)S(1)} custom-call(bf16[8,128,1536]{2,1,0:T(8,128)(2,1)S(1)} %bitcast.343), custom_call_target="tpu_custom_call" | custom-call | tf_op jit(solution)/shard_map/pallas_call | solution.py:188
  200.9 19.2 %shard_map.378 = bf16[8,128,1536]{2,1,0:T(8,128)(2,1)S(1)} custom-call(bf16[128,1536]{1,0:T(8,128)(2,1)S(1)} %multiply_convert_fusion.12.x_ref), custom_call_target="tpu_custom_call" | custom-call | tf_op jit(solution)/shard_map/pallas_call | solution.py:99
  222.2 8.4 fusion.2
  230.6 3.0 copy-done.31
  234.7 6.1 convolution_convert_fusion.5
  240.9 18.5 %shard_map.380 = f32[128,1536]{1,0:T(8,128)S(1)} custom-call(bf16[8,128,1536]{2,1,0:T(8,128)(2,1)S(1)} %bitcast.368), custom_call_target="tpu_custom_call" | custom-call | tf_op jit(solution)/shard_map/pallas_call | solution.py:188
  260.6 19.2 %shard_map.381 = bf16[8,128,1536]{2,1,0:T(8,128)(2,1)S(1)} custom-call(bf16[128,1536]{1,0:T(8,128)(2,1)S(1)} %multiply_convert_fusion.11.x_ref), custom_call_target="tpu_custom_call" | custom-call | tf_op jit(solution)/shard_map/pallas_call | solution.py:99
  279.9 3.4 fusion.29
  288.2 4.6 collective-permute-start.6
  292.8 7.2 collective-permute-start.5
  305.0 11.2 %collective-permute-done.5 = bf16[4,256,128]{2,1,0:T(8,128)(2,1)S(1)} collective-permute-done((bf16[4,256,128]{2,1,0:T(8,128)(2,1)S(1)}, bf16[4,256,128]{2,1,0:T(8,128)(2,1)S(1)}, u32[]{:S(2)}, u32[]{:S(2)}) %collective-permute-start.5) | collective-permute-done | bytes 262176 | tf_op jit(solution)/shard_map/ppermute | solution.py:499
  316.2 11.1 %collective-permute-done.4 = bf16[4,256,128]{2,1,0:T(8,128)(2,1)S(1)} collective-permute-done((bf16[4,256,128]{2,1,0:T(8,128)(2,1)S(1)}, bf16[4,256,128]{2,1,0:T(8,128)(2,1)S(1)}, u32[]{:S(2)}, u32[]{:S(2)}) %collective-permute-start.4) | collective-permute-done | bytes 262176 | tf_op jit(solution)/shard_map/ppermute | solution.py:499
  328.4 11.1 %shard_map.383 = (bf16[4,256,192]{2,1,0:T(8,128)(2,1)}, f32[4,256,8]{2,1,0:T(8,128)}) custom-call(bf16[4,256,192]{2,1,0:T(8,128)(2,1)} %copy.444.q_ref, bf16[4,4,256,128]{3,2,1,0:T(8,128)(2,1)} %pad_maximum_fusion.6.kv_ref, s32[4,256,1]{2,1,0:T(8,128)} %copy.445.pos_ref), custom_call_target="tpu_custom_call" | custom-call | tf_op jit(solution)/shard_map/pallas_call | solution.py:575
  341.9 17.6 %shard_map.384 = f32[128,1536]{1,0:T(8,128)S(1)} custom-call(bf16[8,128,1536]{2,1,0:T(8,128)(2,1)S(1)} %bitcast.348), custom_call_target="tpu_custom_call" | custom-call | tf_op jit(solution)/shard_map/pallas_call | solution.py:188
  360.8 19.3 %shard_map.385 = bf16[8,128,1536]{2,1,0:T(8,128)(2,1)S(1)} custom-call(bf16[128,1536]{1,0:T(8,128)(2,1)S(1)} %multiply_convert_fusion.10.x_ref), custom_call_target="tpu_custom_call" | custom-call | tf_op jit(solution)/shard_map/pallas_call | solution.py:99
  380.2 43.4 %all-gather.15.cloned.1.call-done = bf16[16,96,2688]{2,1,0:T(8,128)(2,1)} async-done(((bf16[4,96,2688]{2,1,0:T(8,128)(2,1)}), bf16[16,96,2688]{2,1,0:T(8,128)(2,1)}) %all-gather.15.cloned.1.call-update) | async-done | bytes 8257552 | tf_op jit(solution)/shard_map/all_gather | solution.py:612
  423.5 8.5 fusion
  436.3 4.8 convolution_convert_fusion.11
  441.2 7.7 multiply_convert_fusion.2
  448.9 4.8 convolution_convert_fusion.10
  453.7 4.8 convolution_convert_fusion.9
  461.0 5.4 fusion.12
  466.4 5.5 add_convert_fusion.1
  471.9 18.8 %shard_map.387 = f32[128,1536]{1,0:T(8,128)S(1)} custom-call(bf16[8,128,1536]{2,1,0:T(8,128)(2,1)S(1)} %bitcast.364), custom_call_target="tpu_custom_call" | custom-call | tf_op jit(solution)/shard_map/pallas_call | solution.py:188
  491.9 11.4 %reduce-scatter.9.cloned.1.call-done = bf16[1,384,896]{2,1,0:T(8,128)(2,1)} async-done(((bf16[4,384,896]{2,1,0:T(8,128)(2,1)}), bf16[1,384,896]{2,1,0:T(8,128)(2,1)}) %reduce-scatter.9.cloned.1.call-update) | async-done | bytes 688144 | tf_op jit(solution)/shard_map/reduce_scatter | solution.py:619
  503.4 20.0 %shard_map.388 = bf16[8,128,1536]{2,1,0:T(8,128)(2,1)S(1)} custom-call(bf16[128,1536]{1,0:T(8,128)(2,1)S(1)} %convert_element_type.291.x_ref), custom_call_target="tpu_custom_call" | custom-call | tf_op jit(solution)/shard_map/pallas_call | solution.py:99
  525.8 15.3 %shard_map.389 = (f32[4,256,192]{2,1,0:T(8,128)}, bf16[4,4,256,128]{3,2,1,0:T(8,128)(2,1)}) custom-call(bf16[4,256,192]{2,1,0:T(8,128)(2,1)} %copy.444.q_ref, bf16[4,4,256,128]{3,2,1,0:T(8,128)(2,1)} %pad_maximum_fusion.6.kv_ref, s32[4,256,1]{2,1,0:T(8,128)} %copy.445.pos_ref, f32[4,256,8]{2,1,0:T(8,128)} %get-tuple-element.71.lse_ref, ...), custom_call_target="tpu_custom_call" | custom-call | tf_op jit(solution)/shard_map/pallas_call | solution.py:591
  541.1 5.5 convolution_convert_fusion.4
  546.6 17.6 %shard_map.390 = f32[128,1536]{1,0:T(8,128)S(1)} custom-call(bf16[8,128,1536]{2,1,0:T(8,128)(2,1)S(1)} %bitcast.365), custom_call_target="tpu_custom_call" | custom-call | tf_op jit(solution)/shard_map/pallas_call | solution.py:188
  579.1 8.1 collective-permute-done.7
  587.2 34.3 %collective-permute-done.8 = bf16[4,256,128]{2,1,0:T(8,128)(2,1)} collective-permute-done((bf16[4,256,128]{2,1,0:T(8,128)(2,1)}, bf16[4,256,128]{2,1,0:T(8,128)(2,1)}, u32[]{:S(2)}, u32[]{:S(2)}) %collective-permute-start.8) | collective-permute-done | bytes 262176 | tf_op jit(solution)/shard_map/ppermute | solution.py:499
  638.3 3.1 convolution_convert_fusion.3
  641.5 17.8 %shard_map.391 = f32[128,1536]{1,0:T(8,128)S(1)} custom-call(bf16[8,128,1536]{2,1,0:T(8,128)(2,1)S(1)} %bitcast.366), custom_call_target="tpu_custom_call" | custom-call | tf_op jit(solution)/shard_map/pallas_call | solution.py:188
  660.5 19.3 %shard_map.392 = bf16[8,128,1536]{2,1,0:T(8,128)(2,1)S(1)} custom-call(bf16[128,1536]{1,0:T(8,128)(2,1)S(1)} %convert_element_type.306.x_ref), custom_call_target="tpu_custom_call" | custom-call | tf_op jit(solution)/shard_map/pallas_call | solution.py:99
  679.9 4.8 convolution_convert_fusion.8
  684.8 9.8 %multiply_convert_fusion = (bf16[1024,896]{1,0:T(8,128)(2,1)S(1)}, bf16[1024,896]{1,0:T(8,128)(2,1)S(1)}) fusion(f32[1024,1792]{1,0:T(8,128)} %copy-done.31, bf16[1024,1536]{1,0:T(8,128)(2,1)} %bitcast.362, bf16[1536,2688]{1,0:T(8,128)(2,1)} %bitcast.468), kind=kOutput, calls=%fused_computation.12 | convolution fusion | flops 2830499840 | bytes 16908288 | tf_op jit(solution)/shard_map/dot_general | solution.py:485
  694.7 5.1 convolution_convert_fusion.7
  699.8 4.9 convolution_convert_fusion.6
  704.7 2.9 copy.464
  712.7 5.8 fusion.9
  718.5 5.6 add_convert_fusion
  724.1 17.6 %shard_map.393 = f32[128,1536]{1,0:T(8,128)S(1)} custom-call(bf16[8,128,1536]{2,1,0:T(8,128)(2,1)S(1)} %bitcast.363), custom_call_target="tpu_custom_call" | custom-call | tf_op jit(solution)/shard_map/pallas_call | solution.py:188
  749.1 19.6 %shard_map.394 = bf16[8,128,1536]{2,1,0:T(8,128)(2,1)S(1)} custom-call(bf16[128,1536]{1,0:T(8,128)(2,1)S(1)} %convert_element_type.313.x_ref), custom_call_target="tpu_custom_call" | custom-call | tf_op jit(solution)/shard_map/pallas_call | solution.py:99
  784.0 3.3 copy.466
  788.9 3.9 fusion.26
  792.8 7.7 collective-permute-done.14
  808.7 4.6 fusion.20
  813.9 28.3 %shard_map.395 = bf16[4,4,96,768]{3,2,1,0:T(8,128)(2,1)} custom-call(bf16[4,4,96,768]{3,2,1,0:T(8,128)(2,1)S(1)} %maximum_bitcast_fusion.x_ref), custom_call_target="tpu_custom_call" | custom-call | tf_op jit(solution)/shard_map/pallas_call | solution.py:272
  842.3 3.0 convolution_convert_fusion
  845.3 17.7 %shard_map.396 = f32[128,1536]{1,0:T(8,128)S(1)} custom-call(bf16[8,128,1536]{2,1,0:T(8,128)(2,1)S(1)} %bitcast.367), custom_call_target="tpu_custom_call" | custom-call | tf_op jit(solution)/shard_map/pallas_call | solution.py:188
  877.5 13.6 %collective-permute-done.17 = bf16[96,3200]{1,0:T(8,128)(2,1)} collective-permute-done((bf16[96,3200]{1,0:T(8,128)(2,1)S(1)}, bf16[96,3200]{1,0:T(8,128)(2,1)}, u32[]{:S(2)}, u32[]{:S(2)}) %collective-permute-start.17) | collective-permute-done | bytes 614432 | tf_op jit(solution)/shard_map/ppermute | solution.py:311
  891.1 12.3 %collective-permute-done.18 = bf16[96,3200]{1,0:T(8,128)(2,1)} collective-permute-done((bf16[96,3200]{1,0:T(8,128)(2,1)S(1)}, bf16[96,3200]{1,0:T(8,128)(2,1)}, u32[]{:S(2)}, u32[]{:S(2)}) %collective-permute-start.18) | collective-permute-done | bytes 614432 | tf_op jit(solution)/shard_map/ppermute | solution.py:311
  906.1 13.7 %shard_map.397 = f32[88,128]{1,0:T(8,128)S(1)} custom-call(f32[88,128]{1,0:T(8,128)S(1)} %pad_bitcast_fusion.x_ref), custom_call_target="tpu_custom_call" | custom-call | tf_op jit(solution)/shard_map/pallas_call | solution.py:445
  (587 shorter events, 177.9 us)
Async XLA Ops:
  7.2 147.1 %all-gather.9.cloned.1.call-start = ((), (), s32[]{:S(2)}) async-start(), calls=%async_computation.16 | async-start | bytes 2949120 | tf_op jit(solution)/shard_map/all_gather | solution.py:612
  21.1 201.1 %all-gather.11.cloned.1.call-start = ((), (), s32[]{:S(2)}) async-start(), calls=%async_computation.17 | async-start | bytes 10321920 | tf_op jit(solution)/shard_map/all_gather | solution.py:612
  21.7 25.0 %copy-start.85 = (bf16[768,96]{0,1:T(8,128)(2,1)S(1)}, bf16[768,96]{0,1:T(8,128)(2,1)}, u32[]{:S(2)}) copy-start(bf16[768,96]{0,1:T(8,128)(2,1)} %param.38) | copy-start | bytes 442372
  21.7 25.3 %copy-start.86 = (bf16[96,768]{1,0:T(8,128)(2,1)S(1)}, bf16[96,768]{1,0:T(8,128)(2,1)}, u32[]{:S(2)}) copy-start(bf16[96,768]{1,0:T(8,128)(2,1)} %param.33) | copy-start | bytes 442372
  21.7 25.5 %copy-start.103 = (bf16[96,256]{1,0:T(8,128)(2,1)S(1)}, bf16[96,256]{1,0:T(8,128)(2,1)}, u32[]{:S(2)}) copy-start(bf16[96,256]{1,0:T(8,128)(2,1)} %param.35) | copy-start | bytes 147460
  21.8 25.7 %copy-start.104 = (bf16[96,256]{1,0:T(8,128)(2,1)S(1)}, bf16[96,256]{1,0:T(8,128)(2,1)}, u32[]{:S(2)}) copy-start(bf16[96,256]{1,0:T(8,128)(2,1)} %param.34) | copy-start | bytes 147460
  46.7 233.2 %all-gather.13.cloned.1.call-start = ((), (), s32[]{:S(2)}) async-start(), calls=%async_computation.18 | async-start | bytes 1966080 | tf_op jit(solution)/shard_map/all_gather | solution.py:612
  55.2 368.3 %all-gather.15.cloned.1.call-start = ((), (), s32[]{:S(2)}) async-start(), calls=%async_computation.19 | async-start | bytes 10321920 | tf_op jit(solution)/shard_map/all_gather | solution.py:612
  55.2 94.7 %collective-permute-start.1 = (s32[1,256]{1,0:T(1,128)}, s32[1,256]{1,0:T(1,128)}, u32[]{:S(2)}, u32[]{:S(2)}) collective-permute-start(s32[1,256]{1,0:T(1,128)} %param.23), channel_id=1, source_target_pairs={{0,8},{8,0},{16,24},{24,16},{1,9},{9,1},{17,25},{25,17},{2,10},{10... | collective-permute-start | bytes 3080 | tf_op jit(solution)/shard_map/ppermute | solution.py:325
  55.9 94.0 %collective-permute-start.2 = (s32[1,256]{1,0:T(1,128)}, s32[1,256]{1,0:T(1,128)}, u32[]{:S(2)}, u32[]{:S(2)}) collective-permute-start(s32[1,256]{1,0:T(1,128)} %param.23), channel_id=1, source_target_pairs={{0,16},{8,24},{16,0},{24,8},{1,17},{9,25},{17,1},{25,9},{2,18},{10... | collective-permute-start | bytes 3080 | tf_op jit(solution)/shard_map/ppermute | solution.py:325
  57.3 92.6 %collective-permute-start.3 = (s32[1,256]{1,0:T(1,128)}, s32[1,256]{1,0:T(1,128)}, u32[]{:S(2)}, u32[]{:S(2)}) collective-permute-start(s32[1,256]{1,0:T(1,128)} %param.23), channel_id=1, source_target_pairs={{0,24},{8,16},{16,8},{24,0},{1,25},{9,17},{17,9},{25,1},{2,26},{10... | collective-permute-start | bytes 3080 | tf_op jit(solution)/shard_map/ppermute | solution.py:325
  57.9 25.4 %copy-start.136 = (bf16[96]{0:T(256)(128)(2,1)S(1)}, bf16[96]{0:T(256)(128)(2,1)}, u32[]{:S(2)}) copy-start(bf16[96]{0:T(256)(128)(2,1)} %param.39) | copy-start | bytes 580
  57.9 25.4 %copy-start.137 = (bf16[96]{0:T(256)(128)(2,1)S(1)}, bf16[96]{0:T(256)(128)(2,1)}, u32[]{:S(2)}) copy-start(bf16[96]{0:T(256)(128)(2,1)} %param.32) | copy-start | bytes 580
  57.9 25.3 %copy-start.138 = (bf16[96]{0:T(256)(128)(2,1)S(1)}, bf16[96]{0:T(256)(128)(2,1)}, u32[]{:S(2)}) copy-start(bf16[96]{0:T(256)(128)(2,1)} %param.28) | copy-start | bytes 580
  57.9 25.3 %copy-start.139 = (bf16[96]{0:T(256)(128)(2,1)S(1)}, bf16[96]{0:T(256)(128)(2,1)}, u32[]{:S(2)}) copy-start(bf16[96]{0:T(256)(128)(2,1)} %param.24) | copy-start | bytes 580
  57.9 36.5 %copy-start.83 = (bf16[1,256,1536]{2,1,0:T(8,128)(2,1)S(1)}, bf16[1,256,1536]{2,1,0:T(8,128)(2,1)}, u32[]{:S(2)}) copy-start(bf16[1,256,1536]{2,1,0:T(8,128)(2,1)} %param.43) | copy-start | bytes 2359300
  57.9 36.5 %copy-start.84 = (bf16[1,256,1536]{2,1,0:T(8,128)(2,1)S(1)}, bf16[1,256,1536]{2,1,0:T(8,128)(2,1)}, u32[]{:S(2)}) copy-start(bf16[1,256,1536]{2,1,0:T(8,128)(2,1)} %param.22) | copy-start | bytes 2359300
  83.2 420.1 %reduce-scatter.9.cloned.1.call-start = ((), (), s32[]{:S(2)}) async-start(), calls=%async_computation.8 | async-start | bytes 3440640 | tf_op jit(solution)/shard_map/reduce_scatter | solution.py:619
  118.2 36.1 %copy-start = (bf16[8,128,1536]{2,1,0:T(8,128)(2,1)}, bf16[8,128,1536]{2,1,0:T(8,128)(2,1)S(1)}, u32[]{:S(2)}) copy-start(bf16[8,128,1536]{2,1,0:T(8,128)(2,1)S(1)} %shard_map.375) | copy-start | bytes 9437188
  145.4 54.5 %copy-start.89 = (f32[1536]{0:T(1024)}, f32[1536]{0:T(1024)S(1)}, u32[]{:S(2)}) copy-start(f32[1536]{0:T(1024)S(1)} %mul.710) | copy-start | bytes 18436
  146.2 113.4 %copy-start.91 = (f32[1536]{0:T(1024)}, f32[1536]{0:T(1024)S(1)}, u32[]{:S(2)}) copy-start(f32[1536]{0:T(1024)S(1)} %mul.718) | copy-start | bytes 18436
  164.6 12.8 %collective-permute-start = (bf16[4,2,192]{1,2,0:T(8,128)(2,1)}, bf16[4,2,192]{1,2,0:T(8,128)(2,1)}, u32[]{:S(2)}, u32[]{:S(2)}) collective-permute-start(bf16[4,2,192]{1,2,0:T(8,128)(2,1)} %slice.359), channel_id=1, source_target_pairs={{0,2},{2,4},{4,6},{1,3},{3,5},{5,7},{8,10},{10,12},{12,14},{9,11},... | collective-permute-start | bytes 9224 | tf_op jit(solution)/shard_map/ppermute | solution.py:499
  240.9 18.5 %copy-start.20 = (f32[128,1536]{1,0:T(8,128)S(1)}, f32[128,1536]{1,0:T(8,128)}, u32[]{:S(2)}) copy-start(f32[128,1536]{1,0:T(8,128)} %copy-done.19) | copy-start | bytes 2359300
  288.2 16.8 %collective-permute-start.6 = (bf16[4,256,128]{2,1,0:T(8,128)(2,1)S(1)}, bf16[4,256,128]{2,1,0:T(8,128)(2,1)S(1)}, u32[]{:S(2)}, u32[]{:S(2)}) collective-permute-start(bf16[4,256,128]{2,1,0:T(8,128)(2,1)S(1)} %get-tuple-element.326), channel_id=1, source_target_pairs={{0,2},{2,4},{4,6},{1,3},{3,5},{5,7},{8,10},{10,12},{12,14},{9,11},... | collective-permute-start | bytes 786440 | tf_op jit(solution)/shard_map/ppermute | solution.py:499
  292.8 23.5 %collective-permute-start.5 = (bf16[4,256,128]{2,1,0:T(8,128)(2,1)S(1)}, bf16[4,256,128]{2,1,0:T(8,128)(2,1)S(1)}, u32[]{:S(2)}, u32[]{:S(2)}) collective-permute-start(bf16[4,256,128]{2,1,0:T(8,128)(2,1)S(1)} %get-tuple-element.326), channel_id=1, source_target_pairs={{0,4},{2,6},{1,5},{3,7},{8,12},{10,14},{9,13},{11,15},{16,20},{18,... | collective-permute-start | bytes 786440 | tf_op jit(solution)/shard_map/ppermute | solution.py:499
  300.0 27.3 %collective-permute-start.4 = (bf16[4,256,128]{2,1,0:T(8,128)(2,1)S(1)}, bf16[4,256,128]{2,1,0:T(8,128)(2,1)S(1)}, u32[]{:S(2)}, u32[]{:S(2)}) collective-permute-start(bf16[4,256,128]{2,1,0:T(8,128)(2,1)S(1)} %get-tuple-element.326), channel_id=1, source_target_pairs={{0,6},{1,7},{8,14},{9,15},{16,22},{17,23},{24,30},{25,31}} | collective-permute-start | bytes 786440 | tf_op jit(solution)/shard_map/ppermute | solution.py:499
  341.9 18.7 %copy-start.93 = (f32[1536]{0:T(1024)S(1)}, f32[1536]{0:T(1024)}, u32[]{:S(2)}) copy-start(f32[1536]{0:T(1024)} %mul.751) | copy-start | bytes 18436
  380.1 43.4 %copy-start.9 = (bf16[8,128,1536]{2,1,0:T(8,128)(2,1)}, bf16[8,128,1536]{2,1,0:T(8,128)(2,1)S(1)}, u32[]{:S(2)}) copy-start(bf16[8,128,1536]{2,1,0:T(8,128)(2,1)S(1)} %shard_map.385) | copy-start | bytes 9437188
  441.1 219.3 %reduce-scatter.11.cloned.1.call-start = ((), (), s32[]{:S(2)}) async-start(), calls=%async_computation.9 | async-start | bytes 3440640 | tf_op jit(solution)/shard_map/reduce_scatter | solution.py:619
  458.5 201.9 %reduce-scatter.13.cloned.1.call-start = ((), (), s32[]{:S(2)}) async-start(), calls=%async_computation.10 | async-start | bytes 3440640 | tf_op jit(solution)/shard_map/reduce_scatter | solution.py:619
  471.9 18.8 %copy-start.26 = (f32[128,1536]{1,0:T(8,128)S(1)}, f32[128,1536]{1,0:T(8,128)}, u32[]{:S(2)}) copy-start(f32[128,1536]{1,0:T(8,128)} %copy-done.25) | copy-start | bytes 2359300
  471.9 18.8 %copy-start.94 = (f32[1536]{0:T(1024)S(1)}, f32[1536]{0:T(1024)}, u32[]{:S(2)}) copy-start(f32[1536]{0:T(1024)} %mul.751) | copy-start | bytes 18436
  471.9 18.8 %copy-start.128 = (f32[128]{0:T(128)S(1)}, f32[128]{0:T(128)}, u32[]{:S(2)}) copy-start(f32[128]{0:T(128)} %copy-done.127) | copy-start | bytes 1540
  491.6 257.5 %reduce-scatter.15.cloned.1.call-start = ((), (), s32[]{:S(2)}) async-start(), calls=%async_computation.11 | async-start | bytes 1966080 | tf_op jit(solution)/shard_map/reduce_scatter | solution.py:619
  503.3 20.1 %copy-start.82 = (bf16[16,96,512]{2,1,0:T(8,128)(2,1)S(1)}, bf16[16,96,512]{2,1,0:T(8,128)(2,1)}, u32[]{:S(2)}) copy-start(bf16[16,96,512]{2,1,0:T(8,128)(2,1)} %all-gather.13.cloned.1.call-done) | copy-start | bytes 4718596
  546.6 18.5 %copy-start.64 = (bf16[4,4,256,128]{3,2,1,0:T(8,128)(2,1)S(1)}, bf16[4,4,256,128]{3,2,1,0:T(8,128)(2,1)}, u32[]{:S(2)}) copy-start(bf16[4,4,256,128]{3,2,1,0:T(8,128)(2,1)} %get-tuple-element.80) | copy-start | bytes 3145732
  546.6 25.8 %copy-start.63 = (f32[4,256,32]{1,2,0:T(8,128)S(1)}, f32[4,256,32]{1,2,0:T(8,128)}, u32[]{:S(2)}) copy-start(f32[4,256,32]{1,2,0:T(8,128)} %get-tuple-element.339) | copy-start | bytes 393220
  546.6 25.8 %copy-start.78 = (f32[4,256,32]{1,2,0:T(8,128)S(1)}, f32[4,256,32]{1,2,0:T(8,128)}, u32[]{:S(2)}) copy-start(f32[4,256,32]{1,2,0:T(8,128)} %get-tuple-element.337) | copy-start | bytes 393220
  566.0 21.2 %collective-permute-start.7 = (bf16[4,256,128]{2,1,0:T(8,128)(2,1)}, bf16[4,256,128]{2,1,0:T(8,128)(2,1)}, u32[]{:S(2)}, u32[]{:S(2)}) collective-permute-start(bf16[4,256,128]{2,1,0:T(8,128)(2,1)} %get-tuple-element.313), channel_id=1, source_target_pairs={{2,0},{4,2},{6,4},{3,1},{5,3},{7,5},{10,8},{12,10},{14,12},{11,9},... | collective-permute-start | bytes 786440 | tf_op jit(solution)/shard_map/ppermute | solution.py:499
  567.3 54.2 %collective-permute-start.8 = (bf16[4,256,128]{2,1,0:T(8,128)(2,1)}, bf16[4,256,128]{2,1,0:T(8,128)(2,1)}, u32[]{:S(2)}, u32[]{:S(2)}) collective-permute-start(bf16[4,256,128]{2,1,0:T(8,128)(2,1)} %get-tuple-element.312), channel_id=1, source_target_pairs={{4,0},{6,2},{5,1},{7,3},{12,8},{14,10},{13,9},{15,11},{20,16},{22,... | collective-permute-start | bytes 786440 | tf_op jit(solution)/shard_map/ppermute | solution.py:499
  568.6 52.9 %collective-permute-start.9 = (bf16[4,256,128]{2,1,0:T(8,128)(2,1)}, bf16[4,256,128]{2,1,0:T(8,128)(2,1)}, u32[]{:S(2)}, u32[]{:S(2)}) collective-permute-start(bf16[4,256,128]{2,1,0:T(8,128)(2,1)} %get-tuple-element.311), channel_id=1, source_target_pairs={{6,0},{7,1},{14,8},{15,9},{22,16},{23,17},{30,24},{31,25}} | collective-permute-start | bytes 786440 | tf_op jit(solution)/shard_map/ppermute | solution.py:499
  578.9 44.9 %copy-start.98 = (f32[4,256]{1,0:T(4,128)S(1)}, f32[4,256]{1,0:T(4,128)}, u32[]{:S(2)}) copy-start(f32[4,256]{1,0:T(4,128)} %copy-done.96) | copy-start | bytes 12292
  578.9 44.9 %copy-start.124 = (f32[32]{0:T(128)S(1)}, f32[32]{0:T(128)}, u32[]{:S(2)}) copy-start(f32[32]{0:T(128)} %multiply_exponential_fusion) | copy-start | bytes 388
  638.3 233.2 %reduce-scatter.23.cloned.1.call-start = ((), (), s32[]{:S(2)}) async-start(), calls=%async_computation.15 | async-start | bytes 3440640 | tf_op jit(solution)/shard_map/reduce_scatter | solution.py:619
  641.5 17.9 %copy-start.24 = (f32[128,1536]{1,0:T(8,128)S(1)}, f32[128,1536]{1,0:T(8,128)}, u32[]{:S(2)}) copy-start(f32[128,1536]{1,0:T(8,128)} %copy-done.22) | copy-start | bytes 2359300
  641.5 17.9 %copy-start.92 = (f32[1536]{0:T(1024)S(1)}, f32[1536]{0:T(1024)}, u32[]{:S(2)}) copy-start(f32[1536]{0:T(1024)} %copy-done.91) | copy-start | bytes 18436
  641.5 18.7 %copy-start.42 = (f32[128,1536]{1,0:T(8,128)S(1)}, f32[128,1536]{1,0:T(8,128)}, u32[]{:S(2)}) copy-start(f32[128,1536]{1,0:T(8,128)} %copy-done.41) | copy-start | bytes 2359300
  660.4 24.3 %copy-start.43 = (f32[128,1536]{1,0:T(8,128)}, f32[128,1536]{1,0:T(8,128)S(1)}, u32[]{:S(2)}) copy-start(f32[128,1536]{1,0:T(8,128)S(1)} %multiply_add_fusion.1) | copy-start | bytes 2359300
  660.4 19.4 %copy-start.57 = (bf16[1024,896]{1,0:T(8,128)(2,1)S(1)}, bf16[1024,896]{1,0:T(8,128)(2,1)}, u32[]{:S(2)}) copy-start(bf16[1024,896]{1,0:T(8,128)(2,1)} %copy-done.56) | copy-start | bytes 5505028
  684.7 186.7 %reduce-scatter.21.cloned.1.call-start = ((), (), s32[]{:S(2)}) async-start(), calls=%async_computation.14 | async-start | bytes 3440640 | tf_op jit(solution)/shard_map/reduce_scatter | solution.py:619
  704.6 166.8 %reduce-scatter.19.cloned.1.call-start = ((), (), s32[]{:S(2)}) async-start(), calls=%async_computation.13 | async-start | bytes 3440640 | tf_op jit(solution)/shard_map/reduce_scatter | solution.py:619
  711.6 35.6 %collective-permute-start.10 = (bf16[128,1536]{0,1:T(8,128)(2,1)S(1)}, bf16[128,1536]{0,1:T(8,128)(2,1)}, u32[]{:S(2)}, u32[]{:S(2)}) collective-permute-start(bf16[128,1536]{0,1:T(8,128)(2,1)S(1)} %bitcast.419), channel_id=1, source_target_pairs={{0,1},{1,0},{2,3},{3,2},{4,5},{5,4},{6,7},{7,6},{8,9},{9,8},{10,11... | collective-permute-start | bytes 1179656 | tf_op jit(solution)/shard_map/ppermute | solution.py:782
  724.1 18.7 %copy-start.44 = (f32[128,1536]{1,0:T(8,128)S(1)}, f32[128,1536]{1,0:T(8,128)}, u32[]{:S(2)}) copy-start(f32[128,1536]{1,0:T(8,128)} %copy-done.43) | copy-start | bytes 2359300
  743.8 162.3 %reduce-scatter.17.cloned.1.call-start = ((), (), s32[]{:S(2)}) async-start(), calls=%async_computation.12 | async-start | bytes 2949120 | tf_op jit(solution)/shard_map/reduce_scatter | solution.py:863
  775.8 17.0 %collective-permute-start.12 = (bf16[96,2688]{1,0:T(8,128)(2,1)}, bf16[96,2688]{1,0:T(8,128)(2,1)}, u32[]{:S(2)}, u32[]{:S(2)}) collective-permute-start(bf16[96,2688]{1,0:T(8,128)(2,1)} %get-tuple-element.298), channel_id=1, source_target_pairs={{0,8},{8,0},{16,24},{24,16},{1,9},{9,1},{17,25},{25,17},{2,10},{10... | collective-permute-start | bytes 1548296 | tf_op jit(solution)/shard_map/ppermute | solution.py:311
  776.2 16.6 %collective-permute-start.13 = (bf16[96,2688]{1,0:T(8,128)(2,1)}, bf16[96,2688]{1,0:T(8,128)(2,1)}, u32[]{:S(2)}, u32[]{:S(2)}) collective-permute-start(bf16[96,2688]{1,0:T(8,128)(2,1)} %get-tuple-element.296), channel_id=1, source_target_pairs={{0,16},{8,24},{16,0},{24,8},{1,17},{9,25},{17,1},{25,9},{2,18},{10... | collective-permute-start | bytes 1548296 | tf_op jit(solution)/shard_map/ppermute | solution.py:311
  777.1 23.4 %collective-permute-start.14 = (bf16[96,2688]{1,0:T(8,128)(2,1)}, bf16[96,2688]{1,0:T(8,128)(2,1)}, u32[]{:S(2)}, u32[]{:S(2)}) collective-permute-start(bf16[96,2688]{1,0:T(8,128)(2,1)} %get-tuple-element.297), channel_id=1, source_target_pairs={{0,24},{8,16},{16,8},{24,0},{1,25},{9,17},{17,9},{25,1},{2,26},{10... | collective-permute-start | bytes 1548296 | tf_op jit(solution)/shard_map/ppermute | solution.py:311
  782.7 22.0 %collective-permute-start.11 = (f32[4,2,192]{1,2,0:T(8,128)}, f32[4,2,192]{1,2,0:T(8,128)}, u32[]{:S(2)}, u32[]{:S(2)}) collective-permute-start(f32[4,2,192]{1,2,0:T(8,128)} %slice.323), channel_id=1, source_target_pairs={{2,0},{4,2},{6,4},{3,1},{5,3},{7,5},{10,8},{12,10},{14,12},{11,9},... | collective-permute-start | bytes 18440 | tf_op jit(solution)/shard_map/ppermute | solution.py:499
  813.9 28.3 %copy-start.55 = (bf16[16,96,768]{2,1,0:T(8,128)(2,1)S(1)}, bf16[16,96,768]{2,1,0:T(8,128)(2,1)}, u32[]{:S(2)}) copy-start(bf16[16,96,768]{2,1,0:T(8,128)(2,1)} %all-gather.9.cloned.1.call-done) | copy-start | bytes 7077892
  845.3 18.1 %copy-start.40 = (f32[128,1536]{1,0:T(8,128)S(1)}, f32[128,1536]{1,0:T(8,128)}, u32[]{:S(2)}) copy-start(f32[128,1536]{1,0:T(8,128)} %copy-done.39) | copy-start | bytes 2359300
  863.8 12.3 %collective-permute-start.15 = (bf16[128,1536]{0,1:T(8,128)(2,1)S(1)}, bf16[128,1536]{0,1:T(8,128)(2,1)S(1)}, u32[]{:S(2)}, u32[]{:S(2)}) collective-permute-start(bf16[128,1536]{0,1:T(8,128)(2,1)S(1)} %bitcast.418), channel_id=1, source_target_pairs={{0,1},{1,0},{2,3},{3,2},{4,5},{5,4},{6,7},{7,6},{8,9},{9,8},{10,11... | collective-permute-start | bytes 1179656 | tf_op jit(solution)/shard_map/ppermute | solution.py:782
  874.3 3.2 collective-permute-start.16
  874.3 16.8 %collective-permute-start.17 = (bf16[96,3200]{1,0:T(8,128)(2,1)S(1)}, bf16[96,3200]{1,0:T(8,128)(2,1)}, u32[]{:S(2)}, u32[]{:S(2)}) collective-permute-start(bf16[96,3200]{1,0:T(8,128)(2,1)S(1)} %get-tuple-element.290), channel_id=1, source_target_pairs={{0,16},{8,24},{16,0},{24,8},{1,17},{9,25},{17,1},{25,9},{2,18},{10... | collective-permute-start | bytes 1843208 | tf_op jit(solution)/shard_map/ppermute | solution.py:311
  875.5 27.9 %collective-permute-start.18 = (bf16[96,3200]{1,0:T(8,128)(2,1)S(1)}, bf16[96,3200]{1,0:T(8,128)(2,1)}, u32[]{:S(2)}, u32[]{:S(2)}) collective-permute-start(bf16[96,3200]{1,0:T(8,128)(2,1)S(1)} %get-tuple-element.289), channel_id=1, source_target_pairs={{0,24},{8,16},{16,8},{24,0},{1,25},{9,17},{17,9},{25,1},{2,26},{10... | collective-permute-start | bytes 1843208 | tf_op jit(solution)/shard_map/ppermute | solution.py:311
  (115 other events, 647.9 us)
Sparse Core Ops, SparseCore 0:
  21.2 51.6 all-gather.8
  74.5 147.6 all-gather.10
  223.8 39.3 all-gather.12
  264.6 158.9 all-gather.14
  441.2 62.0 reduce-scatter.8
  505.5 53.8 reduce-scatter.10
  561.7 72.2 reduce-scatter.12
  638.4 35.5 reduce-scatter.14
  684.9 51.4 reduce-scatter.22
  738.5 58.5 reduce-scatter.20
  799.4 56.6 reduce-scatter.18
  858.3 47.8 reduce-scatter.16

commit v3 on v2

--- a/solution.py
+++ b/solution.py
@@ -312,10 +312,13 @@
     return parts
 
 
-def by_source(parts):
+def by_source(parts, start, count):
     dp = lax.axis_index("dp")
     devices = range(lax.axis_size("dp"))
-    return jnp.stack([wide(lax.select_n(dp, *(parts[j ^ i] for i in devices))) for j in devices], 1)
+    cut = [part[:, start : start + count] for part in parts]
+    return jnp.concatenate(
+        [wide(lax.select_n(dp, *(cut[j ^ i] for i in devices))) for j in devices], 1
+    )
 
 
 def from_all_dp(block):
@@ -793,9 +796,9 @@
     grad_three, second_gain_grad = norm_step(
         upstream, stream_three, gains[3], plane_scatter(partial)
     )
-    grad_three, second_sums[2] = together(grad_three, second_sums[2])
 
     grad_all = plane_gather(low(grad_three))
+    grad_all, second_sums[2] = together(grad_all, second_sums[2])
     attend_out_grad = dot_tn(grad_all, context)
     context_grad = low(dot_nn(grad_all, attend_out_w)).reshape(seqs, rows, q_cols)
     query_acc, kv_acc = attend_back(query_rows, kv_all, positions, totals, context_grad)
@@ -826,7 +829,7 @@
         gains[2],
         plane_scatter(dot_nt(qkv_grad, qkv_w)),
     )
-    grad_two, *second_sums[:2] = together(grad_two, *second_sums[:2])
+    grad_two, *second_sums = together(grad_two, *second_sums)
 
     grad_all = plane_gather(low(grad_two))
     partial, first_grads = feed_backward(grad_all, first_norm, first_w, feed_width, first_saved)
@@ -848,8 +851,7 @@
         spread = spread + jnp.pad(own_taps[j] * masked, ((0, 0), (2 - j, j), (0, 0)))
     spread, second_cat = together(spread, second_cat)
     returned = shifted(spread[:, :2], "ctx", -1)
-    second_done = by_source(send_back(second_cat))
-    returned, second_done = together(returned, second_done)
+    returned, *second_parts = together(returned, *send_back(second_cat))
     src_grad = spread[:, 2:] + jnp.pad(returned, ((0, 0), (rows - 2, 0), (0, 0)))
     proj_grad = jnp.concatenate(
         [low(src_grad * conv_input), gate_c_grad, low(src_grad * gate_b)], -1
@@ -881,12 +883,10 @@
     small = jnp.concatenate(
         [gain_rows.reshape(-1), query_gain_part, key_gain_part, taps_part.reshape(-1)]
     )
-    first_cat = jnp.concatenate(first_sums + [attend_sums], -1)
-    first_parts = send_back(first_cat)
-    small, mixer_sums, *first_parts = together(small, mixer_sums, *first_parts)
-    first_done = by_source(first_parts)
+    small = small_sum(small, 5)
+    first_parts = send_back(jnp.concatenate(first_sums + [attend_sums], -1))
+    hidden_grad, mixer_sums = together(hidden_grad, mixer_sums)
     mixer_done = wide(mixer_sums).reshape(seqs, part, -1).swapaxes(0, 1)
-    small = small_sum(small, 5)
     gain_sums = lax.dynamic_slice_in_dim(
         small[: 4 * width].reshape(4, width), (dp * ctxs + ctx) * part, part, 1
     )
@@ -899,8 +899,8 @@
     def columns(done, start, count):
         return done[:, :, start : start + count].reshape(part, -1)
 
-    def feed_columns(done, number):
-        return columns(done, number * feed_width, feed_width)[:, :units]
+    def feed_columns(parts, number):
+        return by_source(parts, number * feed_width, feed_width)[:, :units]
 
     attend_at = 3 * feed_width
 
@@ -912,20 +912,20 @@
         taps_grad,
         columns(mixer_done, 3 * channels, channels).T,
         gain_sums[1],
-        feed_columns(first_done, 0),
-        feed_columns(first_done, 1),
-        feed_columns(first_done, 2).T,
+        feed_columns(first_parts, 0),
+        feed_columns(first_parts, 1),
+        feed_columns(first_parts, 2).T,
         gain_sums[2],
-        columns(first_done, attend_at, q_cols),
-        columns(first_done, attend_at + q_cols, kv_cols),
-        columns(first_done, attend_at + q_cols + kv_cols, kv_cols),
+        by_source(first_parts, attend_at, q_cols),
+        by_source(first_parts, attend_at + q_cols, kv_cols),
+        by_source(first_parts, attend_at + q_cols + kv_cols, kv_cols),
         query_gain_grad,
         key_gain_grad,
-        columns(first_done, attend_at + q_cols + 2 * kv_cols, q_cols).T,
+        by_source(first_parts, attend_at + q_cols + 2 * kv_cols, q_cols).T,
         gain_sums[3],
-        feed_columns(second_done, 0),
-        feed_columns(second_done, 1),
-        feed_columns(second_done, 2).T,
+        feed_columns(second_parts, 0),
+        feed_columns(second_parts, 1),
+        feed_columns(second_parts, 2).T,
     )
 
 

time: 957 us -> 945 us (0.987)
  local copies, waits for them, and re-layouts: 95.6 us -> 83.1 us
    reduce_scatter x7, waiting for transfers between devices: 11.4 us -> 0.01 us  [collect_grads(): summed = lax.psum_scatter(grad, 'ctx', scatter_dimension=0, tiled=False)]
  transfers between devices with their start and end apart: 31 -> 31, of which waited for: 13 -> 13; matrix products, arithmetic and copies ran while one was open for 24% -> 26% of each run, Pallas kernels for 45% -> 47%
where the time goes in v3:
time: 945 us; the launch traced here: 935 us
  Pallas kernels  446 us (47%)
  waiting for transfers between devices  158 us (17%)
  matrix products  134 us (14%)
  local copies, waits for them, and re-layouts  83.1 us (9%)
  other arithmetic  66.2 us (7%)
  starting transfers between devices  30.4 us (3%)
  between operations  17.3 us (2%)
    pallas_call x8, Pallas kernels, plane_gather(): pl.pallas_call(gather_kernel, out_shape=jax.ShapeDtypeStruct((slots, rows...  156 us
    pallas_call x8, Pallas kernels, plane_scatter(): pl.pallas_call(scatter_kernel, out_shape=jax.ShapeDtypeStruct(block, jnp....  143 us
    ppermute x8, waiting for transfers between devices, shifted(): return lax.ppermute(block, axis, route)  78.5 us
    pallas_call x4, Pallas kernels, swap_blocks(): pl.pallas_call(swap_kernel, out_shape=jax.ShapeDtypeStruct(blocks.shape,...  67.9 us
    dot_general x8, matrix products, dot_nn(): lax.dot_general(left, right, (((1,), (0,)), ((), ())), preferred_element_...  48.5 us
    all_gather x4, waiting for transfers between devices, spread_weights(): whole = lax.all_gather(mine, 'ctx', axis=0, tiled=False)  45.5 us
    dot_general x10, matrix products, dot_nt(): lax.dot_general(left, right, (((1,), (1,)), ((), ())), preferred_element_...  42.8 us
    dot_general x10, matrix products, dot_tn(): lax.dot_general(left, right, (((0,), (0,)), ((), ())), preferred_element_...  42.8 us
  transfers between devices with their start and end apart: 31, of which 13 were waited for; matrix products, arithmetic and copies ran while one was open for 26% of the time, Pallas kernels for 47%

profile of v3, /device:TPU:0, one launch (start us, length us, event | category | flops | bytes accessed | tf_op | source)
XLA Modules:
  0.0 935.5 jit_solution(8154853515134884545)
XLA Ops:
  10.4 10.6 %shard_map.373 = bf16[4,96,768]{2,1,0:T(8,128)(2,1)} custom-call(bf16[4,96,768]{2,1,0:T(8,128)(2,1)S(1)} %pad_maximum_fusion.28.x_ref), custom_call_target="tpu_custom_call" | custom-call | tf_op jit(solution)/shard_map/pallas_call | solution.py:289
  21.8 24.9 %shard_map.379 = bf16[4,96,2688]{2,1,0:T(8,128)(2,1)} custom-call(bf16[4,96,2688]{2,1,0:T(8,128)(2,1)S(1)} %pad_maximum_fusion.1.x_ref), custom_call_target="tpu_custom_call" | custom-call | tf_op jit(solution)/shard_map/pallas_call | solution.py:289
  48.0 7.2 shard_map.382
  58.0 25.2 %shard_map.386 = bf16[4,96,2688]{2,1,0:T(8,128)(2,1)} custom-call(bf16[4,96,2688]{2,1,0:T(8,128)(2,1)S(1)} %pad_maximum_fusion.2.x_ref), custom_call_target="tpu_custom_call" | custom-call | tf_op jit(solution)/shard_map/pallas_call | solution.py:289
  83.3 11.1 %shard_map.374 = f32[4,4,8,128]{3,2,1,0:T(8,128)S(1)} custom-call(f32[8,128]{1,0:T(8,128)S(1)} %fusion.71.x_ref), custom_call_target="tpu_custom_call" | custom-call | tf_op jit(solution)/shard_map/pallas_call | solution.py:424
  98.1 20.0 %shard_map.375 = bf16[8,128,1536]{2,1,0:T(8,128)(2,1)S(1)} custom-call(bf16[128,1536]{1,0:T(8,128)(2,1)S(1)} %multiply_convert_fusion.15.x_ref), custom_call_target="tpu_custom_call" | custom-call | tf_op jit(solution)/shard_map/pallas_call | solution.py:99
  123.5 20.1 %shard_map.376 = bf16[8,128,1536]{2,1,0:T(8,128)(2,1)S(1)} custom-call(bf16[128,1536]{1,0:T(8,128)(2,1)S(1)} %copy.366.x_ref), custom_call_target="tpu_custom_call" | custom-call | tf_op jit(solution)/shard_map/pallas_call | solution.py:99
  154.3 5.0 fusion.24
  164.6 4.3 collective-permute-start
  174.2 3.2 collective-permute-done
  182.0 17.6 %shard_map.377 = f32[128,1536]{1,0:T(8,128)S(1)} custom-call(bf16[8,128,1536]{2,1,0:T(8,128)(2,1)S(1)} %bitcast.289), custom_call_target="tpu_custom_call" | custom-call | tf_op jit(solution)/shard_map/pallas_call | solution.py:188
  200.9 19.2 %shard_map.378 = bf16[8,128,1536]{2,1,0:T(8,128)(2,1)S(1)} custom-call(bf16[128,1536]{1,0:T(8,128)(2,1)S(1)} %multiply_convert_fusion.12.x_ref), custom_call_target="tpu_custom_call" | custom-call | tf_op jit(solution)/shard_map/pallas_call | solution.py:99
  222.2 8.4 fusion.2
  230.6 3.0 copy-done.31
  234.7 6.1 convolution_convert_fusion.5
  240.9 18.5 %shard_map.380 = f32[128,1536]{1,0:T(8,128)S(1)} custom-call(bf16[8,128,1536]{2,1,0:T(8,128)(2,1)S(1)} %bitcast.314), custom_call_target="tpu_custom_call" | custom-call | tf_op jit(solution)/shard_map/pallas_call | solution.py:188
  260.6 19.2 %shard_map.381 = bf16[8,128,1536]{2,1,0:T(8,128)(2,1)S(1)} custom-call(bf16[128,1536]{1,0:T(8,128)(2,1)S(1)} %multiply_convert_fusion.11.x_ref), custom_call_target="tpu_custom_call" | custom-call | tf_op jit(solution)/shard_map/pallas_call | solution.py:99
  279.9 3.4 fusion.29
  288.2 4.6 collective-permute-start.6
  292.8 7.2 collective-permute-start.5
  305.0 11.2 %collective-permute-done.5 = bf16[4,256,128]{2,1,0:T(8,128)(2,1)S(1)} collective-permute-done((bf16[4,256,128]{2,1,0:T(8,128)(2,1)S(1)}, bf16[4,256,128]{2,1,0:T(8,128)(2,1)S(1)}, u32[]{:S(2)}, u32[]{:S(2)}) %collective-permute-start.5) | collective-permute-done | bytes 262176 | tf_op jit(solution)/shard_map/ppermute | solution.py:502
  316.3 11.0 %collective-permute-done.4 = bf16[4,256,128]{2,1,0:T(8,128)(2,1)S(1)} collective-permute-done((bf16[4,256,128]{2,1,0:T(8,128)(2,1)S(1)}, bf16[4,256,128]{2,1,0:T(8,128)(2,1)S(1)}, u32[]{:S(2)}, u32[]{:S(2)}) %collective-permute-start.4) | collective-permute-done | bytes 262176 | tf_op jit(solution)/shard_map/ppermute | solution.py:502
  328.4 11.1 %shard_map.383 = (bf16[4,256,192]{2,1,0:T(8,128)(2,1)}, f32[4,256,8]{2,1,0:T(8,128)}) custom-call(bf16[4,256,192]{2,1,0:T(8,128)(2,1)} %copy.386.q_ref, bf16[4,4,256,128]{3,2,1,0:T(8,128)(2,1)} %pad_maximum_fusion.6.kv_ref, s32[4,256,1]{2,1,0:T(8,128)} %copy.387.pos_ref), custom_call_target="tpu_custom_call" | custom-call | tf_op jit(solution)/shard_map/pallas_call | solution.py:578
  342.0 17.6 %shard_map.384 = f32[128,1536]{1,0:T(8,128)S(1)} custom-call(bf16[8,128,1536]{2,1,0:T(8,128)(2,1)S(1)} %bitcast.294), custom_call_target="tpu_custom_call" | custom-call | tf_op jit(solution)/shard_map/pallas_call | solution.py:188
  360.8 19.3 %shard_map.385 = bf16[8,128,1536]{2,1,0:T(8,128)(2,1)S(1)} custom-call(bf16[128,1536]{1,0:T(8,128)(2,1)S(1)} %multiply_convert_fusion.10.x_ref), custom_call_target="tpu_custom_call" | custom-call | tf_op jit(solution)/shard_map/pallas_call | solution.py:99
  380.1 43.4 %all-gather.15.cloned.1.call-done = bf16[16,96,2688]{2,1,0:T(8,128)(2,1)} async-done(((bf16[4,96,2688]{2,1,0:T(8,128)(2,1)}), bf16[16,96,2688]{2,1,0:T(8,128)(2,1)}) %all-gather.15.cloned.1.call-update) | async-done | bytes 8257552 | tf_op jit(solution)/shard_map/all_gather | solution.py:615
  423.5 8.4 fusion
  436.2 4.8 convolution_convert_fusion.11
  441.1 7.7 multiply_convert_fusion.2
  448.8 4.8 convolution_convert_fusion.10
  453.6 4.8 convolution_convert_fusion.9
  460.8 5.4 fusion.12
  466.2 5.5 add_convert_fusion.1
  471.8 18.8 %shard_map.387 = f32[128,1536]{1,0:T(8,128)S(1)} custom-call(bf16[8,128,1536]{2,1,0:T(8,128)(2,1)S(1)} %bitcast.310), custom_call_target="tpu_custom_call" | custom-call | tf_op jit(solution)/shard_map/pallas_call | solution.py:188
  491.8 19.2 %shard_map.388 = bf16[8,128,1536]{2,1,0:T(8,128)(2,1)S(1)} custom-call(bf16[128,1536]{1,0:T(8,128)(2,1)S(1)} %fusion.77.x_ref), custom_call_target="tpu_custom_call" | custom-call | tf_op jit(solution)/shard_map/pallas_call | solution.py:99
  512.7 3.5 convolution_convert_fusion.14
  517.2 15.3 %shard_map.389 = (f32[4,256,192]{2,1,0:T(8,128)}, bf16[4,4,256,128]{3,2,1,0:T(8,128)(2,1)}) custom-call(bf16[4,256,192]{2,1,0:T(8,128)(2,1)} %copy.386.q_ref, bf16[4,4,256,128]{3,2,1,0:T(8,128)(2,1)} %pad_maximum_fusion.6.kv_ref, s32[4,256,1]{2,1,0:T(8,128)} %copy.387.pos_ref, f32[4,256,8]{2,1,0:T(8,128)} %get-tuple-element.71.lse_ref, ...), custom_call_target="tpu_custom_call" | custom-call | tf_op jit(solution)/shard_map/pallas_call | solution.py:594
  532.5 5.5 convolution_convert_fusion.4
  538.0 17.6 %shard_map.390 = f32[128,1536]{1,0:T(8,128)S(1)} custom-call(bf16[8,128,1536]{2,1,0:T(8,128)(2,1)S(1)} %bitcast.311), custom_call_target="tpu_custom_call" | custom-call | tf_op jit(solution)/shard_map/pallas_call | solution.py:188
  571.3 6.4 collective-permute-done.7
  577.7 36.9 %collective-permute-done.8 = bf16[4,256,128]{2,1,0:T(8,128)(2,1)} collective-permute-done((bf16[4,256,128]{2,1,0:T(8,128)(2,1)}, bf16[4,256,128]{2,1,0:T(8,128)(2,1)}, u32[]{:S(2)}, u32[]{:S(2)}) %collective-permute-start.8) | collective-permute-done | bytes 262176 | tf_op jit(solution)/shard_map/ppermute | solution.py:502
  618.7 3.0 fusion.51
  625.1 3.4 convolution_convert_fusion.12
  632.5 3.1 convolution_convert_fusion.3
  635.7 17.6 %shard_map.391 = f32[128,1536]{1,0:T(8,128)S(1)} custom-call(bf16[8,128,1536]{2,1,0:T(8,128)(2,1)S(1)} %bitcast.312), custom_call_target="tpu_custom_call" | custom-call | tf_op jit(solution)/shard_map/pallas_call | solution.py:188
  655.3 19.4 %shard_map.392 = bf16[8,128,1536]{2,1,0:T(8,128)(2,1)S(1)} custom-call(bf16[128,1536]{1,0:T(8,128)(2,1)S(1)} %convert_element_type.338.x_ref), custom_call_target="tpu_custom_call" | custom-call | tf_op jit(solution)/shard_map/pallas_call | solution.py:99
  674.7 4.8 convolution_convert_fusion.8
  679.6 9.8 %multiply_convert_fusion = (bf16[1024,896]{1,0:T(8,128)(2,1)S(1)}, bf16[1024,896]{1,0:T(8,128)(2,1)S(1)}) fusion(f32[1024,1792]{1,0:T(8,128)} %copy-done.31, bf16[1024,1536]{1,0:T(8,128)(2,1)} %bitcast.308, bf16[1536,2688]{1,0:T(8,128)(2,1)} %bitcast.405), kind=kOutput, calls=%fused_computation.12 | convolution fusion | flops 2830499840 | bytes 16908288 | tf_op jit(solution)/shard_map/dot_general | solution.py:488
  689.5 5.1 convolution_convert_fusion.7
  694.6 4.8 convolution_convert_fusion.6
  707.5 5.2 fusion.9
  712.7 5.6 add_convert_fusion
  718.4 17.6 %shard_map.393 = f32[128,1536]{1,0:T(8,128)S(1)} custom-call(bf16[8,128,1536]{2,1,0:T(8,128)(2,1)S(1)} %bitcast.309), custom_call_target="tpu_custom_call" | custom-call | tf_op jit(solution)/shard_map/pallas_call | solution.py:188
  743.6 19.2 %shard_map.394 = bf16[8,128,1536]{2,1,0:T(8,128)(2,1)S(1)} custom-call(bf16[128,1536]{1,0:T(8,128)(2,1)S(1)} %convert_element_type.345.x_ref), custom_call_target="tpu_custom_call" | custom-call | tf_op jit(solution)/shard_map/pallas_call | solution.py:99
  778.1 3.3 copy.408
  781.4 4.0 fusion.26
  786.3 7.5 collective-permute-done.11
  798.2 4.6 fusion.20
  803.4 28.3 %shard_map.395 = bf16[4,4,96,768]{3,2,1,0:T(8,128)(2,1)} custom-call(bf16[4,4,96,768]{3,2,1,0:T(8,128)(2,1)S(1)} %maximum_bitcast_fusion.x_ref), custom_call_target="tpu_custom_call" | custom-call | tf_op jit(solution)/shard_map/pallas_call | solution.py:272
  834.8 17.6 %shard_map.396 = f32[128,1536]{1,0:T(8,128)S(1)} custom-call(bf16[8,128,1536]{2,1,0:T(8,128)(2,1)S(1)} %bitcast.313), custom_call_target="tpu_custom_call" | custom-call | tf_op jit(solution)/shard_map/pallas_call | solution.py:188
  853.1 13.9 %shard_map.397 = f32[88,128]{1,0:T(8,128)S(1)} custom-call(f32[88,128]{1,0:T(8,128)S(1)} %pad_bitcast_fusion.x_ref), custom_call_target="tpu_custom_call" | custom-call | tf_op jit(solution)/shard_map/pallas_call | solution.py:448
  882.0 13.2 %collective-permute-done.18 = bf16[96,3200]{1,0:T(8,128)(2,1)S(1)} collective-permute-done((bf16[96,3200]{1,0:T(8,128)(2,1)S(1)}, bf16[96,3200]{1,0:T(8,128)(2,1)S(1)}, u32[]{:S(2)}, u32[]{:S(2)}) %collective-permute-start.18) | collective-permute-done | bytes 614432 | tf_op jit(solution)/shard_map/ppermute | solution.py:311
  895.1 13.8 %collective-permute-done.17 = bf16[96,3200]{1,0:T(8,128)(2,1)S(1)} collective-permute-done((bf16[96,3200]{1,0:T(8,128)(2,1)S(1)}, bf16[96,3200]{1,0:T(8,128)(2,1)S(1)}, u32[]{:S(2)}, u32[]{:S(2)}) %collective-permute-start.17) | collective-permute-done | bytes 614432 | tf_op jit(solution)/shard_map/ppermute | solution.py:311
  916.4 6.1 reduce-scatter.17.cloned.1.call-done
  (581 shorter events, 169.9 us)
Async XLA Ops:
  7.2 147.1 %all-gather.9.cloned.1.call-start = ((), (), s32[]{:S(2)}) async-start(), calls=%async_computation.16 | async-start | bytes 2949120 | tf_op jit(solution)/shard_map/all_gather | solution.py:615
  21.1 201.1 %all-gather.11.cloned.1.call-start = ((), (), s32[]{:S(2)}) async-start(), calls=%async_computation.17 | async-start | bytes 10321920 | tf_op jit(solution)/shard_map/all_gather | solution.py:615
  21.7 25.0 %copy-start.84 = (bf16[768,96]{0,1:T(8,128)(2,1)S(1)}, bf16[768,96]{0,1:T(8,128)(2,1)}, u32[]{:S(2)}) copy-start(bf16[768,96]{0,1:T(8,128)(2,1)} %param.38) | copy-start | bytes 442372
  21.7 25.3 %copy-start.85 = (bf16[96,768]{1,0:T(8,128)(2,1)S(1)}, bf16[96,768]{1,0:T(8,128)(2,1)}, u32[]{:S(2)}) copy-start(bf16[96,768]{1,0:T(8,128)(2,1)} %param.33) | copy-start | bytes 442372
  21.7 25.5 %copy-start.100 = (bf16[96,256]{1,0:T(8,128)(2,1)S(1)}, bf16[96,256]{1,0:T(8,128)(2,1)}, u32[]{:S(2)}) copy-start(bf16[96,256]{1,0:T(8,128)(2,1)} %param.35) | copy-start | bytes 147460
  21.8 25.7 %copy-start.101 = (bf16[96,256]{1,0:T(8,128)(2,1)S(1)}, bf16[96,256]{1,0:T(8,128)(2,1)}, u32[]{:S(2)}) copy-start(bf16[96,256]{1,0:T(8,128)(2,1)} %param.34) | copy-start | bytes 147460
  46.7 233.2 %all-gather.13.cloned.1.call-start = ((), (), s32[]{:S(2)}) async-start(), calls=%async_computation.18 | async-start | bytes 1966080 | tf_op jit(solution)/shard_map/all_gather | solution.py:615
  55.2 368.3 %all-gather.15.cloned.1.call-start = ((), (), s32[]{:S(2)}) async-start(), calls=%async_computation.19 | async-start | bytes 10321920 | tf_op jit(solution)/shard_map/all_gather | solution.py:615
  55.2 94.6 %collective-permute-start.1 = (s32[1,256]{1,0:T(1,128)}, s32[1,256]{1,0:T(1,128)}, u32[]{:S(2)}, u32[]{:S(2)}) collective-permute-start(s32[1,256]{1,0:T(1,128)} %param.23), channel_id=1, source_target_pairs={{0,8},{8,0},{16,24},{24,16},{1,9},{9,1},{17,25},{25,17},{2,10},{10... | collective-permute-start | bytes 3080 | tf_op jit(solution)/shard_map/ppermute | solution.py:328
  55.9 94.0 %collective-permute-start.2 = (s32[1,256]{1,0:T(1,128)}, s32[1,256]{1,0:T(1,128)}, u32[]{:S(2)}, u32[]{:S(2)}) collective-permute-start(s32[1,256]{1,0:T(1,128)} %param.23), channel_id=1, source_target_pairs={{0,16},{8,24},{16,0},{24,8},{1,17},{9,25},{17,1},{25,9},{2,18},{10... | collective-permute-start | bytes 3080 | tf_op jit(solution)/shard_map/ppermute | solution.py:328
  57.3 92.6 %collective-permute-start.3 = (s32[1,256]{1,0:T(1,128)}, s32[1,256]{1,0:T(1,128)}, u32[]{:S(2)}, u32[]{:S(2)}) collective-permute-start(s32[1,256]{1,0:T(1,128)} %param.23), channel_id=1, source_target_pairs={{0,24},{8,16},{16,8},{24,0},{1,25},{9,17},{17,9},{25,1},{2,26},{10... | collective-permute-start | bytes 3080 | tf_op jit(solution)/shard_map/ppermute | solution.py:328
  57.9 25.4 %copy-start.137 = (bf16[96]{0:T(256)(128)(2,1)S(1)}, bf16[96]{0:T(256)(128)(2,1)}, u32[]{:S(2)}) copy-start(bf16[96]{0:T(256)(128)(2,1)} %param.39) | copy-start | bytes 580
  57.9 25.4 %copy-start.138 = (bf16[96]{0:T(256)(128)(2,1)S(1)}, bf16[96]{0:T(256)(128)(2,1)}, u32[]{:S(2)}) copy-start(bf16[96]{0:T(256)(128)(2,1)} %param.32) | copy-start | bytes 580
  57.9 25.3 %copy-start.139 = (bf16[96]{0:T(256)(128)(2,1)S(1)}, bf16[96]{0:T(256)(128)(2,1)}, u32[]{:S(2)}) copy-start(bf16[96]{0:T(256)(128)(2,1)} %param.28) | copy-start | bytes 580
  57.9 25.3 %copy-start.140 = (bf16[96]{0:T(256)(128)(2,1)S(1)}, bf16[96]{0:T(256)(128)(2,1)}, u32[]{:S(2)}) copy-start(bf16[96]{0:T(256)(128)(2,1)} %param.24) | copy-start | bytes 580
  57.9 36.5 %copy-start.82 = (bf16[1,256,1536]{2,1,0:T(8,128)(2,1)S(1)}, bf16[1,256,1536]{2,1,0:T(8,128)(2,1)}, u32[]{:S(2)}) copy-start(bf16[1,256,1536]{2,1,0:T(8,128)(2,1)} %param.43) | copy-start | bytes 2359300
  57.9 36.5 %copy-start.83 = (bf16[1,256,1536]{2,1,0:T(8,128)(2,1)S(1)}, bf16[1,256,1536]{2,1,0:T(8,128)(2,1)}, u32[]{:S(2)}) copy-start(bf16[1,256,1536]{2,1,0:T(8,128)(2,1)} %param.22) | copy-start | bytes 2359300
  83.2 429.5 %reduce-scatter.9.cloned.1.call-start = ((), (), s32[]{:S(2)}) async-start(), calls=%async_computation.8 | async-start | bytes 3440640 | tf_op jit(solution)/shard_map/reduce_scatter | solution.py:622
  118.1 36.1 %copy-start = (bf16[8,128,1536]{2,1,0:T(8,128)(2,1)}, bf16[8,128,1536]{2,1,0:T(8,128)(2,1)S(1)}, u32[]{:S(2)}) copy-start(bf16[8,128,1536]{2,1,0:T(8,128)(2,1)S(1)} %shard_map.375) | copy-start | bytes 9437188
  145.4 54.5 %copy-start.88 = (f32[1536]{0:T(1024)}, f32[1536]{0:T(1024)S(1)}, u32[]{:S(2)}) copy-start(f32[1536]{0:T(1024)S(1)} %mul.710) | copy-start | bytes 18436
  146.1 113.5 %copy-start.90 = (f32[1536]{0:T(1024)}, f32[1536]{0:T(1024)S(1)}, u32[]{:S(2)}) copy-start(f32[1536]{0:T(1024)S(1)} %mul.718) | copy-start | bytes 18436
  164.6 12.8 %collective-permute-start = (bf16[4,2,192]{1,2,0:T(8,128)(2,1)}, bf16[4,2,192]{1,2,0:T(8,128)(2,1)}, u32[]{:S(2)}, u32[]{:S(2)}) collective-permute-start(bf16[4,2,192]{1,2,0:T(8,128)(2,1)} %slice.497), channel_id=1, source_target_pairs={{0,2},{2,4},{4,6},{1,3},{3,5},{5,7},{8,10},{10,12},{12,14},{9,11},... | collective-permute-start | bytes 9224 | tf_op jit(solution)/shard_map/ppermute | solution.py:502
  240.9 18.5 %copy-start.22 = (f32[128,1536]{1,0:T(8,128)S(1)}, f32[128,1536]{1,0:T(8,128)}, u32[]{:S(2)}) copy-start(f32[128,1536]{1,0:T(8,128)} %copy-done.21) | copy-start | bytes 2359300
  288.2 16.8 %collective-permute-start.6 = (bf16[4,256,128]{2,1,0:T(8,128)(2,1)S(1)}, bf16[4,256,128]{2,1,0:T(8,128)(2,1)S(1)}, u32[]{:S(2)}, u32[]{:S(2)}) collective-permute-start(bf16[4,256,128]{2,1,0:T(8,128)(2,1)S(1)} %get-tuple-element.351), channel_id=1, source_target_pairs={{0,2},{2,4},{4,6},{1,3},{3,5},{5,7},{8,10},{10,12},{12,14},{9,11},... | collective-permute-start | bytes 786440 | tf_op jit(solution)/shard_map/ppermute | solution.py:502
  292.8 23.5 %collective-permute-start.5 = (bf16[4,256,128]{2,1,0:T(8,128)(2,1)S(1)}, bf16[4,256,128]{2,1,0:T(8,128)(2,1)S(1)}, u32[]{:S(2)}, u32[]{:S(2)}) collective-permute-start(bf16[4,256,128]{2,1,0:T(8,128)(2,1)S(1)} %get-tuple-element.351), channel_id=1, source_target_pairs={{0,4},{2,6},{1,5},{3,7},{8,12},{10,14},{9,13},{11,15},{16,20},{18,... | collective-permute-start | bytes 786440 | tf_op jit(solution)/shard_map/ppermute | solution.py:502
  300.0 27.3 %collective-permute-start.4 = (bf16[4,256,128]{2,1,0:T(8,128)(2,1)S(1)}, bf16[4,256,128]{2,1,0:T(8,128)(2,1)S(1)}, u32[]{:S(2)}, u32[]{:S(2)}) collective-permute-start(bf16[4,256,128]{2,1,0:T(8,128)(2,1)S(1)} %get-tuple-element.351), channel_id=1, source_target_pairs={{0,6},{1,7},{8,14},{9,15},{16,22},{17,23},{24,30},{25,31}} | collective-permute-start | bytes 786440 | tf_op jit(solution)/shard_map/ppermute | solution.py:502
  342.0 18.7 %copy-start.79 = (f32[1536]{0:T(1024)S(1)}, f32[1536]{0:T(1024)}, u32[]{:S(2)}) copy-start(f32[1536]{0:T(1024)} %mul.751) | copy-start | bytes 18436
  380.1 43.4 %copy-start.10 = (bf16[8,128,1536]{2,1,0:T(8,128)(2,1)}, bf16[8,128,1536]{2,1,0:T(8,128)(2,1)S(1)}, u32[]{:S(2)}) copy-start(bf16[8,128,1536]{2,1,0:T(8,128)(2,1)S(1)} %shard_map.385) | copy-start | bytes 9437188
  441.0 214.3 %reduce-scatter.11.cloned.1.call-start = ((), (), s32[]{:S(2)}) async-start(), calls=%async_computation.9 | async-start | bytes 3440640 | tf_op jit(solution)/shard_map/reduce_scatter | solution.py:622
  458.4 196.8 %reduce-scatter.13.cloned.1.call-start = ((), (), s32[]{:S(2)}) async-start(), calls=%async_computation.10 | async-start | bytes 3440640 | tf_op jit(solution)/shard_map/reduce_scatter | solution.py:622
  471.8 18.8 %copy-start.25 = (f32[128,1536]{1,0:T(8,128)S(1)}, f32[128,1536]{1,0:T(8,128)}, u32[]{:S(2)}) copy-start(f32[128,1536]{1,0:T(8,128)} %copy-done.24) | copy-start | bytes 2359300
  471.8 18.8 %copy-start.80 = (f32[1536]{0:T(1024)S(1)}, f32[1536]{0:T(1024)}, u32[]{:S(2)}) copy-start(f32[1536]{0:T(1024)} %mul.751) | copy-start | bytes 18436
  471.8 18.8 %copy-start.117 = (f32[128]{0:T(128)S(1)}, f32[128]{0:T(128)}, u32[]{:S(2)}) copy-start(f32[128]{0:T(128)} %copy-done.116) | copy-start | bytes 1540
  491.4 19.6 %copy-start.133 = (f32[128]{0:T(128)}, f32[128]{0:T(128)S(1)}, u32[]{:S(2)}) copy-start(f32[128]{0:T(128)S(1)} %broadcast_multiply_fusion.5) | copy-start | bytes 1540
  491.5 252.1 %reduce-scatter.15.cloned.1.call-start = ((), (), s32[]{:S(2)}) async-start(), calls=%async_computation.11 | async-start | bytes 1966080 | tf_op jit(solution)/shard_map/reduce_scatter | solution.py:622
  556.5 21.2 %collective-permute-start.7 = (bf16[4,256,128]{2,1,0:T(8,128)(2,1)}, bf16[4,256,128]{2,1,0:T(8,128)(2,1)}, u32[]{:S(2)}, u32[]{:S(2)}) collective-permute-start(bf16[4,256,128]{2,1,0:T(8,128)(2,1)} %get-tuple-element.336), channel_id=1, source_target_pairs={{2,0},{4,2},{6,4},{3,1},{5,3},{7,5},{10,8},{12,10},{14,12},{11,9},... | collective-permute-start | bytes 786440 | tf_op jit(solution)/shard_map/ppermute | solution.py:502
  557.8 56.8 %collective-permute-start.8 = (bf16[4,256,128]{2,1,0:T(8,128)(2,1)}, bf16[4,256,128]{2,1,0:T(8,128)(2,1)}, u32[]{:S(2)}, u32[]{:S(2)}) collective-permute-start(bf16[4,256,128]{2,1,0:T(8,128)(2,1)} %get-tuple-element.335), channel_id=1, source_target_pairs={{4,0},{6,2},{5,1},{7,3},{12,8},{14,10},{13,9},{15,11},{20,16},{22,... | collective-permute-start | bytes 786440 | tf_op jit(solution)/shard_map/ppermute | solution.py:502
  559.1 55.5 %collective-permute-start.9 = (bf16[4,256,128]{2,1,0:T(8,128)(2,1)}, bf16[4,256,128]{2,1,0:T(8,128)(2,1)}, u32[]{:S(2)}, u32[]{:S(2)}) collective-permute-start(bf16[4,256,128]{2,1,0:T(8,128)(2,1)} %get-tuple-element.334), channel_id=1, source_target_pairs={{6,0},{7,1},{14,8},{15,9},{22,16},{23,17},{30,24},{31,25}} | collective-permute-start | bytes 786440 | tf_op jit(solution)/shard_map/ppermute | solution.py:502
  571.3 50.5 %copy-start.27 = (f32[4,256,64]{2,1,0:T(8,128)S(1)}, f32[4,256,64]{2,1,0:T(8,128)}, u32[]{:S(2)}) copy-start(f32[4,256,64]{2,1,0:T(8,128)} %copy-done.26) | copy-start | bytes 786436
  632.4 245.1 %reduce-scatter.23.cloned.1.call-start = ((), (), s32[]{:S(2)}) async-start(), calls=%async_computation.15 | async-start | bytes 3440640 | tf_op jit(solution)/shard_map/reduce_scatter | solution.py:622
  635.7 18.5 %copy-start.81 = (f32[1536]{0:T(1024)S(1)}, f32[1536]{0:T(1024)}, u32[]{:S(2)}) copy-start(f32[1536]{0:T(1024)} %mul.751) | copy-start | bytes 18436
  635.7 18.5 %copy-start.118 = (f32[128]{0:T(128)S(1)}, f32[128]{0:T(128)}, u32[]{:S(2)}) copy-start(f32[128]{0:T(128)} %copy-done.116) | copy-start | bytes 1540
  635.7 18.5 %copy-start.134 = (f32[128]{0:T(128)S(1)}, f32[128]{0:T(128)}, u32[]{:S(2)}) copy-start(f32[128]{0:T(128)} %copy-done.133) | copy-start | bytes 1540
  655.3 24.3 %copy-start.37 = (f32[128,1536]{1,0:T(8,128)}, f32[128,1536]{1,0:T(8,128)S(1)}, u32[]{:S(2)}) copy-start(f32[128,1536]{1,0:T(8,128)S(1)} %get-tuple-element.90) | copy-start | bytes 2359300
  655.3 19.5 %copy-start.57 = (bf16[1024,896]{1,0:T(8,128)(2,1)S(1)}, bf16[1024,896]{1,0:T(8,128)(2,1)}, u32[]{:S(2)}) copy-start(bf16[1024,896]{1,0:T(8,128)(2,1)} %copy-done.56) | copy-start | bytes 5505028
  679.6 197.9 %reduce-scatter.21.cloned.1.call-start = ((), (), s32[]{:S(2)}) async-start(), calls=%async_computation.14 | async-start | bytes 3440640 | tf_op jit(solution)/shard_map/reduce_scatter | solution.py:622
  699.5 178.1 %reduce-scatter.19.cloned.1.call-start = ((), (), s32[]{:S(2)}) async-start(), calls=%async_computation.13 | async-start | bytes 3440640 | tf_op jit(solution)/shard_map/reduce_scatter | solution.py:622
  706.5 35.1 %collective-permute-start.10 = (bf16[128,1536]{0,1:T(8,128)(2,1)S(1)}, bf16[128,1536]{0,1:T(8,128)(2,1)}, u32[]{:S(2)}, u32[]{:S(2)}) collective-permute-start(bf16[128,1536]{0,1:T(8,128)(2,1)S(1)} %bitcast.359), channel_id=1, source_target_pairs={{0,1},{1,0},{2,3},{3,2},{4,5},{5,4},{6,7},{7,6},{8,9},{9,8},{10,11... | collective-permute-start | bytes 1179656 | tf_op jit(solution)/shard_map/ppermute | solution.py:785
  718.4 18.7 %copy-start.38 = (f32[128,1536]{1,0:T(8,128)S(1)}, f32[128,1536]{1,0:T(8,128)}, u32[]{:S(2)}) copy-start(f32[128,1536]{1,0:T(8,128)} %copy-done.37) | copy-start | bytes 2359300
  738.0 184.5 %reduce-scatter.17.cloned.1.call-start = ((), (), s32[]{:S(2)}) async-start(), calls=%async_computation.12 | async-start | bytes 2949120 | tf_op jit(solution)/shard_map/reduce_scatter | solution.py:865
  769.9 23.9 %collective-permute-start.12 = (bf16[96,2688]{1,0:T(8,128)(2,1)}, bf16[96,2688]{1,0:T(8,128)(2,1)}, u32[]{:S(2)}, u32[]{:S(2)}) collective-permute-start(bf16[96,2688]{1,0:T(8,128)(2,1)} %get-tuple-element.320), channel_id=1, source_target_pairs={{0,8},{8,0},{16,24},{24,16},{1,9},{9,1},{17,25},{25,17},{2,10},{10... | collective-permute-start | bytes 1548296 | tf_op jit(solution)/shard_map/ppermute | solution.py:311
  770.3 23.5 %collective-permute-start.13 = (bf16[96,2688]{1,0:T(8,128)(2,1)}, bf16[96,2688]{1,0:T(8,128)(2,1)}, u32[]{:S(2)}, u32[]{:S(2)}) collective-permute-start(bf16[96,2688]{1,0:T(8,128)(2,1)} %get-tuple-element.319), channel_id=1, source_target_pairs={{0,16},{8,24},{16,0},{24,8},{1,17},{9,25},{17,1},{25,9},{2,18},{10... | collective-permute-start | bytes 1548296 | tf_op jit(solution)/shard_map/ppermute | solution.py:311
  771.6 23.0 %collective-permute-start.14 = (bf16[96,2688]{1,0:T(8,128)(2,1)}, bf16[96,2688]{1,0:T(8,128)(2,1)}, u32[]{:S(2)}, u32[]{:S(2)}) collective-permute-start(bf16[96,2688]{1,0:T(8,128)(2,1)} %get-tuple-element.318), channel_id=1, source_target_pairs={{0,24},{8,16},{16,8},{24,0},{1,25},{9,17},{17,9},{25,1},{2,26},{10... | collective-permute-start | bytes 1548296 | tf_op jit(solution)/shard_map/ppermute | solution.py:311
  776.8 17.0 %collective-permute-start.11 = (f32[4,2,192]{1,2,0:T(8,128)}, f32[4,2,192]{1,2,0:T(8,128)}, u32[]{:S(2)}, u32[]{:S(2)}) collective-permute-start(f32[4,2,192]{1,2,0:T(8,128)} %slice.427), channel_id=1, source_target_pairs={{2,0},{4,2},{6,4},{3,1},{5,3},{7,5},{10,8},{12,10},{14,12},{11,9},... | collective-permute-start | bytes 18440 | tf_op jit(solution)/shard_map/ppermute | solution.py:502
  803.4 28.3 %copy-start.55 = (bf16[16,96,768]{2,1,0:T(8,128)(2,1)S(1)}, bf16[16,96,768]{2,1,0:T(8,128)(2,1)}, u32[]{:S(2)}) copy-start(bf16[16,96,768]{2,1,0:T(8,128)(2,1)} %all-gather.9.cloned.1.call-done) | copy-start | bytes 7077892
  834.7 18.1 %copy-start.103 = (f32[1,4,4,96]{3,2,1,0:T(4,128)S(1)}, f32[1,4,4,96]{3,2,1,0:T(4,128)}, u32[]{:S(2)}) copy-start(f32[1,4,4,96]{3,2,1,0:T(4,128)} %stack.69) | copy-start | bytes 18436
  834.7 18.3 %copy-start.92 = (f32[4608]{0:T(1024)S(1)}, f32[4608]{0:T(1024)}, u32[]{:S(2)}) copy-start(f32[4608]{0:T(1024)} %reshape.624) | copy-start | bytes 55300
  834.8 18.2 %copy-start.132 = (f32[64]{0:T(128)S(1)}, f32[64]{0:T(128)}, u32[]{:S(2)}) copy-start(f32[64]{0:T(128)} %get-tuple-element.244) | copy-start | bytes 772
  834.8 18.2 %copy-start.135 = (f32[64]{0:T(128)S(1)}, f32[64]{0:T(128)}, u32[]{:S(2)}) copy-start(f32[64]{0:T(128)} %reduce_sum.254) | copy-start | bytes 772
  834.8 32.3 %copy-start.42 = (f32[128,1536]{1,0:T(8,128)S(1)}, f32[128,1536]{1,0:T(8,128)}, u32[]{:S(2)}) copy-start(f32[128,1536]{1,0:T(8,128)} %copy-done.41) | copy-start | bytes 2359300
  867.6 14.2 %collective-permute-start.15 = (bf16[128,1536]{0,1:T(8,128)(2,1)S(1)}, bf16[128,1536]{0,1:T(8,128)(2,1)S(1)}, u32[]{:S(2)}, u32[]{:S(2)}) collective-permute-start(bf16[128,1536]{0,1:T(8,128)(2,1)S(1)} %bitcast.358), channel_id=1, source_target_pairs={{0,1},{1,0},{2,3},{3,2},{4,5},{5,4},{6,7},{7,6},{8,9},{9,8},{10,11... | collective-permute-start | bytes 1179656 | tf_op jit(solution)/shard_map/ppermute | solution.py:785
  879.5 15.6 %collective-permute-start.18 = (bf16[96,3200]{1,0:T(8,128)(2,1)S(1)}, bf16[96,3200]{1,0:T(8,128)(2,1)S(1)}, u32[]{:S(2)}, u32[]{:S(2)}) collective-permute-start(bf16[96,3200]{1,0:T(8,128)(2,1)S(1)} %get-tuple-element.300), channel_id=1, source_target_pairs={{0,24},{8,16},{16,8},{24,0},{1,25},{9,17},{17,9},{25,1},{2,26},{10... | collective-permute-start | bytes 1843208 | tf_op jit(solution)/shard_map/ppermute | solution.py:311
  880.9 28.0 %collective-permute-start.17 = (bf16[96,3200]{1,0:T(8,128)(2,1)S(1)}, bf16[96,3200]{1,0:T(8,128)(2,1)S(1)}, u32[]{:S(2)}, u32[]{:S(2)}) collective-permute-start(bf16[96,3200]{1,0:T(8,128)(2,1)S(1)} %get-tuple-element.301), channel_id=1, source_target_pairs={{0,16},{8,24},{16,0},{24,8},{1,17},{9,25},{17,1},{25,9},{2,18},{10... | collective-permute-start | bytes 1843208 | tf_op jit(solution)/shard_map/ppermute | solution.py:311
  881.8 27.1 %collective-permute-start.16 = (bf16[96,3200]{1,0:T(8,128)(2,1)S(1)}, bf16[96,3200]{1,0:T(8,128)(2,1)S(1)}, u32[]{:S(2)}, u32[]{:S(2)}) collective-permute-start(bf16[96,3200]{1,0:T(8,128)(2,1)S(1)} %get-tuple-element.302), channel_id=1, source_target_pairs={{0,8},{8,0},{16,24},{24,16},{1,9},{9,1},{17,25},{25,17},{2,10},{10... | collective-permute-start | bytes 1843208 | tf_op jit(solution)/shard_map/ppermute | solution.py:311
  (117 other events, 760.3 us)
Sparse Core Ops, SparseCore 0:
  21.2 51.6 all-gather.8
  74.5 147.6 all-gather.10
  223.8 39.3 all-gather.12
  264.6 158.9 all-gather.14
  441.1 62.0 reduce-scatter.8
  505.4 53.8 reduce-scatter.10
  561.6 70.0 reduce-scatter.12
  634.0 36.4 reduce-scatter.14
  679.7 51.3 reduce-scatter.22
  733.3 59.2 reduce-scatter.20
  795.0 56.6 reduce-scatter.18
  874.2 48.2 reduce-scatter.16

commit v4 on v3

--- a/solution.py
+++ b/solution.py
@@ -883,10 +883,10 @@
     small = jnp.concatenate(
         [gain_rows.reshape(-1), query_gain_part, key_gain_part, taps_part.reshape(-1)]
     )
+    small, mixer_sums = together(small, mixer_sums)
     small = small_sum(small, 5)
     first_parts = send_back(jnp.concatenate(first_sums + [attend_sums], -1))
-    hidden_grad, mixer_sums = together(hidden_grad, mixer_sums)
-    mixer_done = wide(mixer_sums).reshape(seqs, part, -1).swapaxes(0, 1)
+    mixer_sums = mixer_sums.reshape(seqs, part, -1)
     gain_sums = lax.dynamic_slice_in_dim(
         small[: 4 * width].reshape(4, width), (dp * ctxs + ctx) * part, part, 1
     )
@@ -896,8 +896,9 @@
         small[4 * width + 2 * HD :].reshape(tens, 3, channels * seqs), ten, 0, keepdims=False
     )
 
-    def columns(done, start, count):
-        return done[:, :, start : start + count].reshape(part, -1)
+    def mixer_columns(number):
+        cut = mixer_sums[:, :, number * channels : (number + 1) * channels]
+        return jnp.concatenate([wide(cut[j]) for j in range(seqs)], 1)
 
     def feed_columns(parts, number):
         return by_source(parts, number * feed_width, feed_width)[:, :units]
@@ -908,9 +909,9 @@
         hidden_out,
         hidden_grad,
         gain_sums[0],
-        jnp.stack([columns(mixer_done, k * channels, channels) for k in range(3)]),
+        jnp.stack([mixer_columns(k) for k in range(3)]),
         taps_grad,
-        columns(mixer_done, 3 * channels, channels).T,
+        mixer_columns(3).T,
         gain_sums[1],
         feed_columns(first_parts, 0),
         feed_columns(first_parts, 1),

time: 945 us -> 942 us (level)
  transfers between devices with their start and end apart: 31 -> 31, of which waited for: 13 -> 13; matrix products, arithmetic and copies ran while one was open for 26% -> 26% of each run, Pallas kernels for 47% -> 45%
where the time goes in v4:
time: 942 us; the launch traced here: 932 us
  Pallas kernels  446 us (47%)
  waiting for transfers between devices  154 us (16%)
  matrix products  134 us (14%)
  local copies, waits for them, and re-layouts  81.9 us (9%)
  other arithmetic  67.4 us (7%)
  starting transfers between devices  31.3 us (3%)
  between operations  17.3 us (2%)
    pallas_call x8, Pallas kernels, plane_gather(): pl.pallas_call(gather_kernel, out_shape=jax.ShapeDtypeStruct((slots, rows...  156 us
    pallas_call x8, Pallas kernels, plane_scatter(): pl.pallas_call(scatter_kernel, out_shape=jax.ShapeDtypeStruct(block, jnp....  143 us
    ppermute x8, waiting for transfers between devices, shifted(): return lax.ppermute(block, axis, route)  78.5 us
    pallas_call x4, Pallas kernels, swap_blocks(): pl.pallas_call(swap_kernel, out_shape=jax.ShapeDtypeStruct(blocks.shape,...  67.9 us
    dot_general x8, matrix products, dot_nn(): lax.dot_general(left, right, (((1,), (0,)), ((), ())), preferred_element_...  48.5 us
    all_gather x4, waiting for transfers between devices, spread_weights(): whole = lax.all_gather(mine, 'ctx', axis=0, tiled=False)  45.5 us
    dot_general x10, matrix products, dot_nt(): lax.dot_general(left, right, (((1,), (1,)), ((), ())), preferred_element_...  42.8 us
    dot_general x10, matrix products, dot_tn(): lax.dot_general(left, right, (((0,), (0,)), ((), ())), preferred_element_...  42.8 us
  transfers between devices with their start and end apart: 31, of which 13 were waited for; matrix products, arithmetic and copies ran while one was open for 26% of the time, Pallas kernels for 45%

profile of v4, /device:TPU:0, one launch (start us, length us, event | category | flops | bytes accessed | tf_op | source)
XLA Modules:
  0.0 932.5 jit_solution(16211578374801426863)
XLA Ops:
  10.4 10.6 %shard_map.373 = bf16[4,96,768]{2,1,0:T(8,128)(2,1)} custom-call(bf16[4,96,768]{2,1,0:T(8,128)(2,1)S(1)} %pad_maximum_fusion.27.x_ref), custom_call_target="tpu_custom_call" | custom-call | tf_op jit(solution)/shard_map/pallas_call | solution.py:289
  21.8 24.9 %shard_map.379 = bf16[4,96,2688]{2,1,0:T(8,128)(2,1)} custom-call(bf16[4,96,2688]{2,1,0:T(8,128)(2,1)S(1)} %pad_maximum_fusion.1.x_ref), custom_call_target="tpu_custom_call" | custom-call | tf_op jit(solution)/shard_map/pallas_call | solution.py:289
  48.0 7.2 shard_map.382
  58.0 25.2 %shard_map.386 = bf16[4,96,2688]{2,1,0:T(8,128)(2,1)} custom-call(bf16[4,96,2688]{2,1,0:T(8,128)(2,1)S(1)} %pad_maximum_fusion.2.x_ref), custom_call_target="tpu_custom_call" | custom-call | tf_op jit(solution)/shard_map/pallas_call | solution.py:289
  83.3 11.1 %shard_map.374 = f32[4,4,8,128]{3,2,1,0:T(8,128)S(1)} custom-call(f32[8,128]{1,0:T(8,128)S(1)} %fusion.71.x_ref), custom_call_target="tpu_custom_call" | custom-call | tf_op jit(solution)/shard_map/pallas_call | solution.py:424
  98.1 20.0 %shard_map.375 = bf16[8,128,1536]{2,1,0:T(8,128)(2,1)S(1)} custom-call(bf16[128,1536]{1,0:T(8,128)(2,1)S(1)} %multiply_convert_fusion.15.x_ref), custom_call_target="tpu_custom_call" | custom-call | tf_op jit(solution)/shard_map/pallas_call | solution.py:99
  123.5 20.1 %shard_map.376 = bf16[8,128,1536]{2,1,0:T(8,128)(2,1)S(1)} custom-call(bf16[128,1536]{1,0:T(8,128)(2,1)S(1)} %copy.360.x_ref), custom_call_target="tpu_custom_call" | custom-call | tf_op jit(solution)/shard_map/pallas_call | solution.py:99
  154.3 5.0 fusion.24
  164.6 4.3 collective-permute-start
  174.2 3.2 collective-permute-done
  182.0 17.6 %shard_map.377 = f32[128,1536]{1,0:T(8,128)S(1)} custom-call(bf16[8,128,1536]{2,1,0:T(8,128)(2,1)S(1)} %bitcast.324), custom_call_target="tpu_custom_call" | custom-call | tf_op jit(solution)/shard_map/pallas_call | solution.py:188
  200.9 19.2 %shard_map.378 = bf16[8,128,1536]{2,1,0:T(8,128)(2,1)S(1)} custom-call(bf16[128,1536]{1,0:T(8,128)(2,1)S(1)} %multiply_convert_fusion.12.x_ref), custom_call_target="tpu_custom_call" | custom-call | tf_op jit(solution)/shard_map/pallas_call | solution.py:99
  222.2 8.4 fusion.2
  230.6 3.0 copy-done.31
  234.7 6.1 convolution_convert_fusion.5
  240.9 18.5 %shard_map.380 = f32[128,1536]{1,0:T(8,128)S(1)} custom-call(bf16[8,128,1536]{2,1,0:T(8,128)(2,1)S(1)} %bitcast.349), custom_call_target="tpu_custom_call" | custom-call | tf_op jit(solution)/shard_map/pallas_call | solution.py:188
  260.6 19.2 %shard_map.381 = bf16[8,128,1536]{2,1,0:T(8,128)(2,1)S(1)} custom-call(bf16[128,1536]{1,0:T(8,128)(2,1)S(1)} %multiply_convert_fusion.11.x_ref), custom_call_target="tpu_custom_call" | custom-call | tf_op jit(solution)/shard_map/pallas_call | solution.py:99
  279.9 3.4 fusion.29
  288.2 4.6 collective-permute-start.6
  292.8 7.2 collective-permute-start.5
  305.0 11.2 %collective-permute-done.5 = bf16[4,256,128]{2,1,0:T(8,128)(2,1)S(1)} collective-permute-done((bf16[4,256,128]{2,1,0:T(8,128)(2,1)S(1)}, bf16[4,256,128]{2,1,0:T(8,128)(2,1)S(1)}, u32[]{:S(2)}, u32[]{:S(2)}) %collective-permute-start.5) | collective-permute-done | bytes 262176 | tf_op jit(solution)/shard_map/ppermute | solution.py:502
  316.3 11.0 %collective-permute-done.4 = bf16[4,256,128]{2,1,0:T(8,128)(2,1)S(1)} collective-permute-done((bf16[4,256,128]{2,1,0:T(8,128)(2,1)S(1)}, bf16[4,256,128]{2,1,0:T(8,128)(2,1)S(1)}, u32[]{:S(2)}, u32[]{:S(2)}) %collective-permute-start.4) | collective-permute-done | bytes 262176 | tf_op jit(solution)/shard_map/ppermute | solution.py:502
  328.4 11.1 %shard_map.383 = (bf16[4,256,192]{2,1,0:T(8,128)(2,1)}, f32[4,256,8]{2,1,0:T(8,128)}) custom-call(bf16[4,256,192]{2,1,0:T(8,128)(2,1)} %copy.380.q_ref, bf16[4,4,256,128]{3,2,1,0:T(8,128)(2,1)} %pad_maximum_fusion.6.kv_ref, s32[4,256,1]{2,1,0:T(8,128)} %copy.381.pos_ref), custom_call_target="tpu_custom_call" | custom-call | tf_op jit(solution)/shard_map/pallas_call | solution.py:578
  342.0 17.6 %shard_map.384 = f32[128,1536]{1,0:T(8,128)S(1)} custom-call(bf16[8,128,1536]{2,1,0:T(8,128)(2,1)S(1)} %bitcast.329), custom_call_target="tpu_custom_call" | custom-call | tf_op jit(solution)/shard_map/pallas_call | solution.py:188
  360.8 19.3 %shard_map.385 = bf16[8,128,1536]{2,1,0:T(8,128)(2,1)S(1)} custom-call(bf16[128,1536]{1,0:T(8,128)(2,1)S(1)} %multiply_convert_fusion.10.x_ref), custom_call_target="tpu_custom_call" | custom-call | tf_op jit(solution)/shard_map/pallas_call | solution.py:99
  380.1 43.4 %all-gather.15.cloned.1.call-done = bf16[16,96,2688]{2,1,0:T(8,128)(2,1)} async-done(((bf16[4,96,2688]{2,1,0:T(8,128)(2,1)}), bf16[16,96,2688]{2,1,0:T(8,128)(2,1)}) %all-gather.15.cloned.1.call-update) | async-done | bytes 8257552 | tf_op jit(solution)/shard_map/all_gather | solution.py:615
  423.5 8.4 fusion
  436.2 4.8 convolution_convert_fusion.11
  441.1 7.7 multiply_convert_fusion.2
  448.8 4.8 convolution_convert_fusion.10
  453.6 4.8 convolution_convert_fusion.9
  460.8 5.4 fusion.12
  466.2 5.5 add_convert_fusion.1
  471.8 18.8 %shard_map.387 = f32[128,1536]{1,0:T(8,128)S(1)} custom-call(bf16[8,128,1536]{2,1,0:T(8,128)(2,1)S(1)} %bitcast.345), custom_call_target="tpu_custom_call" | custom-call | tf_op jit(solution)/shard_map/pallas_call | solution.py:188
  491.8 19.2 %shard_map.388 = bf16[8,128,1536]{2,1,0:T(8,128)(2,1)S(1)} custom-call(bf16[128,1536]{1,0:T(8,128)(2,1)S(1)} %fusion.77.x_ref), custom_call_target="tpu_custom_call" | custom-call | tf_op jit(solution)/shard_map/pallas_call | solution.py:99
  512.7 3.5 convolution_convert_fusion.14
  517.2 15.3 %shard_map.389 = (f32[4,256,192]{2,1,0:T(8,128)}, bf16[4,4,256,128]{3,2,1,0:T(8,128)(2,1)}) custom-call(bf16[4,256,192]{2,1,0:T(8,128)(2,1)} %copy.380.q_ref, bf16[4,4,256,128]{3,2,1,0:T(8,128)(2,1)} %pad_maximum_fusion.6.kv_ref, s32[4,256,1]{2,1,0:T(8,128)} %copy.381.pos_ref, f32[4,256,8]{2,1,0:T(8,128)} %get-tuple-element.71.lse_ref, ...), custom_call_target="tpu_custom_call" | custom-call | tf_op jit(solution)/shard_map/pallas_call | solution.py:594
  532.5 5.5 convolution_convert_fusion.4
  538.0 17.6 %shard_map.390 = f32[128,1536]{1,0:T(8,128)S(1)} custom-call(bf16[8,128,1536]{2,1,0:T(8,128)(2,1)S(1)} %bitcast.346), custom_call_target="tpu_custom_call" | custom-call | tf_op jit(solution)/shard_map/pallas_call | solution.py:188
  571.3 6.4 collective-permute-done.7
  577.7 36.9 %collective-permute-done.8 = bf16[4,256,128]{2,1,0:T(8,128)(2,1)} collective-permute-done((bf16[4,256,128]{2,1,0:T(8,128)(2,1)}, bf16[4,256,128]{2,1,0:T(8,128)(2,1)}, u32[]{:S(2)}, u32[]{:S(2)}) %collective-permute-start.8) | collective-permute-done | bytes 262176 | tf_op jit(solution)/shard_map/ppermute | solution.py:502
  618.7 3.0 fusion.51
  625.1 3.4 convolution_convert_fusion.12
  632.5 3.1 convolution_convert_fusion.3
  635.7 17.6 %shard_map.391 = f32[128,1536]{1,0:T(8,128)S(1)} custom-call(bf16[8,128,1536]{2,1,0:T(8,128)(2,1)S(1)} %bitcast.347), custom_call_target="tpu_custom_call" | custom-call | tf_op jit(solution)/shard_map/pallas_call | solution.py:188
  655.3 19.4 %shard_map.392 = bf16[8,128,1536]{2,1,0:T(8,128)(2,1)S(1)} custom-call(bf16[128,1536]{1,0:T(8,128)(2,1)S(1)} %convert_element_type.401.x_ref), custom_call_target="tpu_custom_call" | custom-call | tf_op jit(solution)/shard_map/pallas_call | solution.py:99
  674.7 4.8 convolution_convert_fusion.8
  679.6 9.8 %multiply_convert_fusion = (bf16[1024,896]{1,0:T(8,128)(2,1)S(1)}, bf16[1024,896]{1,0:T(8,128)(2,1)S(1)}) fusion(f32[1024,1792]{1,0:T(8,128)} %copy-done.31, bf16[1024,1536]{1,0:T(8,128)(2,1)} %bitcast.343, bf16[1536,2688]{1,0:T(8,128)(2,1)} %bitcast.438), kind=kOutput, calls=%fused_computation.12 | convolution fusion | flops 2830499840 | bytes 16908288 | tf_op jit(solution)/shard_map/dot_general | solution.py:488
  689.5 5.1 convolution_convert_fusion.7
  694.6 4.8 convolution_convert_fusion.6
  707.5 5.2 fusion.9
  712.7 5.6 add_convert_fusion
  718.4 17.6 %shard_map.393 = f32[128,1536]{1,0:T(8,128)S(1)} custom-call(bf16[8,128,1536]{2,1,0:T(8,128)(2,1)S(1)} %bitcast.344), custom_call_target="tpu_custom_call" | custom-call | tf_op jit(solution)/shard_map/pallas_call | solution.py:188
  743.6 19.2 %shard_map.394 = bf16[8,128,1536]{2,1,0:T(8,128)(2,1)S(1)} custom-call(bf16[128,1536]{1,0:T(8,128)(2,1)S(1)} %convert_element_type.408.x_ref), custom_call_target="tpu_custom_call" | custom-call | tf_op jit(solution)/shard_map/pallas_call | solution.py:99
  778.1 3.3 copy.402
  781.4 4.0 fusion.26
  786.3 7.5 collective-permute-done.11
  798.2 4.6 fusion.20
  803.4 28.3 %shard_map.395 = bf16[4,4,96,768]{3,2,1,0:T(8,128)(2,1)} custom-call(bf16[4,4,96,768]{3,2,1,0:T(8,128)(2,1)S(1)} %maximum_bitcast_fusion.x_ref), custom_call_target="tpu_custom_call" | custom-call | tf_op jit(solution)/shard_map/pallas_call | solution.py:272
  834.7 17.6 %shard_map.396 = f32[128,1536]{1,0:T(8,128)S(1)} custom-call(bf16[8,128,1536]{2,1,0:T(8,128)(2,1)S(1)} %bitcast.348), custom_call_target="tpu_custom_call" | custom-call | tf_op jit(solution)/shard_map/pallas_call | solution.py:188
  869.5 13.2 %collective-permute-done.18 = bf16[96,3200]{1,0:T(8,128)(2,1)S(1)} collective-permute-done((bf16[96,3200]{1,0:T(8,128)(2,1)}, bf16[96,3200]{1,0:T(8,128)(2,1)S(1)}, u32[]{:S(2)}, u32[]{:S(2)}) %collective-permute-start.18) | collective-permute-done | bytes 614432 | tf_op jit(solution)/shard_map/ppermute | solution.py:311
  882.6 13.2 %collective-permute-done.17 = bf16[96,3200]{1,0:T(8,128)(2,1)S(1)} collective-permute-done((bf16[96,3200]{1,0:T(8,128)(2,1)}, bf16[96,3200]{1,0:T(8,128)(2,1)S(1)}, u32[]{:S(2)}, u32[]{:S(2)}) %collective-permute-start.17) | collective-permute-done | bytes 614432 | tf_op jit(solution)/shard_map/ppermute | solution.py:311
  903.2 3.0 reduce-scatter.17.cloned.1.call-done
  906.3 13.8 %shard_map.397 = f32[88,128]{1,0:T(8,128)S(1)} custom-call(f32[88,128]{1,0:T(8,128)S(1)} %pad_bitcast_fusion.x_ref), custom_call_target="tpu_custom_call" | custom-call | tf_op jit(solution)/shard_map/pallas_call | solution.py:448
  (580 shorter events, 170.8 us)
Async XLA Ops:
  7.2 147.1 %all-gather.9.cloned.1.call-start = ((), (), s32[]{:S(2)}) async-start(), calls=%async_computation.16 | async-start | bytes 2949120 | tf_op jit(solution)/shard_map/all_gather | solution.py:615
  21.1 201.1 %all-gather.11.cloned.1.call-start = ((), (), s32[]{:S(2)}) async-start(), calls=%async_computation.17 | async-start | bytes 10321920 | tf_op jit(solution)/shard_map/all_gather | solution.py:615
  21.7 25.0 %copy-start.84 = (bf16[768,96]{0,1:T(8,128)(2,1)S(1)}, bf16[768,96]{0,1:T(8,128)(2,1)}, u32[]{:S(2)}) copy-start(bf16[768,96]{0,1:T(8,128)(2,1)} %param.38) | copy-start | bytes 442372
  21.7 25.3 %copy-start.85 = (bf16[96,768]{1,0:T(8,128)(2,1)S(1)}, bf16[96,768]{1,0:T(8,128)(2,1)}, u32[]{:S(2)}) copy-start(bf16[96,768]{1,0:T(8,128)(2,1)} %param.33) | copy-start | bytes 442372
  21.7 25.5 %copy-start.100 = (bf16[96,256]{1,0:T(8,128)(2,1)S(1)}, bf16[96,256]{1,0:T(8,128)(2,1)}, u32[]{:S(2)}) copy-start(bf16[96,256]{1,0:T(8,128)(2,1)} %param.35) | copy-start | bytes 147460
  21.8 25.7 %copy-start.101 = (bf16[96,256]{1,0:T(8,128)(2,1)S(1)}, bf16[96,256]{1,0:T(8,128)(2,1)}, u32[]{:S(2)}) copy-start(bf16[96,256]{1,0:T(8,128)(2,1)} %param.34) | copy-start | bytes 147460
  46.7 233.2 %all-gather.13.cloned.1.call-start = ((), (), s32[]{:S(2)}) async-start(), calls=%async_computation.18 | async-start | bytes 1966080 | tf_op jit(solution)/shard_map/all_gather | solution.py:615
  55.2 368.3 %all-gather.15.cloned.1.call-start = ((), (), s32[]{:S(2)}) async-start(), calls=%async_computation.19 | async-start | bytes 10321920 | tf_op jit(solution)/shard_map/all_gather | solution.py:615
  55.2 94.6 %collective-permute-start.1 = (s32[1,256]{1,0:T(1,128)}, s32[1,256]{1,0:T(1,128)}, u32[]{:S(2)}, u32[]{:S(2)}) collective-permute-start(s32[1,256]{1,0:T(1,128)} %param.23), channel_id=1, source_target_pairs={{0,8},{8,0},{16,24},{24,16},{1,9},{9,1},{17,25},{25,17},{2,10},{10... | collective-permute-start | bytes 3080 | tf_op jit(solution)/shard_map/ppermute | solution.py:328
  55.9 94.0 %collective-permute-start.2 = (s32[1,256]{1,0:T(1,128)}, s32[1,256]{1,0:T(1,128)}, u32[]{:S(2)}, u32[]{:S(2)}) collective-permute-start(s32[1,256]{1,0:T(1,128)} %param.23), channel_id=1, source_target_pairs={{0,16},{8,24},{16,0},{24,8},{1,17},{9,25},{17,1},{25,9},{2,18},{10... | collective-permute-start | bytes 3080 | tf_op jit(solution)/shard_map/ppermute | solution.py:328
  57.3 92.6 %collective-permute-start.3 = (s32[1,256]{1,0:T(1,128)}, s32[1,256]{1,0:T(1,128)}, u32[]{:S(2)}, u32[]{:S(2)}) collective-permute-start(s32[1,256]{1,0:T(1,128)} %param.23), channel_id=1, source_target_pairs={{0,24},{8,16},{16,8},{24,0},{1,25},{9,17},{17,9},{25,1},{2,26},{10... | collective-permute-start | bytes 3080 | tf_op jit(solution)/shard_map/ppermute | solution.py:328
  57.9 25.4 %copy-start.137 = (bf16[96]{0:T(256)(128)(2,1)S(1)}, bf16[96]{0:T(256)(128)(2,1)}, u32[]{:S(2)}) copy-start(bf16[96]{0:T(256)(128)(2,1)} %param.39) | copy-start | bytes 580
  57.9 25.4 %copy-start.138 = (bf16[96]{0:T(256)(128)(2,1)S(1)}, bf16[96]{0:T(256)(128)(2,1)}, u32[]{:S(2)}) copy-start(bf16[96]{0:T(256)(128)(2,1)} %param.32) | copy-start | bytes 580
  57.9 25.3 %copy-start.139 = (bf16[96]{0:T(256)(128)(2,1)S(1)}, bf16[96]{0:T(256)(128)(2,1)}, u32[]{:S(2)}) copy-start(bf16[96]{0:T(256)(128)(2,1)} %param.28) | copy-start | bytes 580
  57.9 25.3 %copy-start.140 = (bf16[96]{0:T(256)(128)(2,1)S(1)}, bf16[96]{0:T(256)(128)(2,1)}, u32[]{:S(2)}) copy-start(bf16[96]{0:T(256)(128)(2,1)} %param.24) | copy-start | bytes 580
  57.9 36.5 %copy-start.82 = (bf16[1,256,1536]{2,1,0:T(8,128)(2,1)S(1)}, bf16[1,256,1536]{2,1,0:T(8,128)(2,1)}, u32[]{:S(2)}) copy-start(bf16[1,256,1536]{2,1,0:T(8,128)(2,1)} %param.43) | copy-start | bytes 2359300
  57.9 36.5 %copy-start.83 = (bf16[1,256,1536]{2,1,0:T(8,128)(2,1)S(1)}, bf16[1,256,1536]{2,1,0:T(8,128)(2,1)}, u32[]{:S(2)}) copy-start(bf16[1,256,1536]{2,1,0:T(8,128)(2,1)} %param.22) | copy-start | bytes 2359300
  83.2 429.5 %reduce-scatter.9.cloned.1.call-start = ((), (), s32[]{:S(2)}) async-start(), calls=%async_computation.8 | async-start | bytes 3440640 | tf_op jit(solution)/shard_map/reduce_scatter | solution.py:622
  118.1 36.1 %copy-start = (bf16[8,128,1536]{2,1,0:T(8,128)(2,1)}, bf16[8,128,1536]{2,1,0:T(8,128)(2,1)S(1)}, u32[]{:S(2)}) copy-start(bf16[8,128,1536]{2,1,0:T(8,128)(2,1)S(1)} %shard_map.375) | copy-start | bytes 9437188
  145.4 54.5 %copy-start.88 = (f32[1536]{0:T(1024)}, f32[1536]{0:T(1024)S(1)}, u32[]{:S(2)}) copy-start(f32[1536]{0:T(1024)S(1)} %mul.710) | copy-start | bytes 18436
  146.1 113.5 %copy-start.90 = (f32[1536]{0:T(1024)}, f32[1536]{0:T(1024)S(1)}, u32[]{:S(2)}) copy-start(f32[1536]{0:T(1024)S(1)} %mul.718) | copy-start | bytes 18436
  164.6 12.8 %collective-permute-start = (bf16[4,2,192]{1,2,0:T(8,128)(2,1)}, bf16[4,2,192]{1,2,0:T(8,128)(2,1)}, u32[]{:S(2)}, u32[]{:S(2)}) collective-permute-start(bf16[4,2,192]{1,2,0:T(8,128)(2,1)} %slice.565), channel_id=1, source_target_pairs={{0,2},{2,4},{4,6},{1,3},{3,5},{5,7},{8,10},{10,12},{12,14},{9,11},... | collective-permute-start | bytes 9224 | tf_op jit(solution)/shard_map/ppermute | solution.py:502
  240.9 18.5 %copy-start.22 = (f32[128,1536]{1,0:T(8,128)S(1)}, f32[128,1536]{1,0:T(8,128)}, u32[]{:S(2)}) copy-start(f32[128,1536]{1,0:T(8,128)} %copy-done.21) | copy-start | bytes 2359300
  288.2 16.8 %collective-permute-start.6 = (bf16[4,256,128]{2,1,0:T(8,128)(2,1)S(1)}, bf16[4,256,128]{2,1,0:T(8,128)(2,1)S(1)}, u32[]{:S(2)}, u32[]{:S(2)}) collective-permute-start(bf16[4,256,128]{2,1,0:T(8,128)(2,1)S(1)} %get-tuple-element.347), channel_id=1, source_target_pairs={{0,2},{2,4},{4,6},{1,3},{3,5},{5,7},{8,10},{10,12},{12,14},{9,11},... | collective-permute-start | bytes 786440 | tf_op jit(solution)/shard_map/ppermute | solution.py:502
  292.8 23.5 %collective-permute-start.5 = (bf16[4,256,128]{2,1,0:T(8,128)(2,1)S(1)}, bf16[4,256,128]{2,1,0:T(8,128)(2,1)S(1)}, u32[]{:S(2)}, u32[]{:S(2)}) collective-permute-start(bf16[4,256,128]{2,1,0:T(8,128)(2,1)S(1)} %get-tuple-element.347), channel_id=1, source_target_pairs={{0,4},{2,6},{1,5},{3,7},{8,12},{10,14},{9,13},{11,15},{16,20},{18,... | collective-permute-start | bytes 786440 | tf_op jit(solution)/shard_map/ppermute | solution.py:502
  300.0 27.3 %collective-permute-start.4 = (bf16[4,256,128]{2,1,0:T(8,128)(2,1)S(1)}, bf16[4,256,128]{2,1,0:T(8,128)(2,1)S(1)}, u32[]{:S(2)}, u32[]{:S(2)}) collective-permute-start(bf16[4,256,128]{2,1,0:T(8,128)(2,1)S(1)} %get-tuple-element.347), channel_id=1, source_target_pairs={{0,6},{1,7},{8,14},{9,15},{16,22},{17,23},{24,30},{25,31}} | collective-permute-start | bytes 786440 | tf_op jit(solution)/shard_map/ppermute | solution.py:502
  342.0 18.7 %copy-start.79 = (f32[1536]{0:T(1024)S(1)}, f32[1536]{0:T(1024)}, u32[]{:S(2)}) copy-start(f32[1536]{0:T(1024)} %mul.751) | copy-start | bytes 18436
  380.1 43.4 %copy-start.10 = (bf16[8,128,1536]{2,1,0:T(8,128)(2,1)}, bf16[8,128,1536]{2,1,0:T(8,128)(2,1)S(1)}, u32[]{:S(2)}) copy-start(bf16[8,128,1536]{2,1,0:T(8,128)(2,1)S(1)} %shard_map.385) | copy-start | bytes 9437188
  441.0 214.3 %reduce-scatter.11.cloned.1.call-start = ((), (), s32[]{:S(2)}) async-start(), calls=%async_computation.9 | async-start | bytes 3440640 | tf_op jit(solution)/shard_map/reduce_scatter | solution.py:622
  458.4 196.8 %reduce-scatter.13.cloned.1.call-start = ((), (), s32[]{:S(2)}) async-start(), calls=%async_computation.10 | async-start | bytes 3440640 | tf_op jit(solution)/shard_map/reduce_scatter | solution.py:622
  471.8 18.8 %copy-start.25 = (f32[128,1536]{1,0:T(8,128)S(1)}, f32[128,1536]{1,0:T(8,128)}, u32[]{:S(2)}) copy-start(f32[128,1536]{1,0:T(8,128)} %copy-done.24) | copy-start | bytes 2359300
  471.8 18.8 %copy-start.80 = (f32[1536]{0:T(1024)S(1)}, f32[1536]{0:T(1024)}, u32[]{:S(2)}) copy-start(f32[1536]{0:T(1024)} %mul.751) | copy-start | bytes 18436
  471.8 18.8 %copy-start.117 = (f32[128]{0:T(128)S(1)}, f32[128]{0:T(128)}, u32[]{:S(2)}) copy-start(f32[128]{0:T(128)} %copy-done.116) | copy-start | bytes 1540
  491.4 19.6 %copy-start.133 = (f32[128]{0:T(128)}, f32[128]{0:T(128)S(1)}, u32[]{:S(2)}) copy-start(f32[128]{0:T(128)S(1)} %broadcast_multiply_fusion.5) | copy-start | bytes 1540
  491.5 252.1 %reduce-scatter.15.cloned.1.call-start = ((), (), s32[]{:S(2)}) async-start(), calls=%async_computation.11 | async-start | bytes 1966080 | tf_op jit(solution)/shard_map/reduce_scatter | solution.py:622
  556.5 21.2 %collective-permute-start.7 = (bf16[4,256,128]{2,1,0:T(8,128)(2,1)}, bf16[4,256,128]{2,1,0:T(8,128)(2,1)}, u32[]{:S(2)}, u32[]{:S(2)}) collective-permute-start(bf16[4,256,128]{2,1,0:T(8,128)(2,1)} %get-tuple-element.332), channel_id=1, source_target_pairs={{2,0},{4,2},{6,4},{3,1},{5,3},{7,5},{10,8},{12,10},{14,12},{11,9},... | collective-permute-start | bytes 786440 | tf_op jit(solution)/shard_map/ppermute | solution.py:502
  557.8 56.8 %collective-permute-start.8 = (bf16[4,256,128]{2,1,0:T(8,128)(2,1)}, bf16[4,256,128]{2,1,0:T(8,128)(2,1)}, u32[]{:S(2)}, u32[]{:S(2)}) collective-permute-start(bf16[4,256,128]{2,1,0:T(8,128)(2,1)} %get-tuple-element.331), channel_id=1, source_target_pairs={{4,0},{6,2},{5,1},{7,3},{12,8},{14,10},{13,9},{15,11},{20,16},{22,... | collective-permute-start | bytes 786440 | tf_op jit(solution)/shard_map/ppermute | solution.py:502
  559.1 55.5 %collective-permute-start.9 = (bf16[4,256,128]{2,1,0:T(8,128)(2,1)}, bf16[4,256,128]{2,1,0:T(8,128)(2,1)}, u32[]{:S(2)}, u32[]{:S(2)}) collective-permute-start(bf16[4,256,128]{2,1,0:T(8,128)(2,1)} %get-tuple-element.330), channel_id=1, source_target_pairs={{6,0},{7,1},{14,8},{15,9},{22,16},{23,17},{30,24},{31,25}} | collective-permute-start | bytes 786440 | tf_op jit(solution)/shard_map/ppermute | solution.py:502
  571.3 50.5 %copy-start.27 = (f32[4,256,64]{2,1,0:T(8,128)S(1)}, f32[4,256,64]{2,1,0:T(8,128)}, u32[]{:S(2)}) copy-start(f32[4,256,64]{2,1,0:T(8,128)} %copy-done.26) | copy-start | bytes 786436
  632.4 230.5 %reduce-scatter.23.cloned.1.call-start = ((), (), s32[]{:S(2)}) async-start(), calls=%async_computation.15 | async-start | bytes 3440640 | tf_op jit(solution)/shard_map/reduce_scatter | solution.py:622
  635.6 17.7 %copy-start.17 = (f32[128,1536]{1,0:T(8,128)S(1)}, f32[128,1536]{1,0:T(8,128)}, u32[]{:S(2)}) copy-start(f32[128,1536]{1,0:T(8,128)} %copy-done.15) | copy-start | bytes 2359300
  635.7 18.5 %copy-start.81 = (f32[1536]{0:T(1024)S(1)}, f32[1536]{0:T(1024)}, u32[]{:S(2)}) copy-start(f32[1536]{0:T(1024)} %mul.751) | copy-start | bytes 18436
  635.7 18.5 %copy-start.118 = (f32[128]{0:T(128)S(1)}, f32[128]{0:T(128)}, u32[]{:S(2)}) copy-start(f32[128]{0:T(128)} %copy-done.116) | copy-start | bytes 1540
  635.7 18.5 %copy-start.134 = (f32[128]{0:T(128)S(1)}, f32[128]{0:T(128)}, u32[]{:S(2)}) copy-start(f32[128]{0:T(128)} %copy-done.133) | copy-start | bytes 1540
  655.3 24.3 %copy-start.37 = (f32[128,1536]{1,0:T(8,128)}, f32[128,1536]{1,0:T(8,128)S(1)}, u32[]{:S(2)}) copy-start(f32[128,1536]{1,0:T(8,128)S(1)} %get-tuple-element.90) | copy-start | bytes 2359300
  655.3 19.5 %copy-start.57 = (bf16[1024,896]{1,0:T(8,128)(2,1)S(1)}, bf16[1024,896]{1,0:T(8,128)(2,1)}, u32[]{:S(2)}) copy-start(bf16[1024,896]{1,0:T(8,128)(2,1)} %copy-done.56) | copy-start | bytes 5505028
  679.6 183.3 %reduce-scatter.21.cloned.1.call-start = ((), (), s32[]{:S(2)}) async-start(), calls=%async_computation.14 | async-start | bytes 3440640 | tf_op jit(solution)/shard_map/reduce_scatter | solution.py:622
  699.5 163.5 %reduce-scatter.19.cloned.1.call-start = ((), (), s32[]{:S(2)}) async-start(), calls=%async_computation.13 | async-start | bytes 3440640 | tf_op jit(solution)/shard_map/reduce_scatter | solution.py:622
  706.5 35.1 %collective-permute-start.10 = (bf16[128,1536]{0,1:T(8,128)(2,1)S(1)}, bf16[128,1536]{0,1:T(8,128)(2,1)}, u32[]{:S(2)}, u32[]{:S(2)}) collective-permute-start(bf16[128,1536]{0,1:T(8,128)(2,1)S(1)} %bitcast.393), channel_id=1, source_target_pairs={{0,1},{1,0},{2,3},{3,2},{4,5},{5,4},{6,7},{7,6},{8,9},{9,8},{10,11... | collective-permute-start | bytes 1179656 | tf_op jit(solution)/shard_map/ppermute | solution.py:785
  718.4 17.7 %copy-start.23 = (f32[128,1536]{1,0:T(8,128)S(1)}, f32[128,1536]{1,0:T(8,128)}, u32[]{:S(2)}) copy-start(f32[128,1536]{1,0:T(8,128)} %copy-done.21) | copy-start | bytes 2359300
  718.4 17.7 %copy-start.89 = (f32[1536]{0:T(1024)S(1)}, f32[1536]{0:T(1024)}, u32[]{:S(2)}) copy-start(f32[1536]{0:T(1024)} %copy-done.88) | copy-start | bytes 18436
  718.4 17.7 %copy-start.122 = (f32[128]{0:T(128)S(1)}, f32[128]{0:T(128)}, u32[]{:S(2)}) copy-start(f32[128]{0:T(128)} %copy-done.121) | copy-start | bytes 1540
  718.4 18.7 %copy-start.38 = (f32[128,1536]{1,0:T(8,128)S(1)}, f32[128,1536]{1,0:T(8,128)}, u32[]{:S(2)}) copy-start(f32[128,1536]{1,0:T(8,128)} %copy-done.37) | copy-start | bytes 2359300
  738.0 168.2 %reduce-scatter.17.cloned.1.call-start = ((), (), s32[]{:S(2)}) async-start(), calls=%async_computation.12 | async-start | bytes 2949120 | tf_op jit(solution)/shard_map/reduce_scatter | solution.py:865
  769.9 23.9 %collective-permute-start.12 = (bf16[96,2688]{1,0:T(8,128)(2,1)}, bf16[96,2688]{1,0:T(8,128)(2,1)}, u32[]{:S(2)}, u32[]{:S(2)}) collective-permute-start(bf16[96,2688]{1,0:T(8,128)(2,1)} %get-tuple-element.320), channel_id=1, source_target_pairs={{0,8},{8,0},{16,24},{24,16},{1,9},{9,1},{17,25},{25,17},{2,10},{10... | collective-permute-start | bytes 1548296 | tf_op jit(solution)/shard_map/ppermute | solution.py:311
  770.3 23.5 %collective-permute-start.13 = (bf16[96,2688]{1,0:T(8,128)(2,1)}, bf16[96,2688]{1,0:T(8,128)(2,1)}, u32[]{:S(2)}, u32[]{:S(2)}) collective-permute-start(bf16[96,2688]{1,0:T(8,128)(2,1)} %get-tuple-element.319), channel_id=1, source_target_pairs={{0,16},{8,24},{16,0},{24,8},{1,17},{9,25},{17,1},{25,9},{2,18},{10... | collective-permute-start | bytes 1548296 | tf_op jit(solution)/shard_map/ppermute | solution.py:311
  771.6 23.0 %collective-permute-start.14 = (bf16[96,2688]{1,0:T(8,128)(2,1)}, bf16[96,2688]{1,0:T(8,128)(2,1)}, u32[]{:S(2)}, u32[]{:S(2)}) collective-permute-start(bf16[96,2688]{1,0:T(8,128)(2,1)} %get-tuple-element.318), channel_id=1, source_target_pairs={{0,24},{8,16},{16,8},{24,0},{1,25},{9,17},{17,9},{25,1},{2,26},{10... | collective-permute-start | bytes 1548296 | tf_op jit(solution)/shard_map/ppermute | solution.py:311
  776.8 17.0 %collective-permute-start.11 = (f32[4,2,192]{1,2,0:T(8,128)}, f32[4,2,192]{1,2,0:T(8,128)}, u32[]{:S(2)}, u32[]{:S(2)}) collective-permute-start(f32[4,2,192]{1,2,0:T(8,128)} %slice.483), channel_id=1, source_target_pairs={{2,0},{4,2},{6,4},{3,1},{5,3},{7,5},{10,8},{12,10},{14,12},{11,9},... | collective-permute-start | bytes 18440 | tf_op jit(solution)/shard_map/ppermute | solution.py:502
  803.4 28.3 %copy-start.55 = (bf16[16,96,768]{2,1,0:T(8,128)(2,1)S(1)}, bf16[16,96,768]{2,1,0:T(8,128)(2,1)}, u32[]{:S(2)}) copy-start(bf16[16,96,768]{2,1,0:T(8,128)(2,1)} %all-gather.9.cloned.1.call-done) | copy-start | bytes 7077892
  834.7 18.0 %copy-start.42 = (f32[128,1536]{1,0:T(8,128)S(1)}, f32[128,1536]{1,0:T(8,128)}, u32[]{:S(2)}) copy-start(f32[128,1536]{1,0:T(8,128)} %copy-done.41) | copy-start | bytes 2359300
  853.2 14.9 %collective-permute-start.15 = (bf16[128,1536]{0,1:T(8,128)(2,1)S(1)}, bf16[128,1536]{0,1:T(8,128)(2,1)S(1)}, u32[]{:S(2)}, u32[]{:S(2)}) collective-permute-start(bf16[128,1536]{0,1:T(8,128)(2,1)S(1)} %bitcast.392), channel_id=1, source_target_pairs={{0,1},{1,0},{2,3},{3,2},{4,5},{5,4},{6,7},{7,6},{8,9},{9,8},{10,11... | collective-permute-start | bytes 1179656 | tf_op jit(solution)/shard_map/ppermute | solution.py:785
  866.3 16.4 %collective-permute-start.18 = (bf16[96,3200]{1,0:T(8,128)(2,1)}, bf16[96,3200]{1,0:T(8,128)(2,1)S(1)}, u32[]{:S(2)}, u32[]{:S(2)}) collective-permute-start(bf16[96,3200]{1,0:T(8,128)(2,1)} %get-tuple-element.300), channel_id=1, source_target_pairs={{0,24},{8,16},{16,8},{24,0},{1,25},{9,17},{17,9},{25,1},{2,26},{10... | collective-permute-start | bytes 1843208 | tf_op jit(solution)/shard_map/ppermute | solution.py:311
  866.4 29.4 %collective-permute-start.17 = (bf16[96,3200]{1,0:T(8,128)(2,1)}, bf16[96,3200]{1,0:T(8,128)(2,1)S(1)}, u32[]{:S(2)}, u32[]{:S(2)}) collective-permute-start(bf16[96,3200]{1,0:T(8,128)(2,1)} %get-tuple-element.301), channel_id=1, source_target_pairs={{0,16},{8,24},{16,0},{24,8},{1,17},{9,25},{17,1},{25,9},{2,18},{10... | collective-permute-start | bytes 1843208 | tf_op jit(solution)/shard_map/ppermute | solution.py:311
  867.7 28.1 %collective-permute-start.16 = (bf16[96,3200]{1,0:T(8,128)(2,1)}, bf16[96,3200]{1,0:T(8,128)(2,1)S(1)}, u32[]{:S(2)}, u32[]{:S(2)}) collective-permute-start(bf16[96,3200]{1,0:T(8,128)(2,1)} %get-tuple-element.302), channel_id=1, source_target_pairs={{0,8},{8,0},{16,24},{24,16},{1,9},{9,1},{17,25},{25,17},{2,10},{10... | collective-permute-start | bytes 1843208 | tf_op jit(solution)/shard_map/ppermute | solution.py:311
  (117 other events, 670.2 us)
Sparse Core Ops, SparseCore 0:
  21.2 51.6 all-gather.8
  74.5 147.6 all-gather.10
  223.8 39.3 all-gather.12
  264.6 158.9 all-gather.14
  441.1 62.0 reduce-scatter.8
  505.4 53.8 reduce-scatter.10
  561.6 70.0 reduce-scatter.12
  634.0 36.4 reduce-scatter.14
  679.7 51.3 reduce-scatter.22
  733.3 59.2 reduce-scatter.20
  795.0 56.6 reduce-scatter.18
  859.5 46.7 reduce-scatter.16
